TPU v7x, 32 devices: a whole 2x2x4 slice. The times are simulated.
32 devices in a mesh: groups: 2 (over x), ty: 16 (over z, y, core).
Axes of the slice: x: 2, y: 2, z: 4, core: 2. Of those that a mesh axis runs over, the one named last changes fastest.
Arguments:
- spectrum: float32 [2, 4096, 8192], P(None, ('groups', 'ty')), parts along dimension 1, may hold values from -6 to 6
- pupil: bfloat16 [1024, 1024], replicated, may hold values from 0.19921875 to 1
- measured: bfloat16 [32, 256, 1024], P(('groups', 'ty')), parts along dimension 0, may hold values from 0.29882812 to 3
- centre_rows: int32 [32], P('groups'), parts along dimension 0, may hold values from 512 to 1536
- centre_cols: int32 [32], P('groups'), parts along dimension 0, may hold values from 512 to 7680
Outputs:
- updated: float32 [2, 4096, 8192], P(None, ('groups', 'ty')), parts along dimension 1
There are 2 independent parts, one for each index of `groups`. A program takes and returns all parts, laid end to end along the dimension named above; an argument that names none is the same for every part. Nothing has to cross between parts.
Inputs may be any that keep to these rules, and one draw needn't show every extreme that they name: `centre_rows`: each pupil crop lies inside the slab's rows. `centre_cols`: each pupil crop lies inside the slab's columns.
All inputs are finite; a program needn't handle non-finite values.
Results may differ from a plain program's by a relative error of at most 0.00063.
Values may be sent and summed in bfloat16 or wider, within the bound.
No kernel may reach another device: no remote copies, remote signals or barrier semaphores. Data moves between devices by JAX's collectives and lax.ppermute only.
A program may use at most 128 MiB of HBM per device.

v0:
```python
import math

import jax
import jax.numpy as jnp
from jax import lax
from jax.sharding import PartitionSpec as P

step_size = 0.5


def shifted(value, axis, by):
    size = lax.axis_size(axis)
    pairs = [(i, i + by) for i in range(size) if 0 <= i + by < size]
    return lax.ppermute(value, axis, pairs)


def fourier_tables(crop_width):
    counter = jnp.arange(crop_width, dtype=jnp.int32)
    product = counter[:, None] * counter[None, :] % crop_width
    angle = product.astype(jnp.float32) * (2.0 * math.pi / crop_width)
    factor = 1.0 / math.sqrt(crop_width)
    return (
        (jnp.cos(angle) * factor).astype(jnp.bfloat16),
        (jnp.sin(angle) * factor).astype(jnp.bfloat16),
    )


def pupil_weight(pupil):
    crop_width = pupil.shape[0]
    counter = jnp.arange(crop_width, dtype=jnp.int32)
    centred = 2 * counter - crop_width + 1
    inside = (
        centred[:, None] * centred[:, None] + centred[None, :] * centred[None, :]
        <= crop_width * crop_width
    )
    return jnp.where(inside, pupil.astype(jnp.float32), jnp.float32(0.0))


def product_pair(left_real, left_imag, right_real, right_imag):
    real_part = jnp.dot(left_real, right_real, preferred_element_type=jnp.float32) - jnp.dot(
        left_imag, right_imag, preferred_element_type=jnp.float32
    )
    imag_part = jnp.dot(left_real, right_imag, preferred_element_type=jnp.float32) + jnp.dot(
        left_imag, right_real, preferred_element_type=jnp.float32
    )
    return (real_part, imag_part)


def image_gradient(crop, image, weight, cos_table, sin_table):
    crop_width = weight.shape[0]
    band_rows = image.shape[0]
    band_start = (crop_width - band_rows) // 2
    band_cos = cos_table[band_start : band_start + band_rows]
    band_sin = sin_table[band_start : band_start + band_rows]
    pupiled = (weight[None] * crop.astype(jnp.float32)).astype(jnp.bfloat16)
    mid_real, mid_imag = product_pair(band_cos, band_sin, pupiled[0], pupiled[1])
    mid_real = mid_real.astype(jnp.bfloat16)
    mid_imag = mid_imag.astype(jnp.bfloat16)
    field_real, field_imag = product_pair(mid_real, mid_imag, cos_table, sin_table)
    magnitude = jnp.sqrt(field_real * field_real + field_imag * field_imag)
    keeping = 1.0 - image.astype(jnp.float32) / jnp.maximum(magnitude, 1.0)
    resid_real = (field_real * keeping).astype(jnp.bfloat16)
    resid_imag = (field_imag * keeping).astype(jnp.bfloat16)
    back_real, back_imag = product_pair(resid_real, resid_imag, cos_table, -sin_table)
    back_real = back_real.astype(jnp.bfloat16)
    back_imag = back_imag.astype(jnp.bfloat16)
    grad_real, grad_imag = product_pair(band_cos.T, -band_sin.T, back_real, back_imag)
    return jnp.stack([grad_real * weight, grad_imag * weight])


def per_device(spectrum, pupil, measured, centre_rows, centre_cols):
    tile_count = lax.axis_size("ty")
    position = lax.axis_index("ty")
    tile_rows = spectrum.shape[1]
    slab_columns = spectrum.shape[2]
    crop_width = pupil.shape[0]
    unit_count = crop_width // tile_rows
    crop_starts = centre_rows - crop_width // 2
    crop_lefts = centre_cols - crop_width // 2
    first_tile = crop_starts // tile_rows
    offset = crop_starts % tile_rows
    mine_first = lax.dynamic_index_in_dim(first_tile, position, keepdims=False)
    weight = pupil_weight(pupil)
    cos_table, sin_table = fourier_tables(crop_width)
    spec_low = spectrum.astype(jnp.bfloat16)
    zero_index = jnp.int32(0)
    below = shifted(spec_low, "ty", -1)
    extended = jnp.concatenate([spec_low, below], axis=1)

    def cut_unit(row_start, column_start):
        return lax.dynamic_slice(
            extended, (zero_index, row_start, column_start), (2, tile_rows, crop_width)
        )

    pieces = jax.vmap(cut_unit, out_axes=1)(offset, crop_lefts)
    part_number = position - first_tile
    active = (part_number >= 0) & (part_number < unit_count)
    pieces = jnp.where(active[None, :, None, None], pieces, jnp.zeros_like(pieces))
    arrived = lax.all_to_all(pieces, "ty", split_axis=1, concat_axis=1, tiled=True)
    crop = lax.dynamic_slice_in_dim(arrived, mine_first, unit_count, 1).reshape(
        2, crop_width, crop_width
    )
    gradient = image_gradient(crop, measured[0], weight, cos_table, sin_table)
    outgoing = jnp.zeros((2, tile_count, tile_rows, crop_width), jnp.float32)
    outgoing = lax.dynamic_update_slice(
        outgoing,
        gradient.reshape(2, unit_count, tile_rows, crop_width),
        (zero_index, mine_first, zero_index, zero_index),
    )
    returned = lax.all_to_all(
        outgoing.astype(jnp.bfloat16), "ty", split_axis=1, concat_axis=1, tiled=True
    ).astype(outgoing.dtype)

    def place_unit(source, accumulated):
        piece = lax.dynamic_index_in_dim(returned, source, 1, keepdims=False)
        corner = (
            zero_index,
            lax.dynamic_index_in_dim(offset, source, keepdims=False),
            lax.dynamic_index_in_dim(crop_lefts, source, keepdims=False),
        )
        current = lax.dynamic_slice(accumulated, corner, (2, tile_rows, crop_width))
        return lax.dynamic_update_slice(accumulated, current + piece, corner)

    accumulated = lax.fori_loop(
        0, tile_count, place_unit, jnp.zeros((2, 2 * tile_rows, slab_columns), jnp.float32)
    )
    spill_rows = shifted(accumulated[:, tile_rows:].astype(jnp.bfloat16), "ty", 1).astype(
        jnp.float32
    )
    summed = accumulated[:, :tile_rows] + spill_rows
    return spectrum - step_size * summed


def solution(mesh):
    return jax.shard_map(
        per_device,
        mesh=mesh,
        in_specs=(
            P(None, ("groups", "ty"), None),
            P(),
            P(("groups", "ty"), None, None),
            P("groups"),
            P("groups"),
        ),
        out_specs=P(None, ("groups", "ty"), None),
        check_vma=False,
    )
```

profile of v0, /device:TPU:11, one launch (start us, length us, event | category | flops | bytes accessed | tf_op | source)
XLA Modules:
  0.0 995.5 jit_solution(636100815975088935)
XLA Ops:
  0.0 5.9 convert_element_type.119
  6.0 2.6 collective-permute-start
  8.7 47.5 %collective-permute-done = bf16[2,128,8192]{2,1,0:T(8,128)(2,1)} collective-permute-done((bf16[2,128,8192]{2,1,0:T(8,128)(2,1)}, bf16[2,128,8192]{2,1,0:T(8,128)(2,1)}, u32[]{:S(2)}, u32[]{:S(2)}) %collective-permute-start) | collective-permute-done | bytes 4194336 | tf_op jit(solution)/shard_map/ppermute | solution.py:14
  56.1 7.9 pad_maximum_fusion
  64.0 63.5 %while.17 = (s32[]{:T(128)}, bf16[2,256,8192]{2,1,0:T(8,128)(2,1)}, s32[16,3]{0,1:T(4,128)S(1)}, bf16[16,2,128,1024]{3,2,1,0:T(8,128)(2,1)}) while((s32[]{:T(128)}, bf16[2,256,8192]{2,1,0:T(8,128)(2,1)}, s32[16,3]{0,1:T(4,128)S(1)}, bf16[16,2,128,1024]{3,2,1,0:T(8,128)(2,1)}) %tuple.57), condition=%wide.while_cond.clone, body=%wide.while_body.sunk.clone | while | flops 2 | bytes 1049709 | solution.py:91
  64.6 3.4 bitcast_dynamic-update-slice_fusion.3
  68.6 3.4 bitcast_dynamic-update-slice_fusion.3
  72.5 3.4 bitcast_dynamic-update-slice_fusion.3
  76.5 3.4 bitcast_dynamic-update-slice_fusion.3
  80.5 3.4 bitcast_dynamic-update-slice_fusion.3
  84.5 3.4 bitcast_dynamic-update-slice_fusion.3
  88.4 3.4 bitcast_dynamic-update-slice_fusion.3
  92.4 3.4 bitcast_dynamic-update-slice_fusion.3
  96.4 3.4 bitcast_dynamic-update-slice_fusion.3
  100.3 3.4 bitcast_dynamic-update-slice_fusion.3
  104.3 3.4 bitcast_dynamic-update-slice_fusion.3
  108.3 3.4 bitcast_dynamic-update-slice_fusion.3
  112.3 3.4 bitcast_dynamic-update-slice_fusion.3
  116.2 3.3 bitcast_dynamic-update-slice_fusion.3
  120.2 3.4 bitcast_dynamic-update-slice_fusion.3
  124.2 3.4 bitcast_dynamic-update-slice_fusion.3
  127.5 7.4 select_bitcast_fusion
  134.9 6.3 all-to-all-start
  143.6 2.6 convert_select_fusion
  146.2 15.7 %multiply_convert_fusion.1 = bf16[1024,1024]{1,0:T(8,128)(2,1)S(1)} fusion(), kind=kLoop, calls=%fused_computation.21 | loop fusion | flops 16777216 | bytes 2097152 | tf_op jit(solution)/shard_map/convert_element_type | solution.py:23
  161.9 16.6 %multiply_convert_fusion = bf16[1024,1024]{1,0:T(8,128)(2,1)} fusion(), kind=kLoop, calls=%fused_computation.18 | loop fusion | flops 16777216 | bytes 2097152 | tf_op jit(solution)/shard_map/convert_element_type | solution.py:24
  178.4 142.9 %all-to-all-done = bf16[2,16,128,1024]{3,2,0,1:T(8,128)(2,1)} async-done(((bf16[2,16,128,1024]{3,2,0,1:T(8,128)(2,1)}), bf16[2,16,128,1024]{3,2,0,1:T(8,128)(2,1)}, u32[]{:S(2)}, u32[]{:S(2)}) %all-to-all-start) | async-done | bytes 8388640 | tf_op jit(solution)/shard_map/all_to_all | solution.py:99
  321.3 2.6 constant_dynamic-slice_fusion.1
  330.0 16.3 %fusion.9 = f32[256,1024]{1,0:T(8,128)S(1)} fusion(bf16[256,1024]{1,0:T(8,128)(2,1)S(1)} %fusion.38), kind=kOutput, calls=%fused_computation.29 | convolution fusion | flops 553648128 | bytes 1572864 | tf_op jit(solution)/shard_map/dot_general | solution.py:43
  347.0 16.5 %fusion.10 = f32[256,1024]{1,0:T(8,128)S(1)} fusion(bf16[256,1024]{1,0:T(8,128)(2,1)S(1)} %fusion.39), kind=kOutput, calls=%fused_computation.30 | convolution fusion | flops 553648128 | bytes 1572864 | tf_op jit(solution)/shard_map/dot_general | solution.py:40
  363.5 16.5 %fusion.31 = f32[256,1024]{1,0:T(8,128)S(1)} fusion(f32[256,1024]{1,0:T(8,128)S(1)} %fusion.9, bf16[256,1024]{1,0:T(8,128)(2,1)S(1)} %fusion.39), kind=kOutput, calls=%fused_computation.45 | convolution fusion | flops 553910272 | bytes 2621440 | tf_op jit(solution)/shard_map/dot_general | solution.py:43
  380.1 17.3 %multiply_convert_fusion.13 = (bf16[256,1024]{1,0:T(8,128)(2,1)S(1)}, bf16[256,1024]{1,0:T(8,128)(2,1)S(1)}) fusion(f32[256,1024]{1,0:T(8,128)S(1)} %fusion.31, bf16[1,256,1024]{2,1,0:T(8,128)(2,1)S(1)} %copy-done.6, f32[256,1024]{1,0:T(8,128)S(1)} %fusion.10, bf16[256,1024]{1,0:T(8,128)(2,1)S(1)} %fusion.38), kind=kOutput, calls=%fused_computation.53 | convolution fusion | flops 556793856 | bytes 4194304 | tf_op jit(solution)/shard_map/dot_general | solution.py:40
  397.4 16.3 %fusion.8 = f32[256,1024]{1,0:T(8,128)S(1)} fusion(bf16[256,1024]{1,0:T(8,128)(2,1)S(1)} %get-tuple-element.137), kind=kOutput, calls=%fused_computation.28 | convolution fusion | flops 553648128 | bytes 1572864 | tf_op jit(solution)/shard_map/dot_general | solution.py:40
  413.6 16.4 %fusion.7 = f32[256,1024]{1,0:T(8,128)S(1)} fusion(bf16[256,1024]{1,0:T(8,128)(2,1)S(1)} %get-tuple-element.138), kind=kOutput, calls=%fused_computation.27 | convolution fusion | flops 553648128 | bytes 1572864 | tf_op jit(solution)/shard_map/dot_general | solution.py:43
  430.1 16.4 %fusion.35 = bf16[256,1024]{1,0:T(8,128)(2,1)S(1)} fusion(f32[256,1024]{1,0:T(8,128)S(1)} %fusion.8, bf16[256,1024]{1,0:T(8,128)(2,1)S(1)} %get-tuple-element.138), kind=kOutput, calls=%fused_computation.47 | convolution fusion | flops 557318144 | bytes 2097152 | tf_op jit(solution)/shard_map/dot_general | solution.py:40
  446.5 16.6 %fusion.32 = bf16[256,1024]{1,0:T(8,128)(2,1)S(1)} fusion(f32[256,1024]{1,0:T(8,128)S(1)} %fusion.7, bf16[256,1024]{1,0:T(8,128)(2,1)S(1)} %get-tuple-element.137), kind=kOutput, calls=%fused_computation.46 | convolution fusion | flops 557318144 | bytes 2097152 | tf_op jit(solution)/shard_map/dot_general | solution.py:43
  469.7 189.9 %all_to_all.10 = bf16[2,16,128,1024]{3,2,0,1:T(8,128)(2,1)} all-to-all(bf16[2,16,128,1024]{3,2,0,1:T(8,128)(2,1)S(1)} %maximum_dynamic-update-slice_fusion), channel_id=1, replica_groups=mesh['groups'=2,'ty'=16] {'ty'}, dimensions={1} | all-to-all | bytes 16777216 | tf_op jit(solution)/shard_map/all_to_all | solution.py:110
  659.6 11.3 %convert_element_type.133 = f32[2,16,128,1024]{3,2,0,1:T(8,128)} convert(bf16[2,16,128,1024]{3,2,0,1:T(8,128)(2,1)} %all_to_all.10) | non-fusion elementwise | flops 4194304 | bytes 25165824 | tf_op jit(solution)/shard_map/convert_element_type | solution.py:112
  671.0 7.8 broadcast_in_dim.35
  678.8 254.3 %while.16 = (s32[]{:T(128)}, f32[2,256,8192]{2,1,0:T(8,128)}, s32[16]{0:T(128)S(1)}, s32[16]{0:T(128)S(1)}, f32[2,16,128,1024]{3,2,0,1:T(8,128)}) while((s32[]{:T(128)}, f32[2,256,8192]{2,1,0:T(8,128)}, s32[16]{0:T(128)S(1)}, s32[16]{0:T(128)S(1)}, f32[2,16,128,1024]{3,2,0,1:T(8,128)}) %tuple.60), condition=%wide.region_1.2_spmd.clone, body=%wide.region_0.1_spmd.sunk.clone | while | flops 262152 | bytes 5243057 | solution.py:124
  683.8 2.0 bitcast_add_fusion.3
  685.8 9.1 dynamic_update_slice.14
  700.0 2.0 bitcast_add_fusion.3
  701.9 8.8 dynamic_update_slice.14
  715.8 2.0 bitcast_add_fusion.3
  717.7 8.9 dynamic_update_slice.14
  733.6 9.1 dynamic_update_slice.14
  749.7 9.0 dynamic_update_slice.14
  765.8 9.1 dynamic_update_slice.14
  781.9 8.8 dynamic_update_slice.14
  797.7 9.0 dynamic_update_slice.14
  813.8 9.1 dynamic_update_slice.14
  829.9 9.1 dynamic_update_slice.14
  846.0 9.1 dynamic_update_slice.14
  862.1 9.0 dynamic_update_slice.14
  876.2 2.0 bitcast_add_fusion.3
  878.2 9.1 dynamic_update_slice.14
  894.3 9.1 dynamic_update_slice.14
  910.4 8.3 dynamic_update_slice.14
  925.6 7.5 dynamic_update_slice.14
  933.1 3.9 slice.93
  937.0 2.7 collective-permute-start.1
  939.7 45.4 %collective-permute-done.1 = bf16[2,128,8192]{2,1,0:T(8,128)(2,1)S(1)} collective-permute-done((bf16[2,128,8192]{2,1,0:T(8,128)(2,1)S(1)}, bf16[2,128,8192]{2,1,0:T(8,128)(2,1)S(1)}, u32[]{:S(2)}, u32[]{:S(2)}) %collective-permute-start.1) | collective-permute-done | bytes 4194336 | tf_op jit(solution)/shard_map/ppermute | solution.py:14
  985.1 10.1 %multiply_subtract_fusion = f32[2,128,8192]{2,1,0:T(8,128)} fusion(f32[2,128,8192]{2,1,0:T(8,128)} %param.7, bf16[2,128,8192]{2,1,0:T(8,128)(2,1)S(1)} %collective-permute-done.1, f32[2,256,8192]{2,1,0:T(8,128)} %get-tuple-element.99), kind=kLoop, calls=%fused_computation.8 | loop fusion | flops 8388608 | bytes 29360128 | tf_op jit(solution)/shard_map/sub | solution.py:131
  (109 shorter events, 66.0 us)
Async XLA Ops:
  0.0 8.6 copy-start.4
  0.0 8.6 copy-start.5
  6.0 50.2 %collective-permute-start = (bf16[2,128,8192]{2,1,0:T(8,128)(2,1)}, bf16[2,128,8192]{2,1,0:T(8,128)(2,1)}, u32[]{:S(2)}, u32[]{:S(2)}) collective-permute-start(bf16[2,128,8192]{2,1,0:T(8,128)(2,1)} %convert_element_type.119), channel_id=1, source_target_pairs={{1,0},{2,1},{3,2},{4,3},{5,4},{6,5},{7,6},{8,7},{9,8},{10,9},{11,1... | collective-permute-start | bytes 12582920 | tf_op jit(solution)/shard_map/ppermute | solution.py:14
  134.9 8.6 copy-start.1
  134.9 186.4 %all-to-all-start = ((bf16[2,16,128,1024]{3,2,0,1:T(8,128)(2,1)}), bf16[2,16,128,1024]{3,2,0,1:T(8,128)(2,1)}, u32[]{:S(2)}, u32[]{:S(2)}) async-start(bf16[2,16,128,1024]{3,2,0,1:T(8,128)(2,1)} %select_bitcast_fusion), calls=%async_computation | async-start | bytes 16777216 | tf_op jit(solution)/shard_map/all_to_all | solution.py:99
  323.9 2.2 copy-start
  326.1 1.7 copy-start.3
  363.5 16.5 %copy-start.6 = (bf16[1,256,1024]{2,1,0:T(8,128)(2,1)S(1)}, bf16[1,256,1024]{2,1,0:T(8,128)(2,1)}, u32[]{:S(2)}) copy-start(bf16[1,256,1024]{2,1,0:T(8,128)(2,1)} %param.9) | copy-start | bytes 1572868
  463.8 1.6 copy-start.2
  937.0 48.1 %collective-permute-start.1 = (bf16[2,128,8192]{2,1,0:T(8,128)(2,1)S(1)}, bf16[2,128,8192]{2,1,0:T(8,128)(2,1)S(1)}, u32[]{:S(2)}, u32[]{:S(2)}) collective-permute-start(bf16[2,128,8192]{2,1,0:T(8,128)(2,1)S(1)} %slice.93), channel_id=1, source_target_pairs={{0,1},{1,2},{2,3},{3,4},{4,5},{5,6},{6,7},{7,8},{8,9},{9,10},{10,1... | collective-permute-start | bytes 12582920 | tf_op jit(solution)/shard_map/ppermute | solution.py:14
where the time goes:
time: 1010 us; the launch traced here: 995 us
  local copies, waits for them, and re-layouts  243 us (24%)
  waiting for transfers between devices  236 us (23%)
  blocking collectives  190 us (19%)
  matrix products  139 us (14%)
  other arithmetic  111 us (11%)
  loops' own time  62.3 us (6%)
  starting transfers between devices  11.5 us (1%)
    all_to_all x1, blocking collectives, per_device(): lax.all_to_all(outgoing.astype(jnp.bfloat16), 'ty', split_axis=1, concat_...  190 us
    all_to_all x1, waiting for transfers between devices, per_device(): lax.all_to_all(pieces, 'ty', split_axis=1, concat_axis=1, tiled=True)  143 us
    dynamic_update_slice x16, local copies, waits for them, and re-layouts, place_unit(): return lax.dynamic_update_slice(accumulated, current + piece, corner)  142 us
    ppermute x2, waiting for transfers between devices, shifted(): return lax.ppermute(value, axis, pairs)  92.9 us
    gather x48, local copies, waits for them, and re-layouts  63.5 us
    another operation x1, loops' own time, per_device(): lax.fori_loop(0, tile_count, place_unit, jnp.zeros((2, 2 * tile_rows, sla...  62.3 us
    dot_general x4, matrix products, product_pair(): jnp.dot(left_imag, right_imag, preferred_element_type=jnp.float32)  35.7 us
    dot_general x4, matrix products, product_pair(): jnp.dot(left_imag, right_real, preferred_element_type=jnp.float32)  34.7 us
  transfers between devices with their start and end apart: 3, of which 3 were waited for; matrix products, arithmetic and copies ran while one was open for 4% of the time, Pallas kernels for 0%

commit v1 on v0

v1 whole, which is shorter than its diff:
```python
import functools
import math

import jax
import jax.numpy as jnp
import numpy as np
from jax import lax
from jax.experimental import pallas as pl
from jax.experimental.pallas import tpu as pltpu
from jax.sharding import PartitionSpec as P

step_size = 0.5
lane = 128
sublane = 8
vmem_bytes = 56 * 1024 * 1024


def fourier_tables(crop_width):
    counter = np.arange(crop_width, dtype=np.int64)
    angle = (counter[:, None] * counter[None, :] % crop_width) * (2.0 * math.pi / crop_width)
    factor = 1.0 / math.sqrt(crop_width)
    cos_table = (np.cos(angle) * factor).astype(np.float32).astype(jnp.bfloat16)
    sin_table = (np.sin(angle) * factor).astype(np.float32).astype(jnp.bfloat16)
    return cos_table, sin_table


def pupil_weight(pupil):
    crop_width = pupil.shape[0]
    counter = jnp.arange(crop_width, dtype=jnp.int32)
    centred = 2 * counter - crop_width + 1
    inside = (
        centred[:, None] * centred[:, None] + centred[None, :] * centred[None, :]
        <= crop_width * crop_width
    )
    return jnp.where(inside, pupil.astype(jnp.float32), jnp.float32(0.0))


def shifted_rows(window_ref, residual, tile_rows):
    window = window_ref.shape[0]
    return pltpu.roll(window_ref[...], (window - residual) % window, 0)[:tile_rows]


def band_rows_matrix(bt_ref, residual, tile_rows):
    rows = shifted_rows(bt_ref, residual, tile_rows)
    band = rows.shape[1] // 2
    turned = jnp.concatenate([-rows[:, band:], rows[:, :band]], axis=1)
    return jnp.concatenate([rows, turned], axis=0).astype(jnp.bfloat16)


def forward_kernel(info_ref, spec_ref, weight_ref, bt_ref, out_ref, *, tile_rows, crop_width, band):
    step = pl.program_id(0)
    residual = info_ref[1, step]
    col_shift = info_ref[3, step]
    active = info_ref[4, step]
    width = spec_ref.shape[2]

    @pl.when(active == 0)
    def _():
        out_ref[...] = jnp.zeros_like(out_ref)

    @pl.when(active != 0)
    def _():
        weight = shifted_rows(weight_ref, residual, tile_rows)
        parts = []
        for part in range(2):
            low = spec_ref[part].astype(jnp.bfloat16).astype(jnp.float32)
            low = pltpu.roll(low, (width - col_shift) % width, 1)[:, :crop_width]
            parts.append((weight * low).astype(jnp.bfloat16))
        pupiled = jnp.concatenate(parts, axis=0)
        left = band_rows_matrix(bt_ref, residual, tile_rows)
        mid = lax.dot_general(
            left, pupiled, (((0,), (0,)), ((), ())), preferred_element_type=jnp.float32
        )
        out_ref[0] = mid.astype(jnp.bfloat16).reshape(2, band, crop_width)


def backward_kernel(
    info_ref, spec_ref, back_ref, weight_ref, bt_ref, out_ref, *, tile_rows, crop_width, band, width
):
    step = pl.program_id(0)
    residual = info_ref[1, step]
    col_start = info_ref[2, step]
    col_shift = info_ref[3, step]
    active = info_ref[4, step]

    @pl.when(step == 0)
    def _():
        out_ref[...] = spec_ref[...]

    @pl.when(active != 0)
    def _():
        weight = shifted_rows(weight_ref, residual, tile_rows)
        left = band_rows_matrix(bt_ref, residual, tile_rows)
        back = back_ref[0].reshape(2 * band, crop_width)
        grad = jnp.dot(left, back, preferred_element_type=jnp.float32)
        columns = pl.ds(pl.multiple_of(col_start, lane), width)
        pad = jnp.zeros((tile_rows, width - crop_width), jnp.float32)
        for part in range(2):
            piece = grad[part * tile_rows : (part + 1) * tile_rows] * weight * step_size
            piece = pltpu.roll(jnp.concatenate([piece, pad], axis=1), col_shift, 1)
            out_ref[part, :, columns] = out_ref[part, :, columns] - piece


def middle_kernel(mid_ref, image_ref, cos_ref, sin_ref, out_ref, real_ref, imag_ref):
    step = pl.program_id(0)
    hr, hi = mid_ref[0], mid_ref[1]
    cos, sin = cos_ref[...], sin_ref[...]
    dot = functools.partial(jnp.dot, preferred_element_type=jnp.float32)
    field_real = dot(hr, cos) - dot(hi, sin)
    field_imag = dot(hr, sin) + dot(hi, cos)
    magnitude = jnp.sqrt(field_real * field_real + field_imag * field_imag)
    keeping = 1.0 - image_ref[0].astype(jnp.float32) / jnp.maximum(magnitude, 1.0)
    qr = (field_real * keeping).astype(jnp.bfloat16)
    qi = (field_imag * keeping).astype(jnp.bfloat16)

    def turned(left, table):
        return lax.dot_general(
            left, table, (((1,), (1,)), ((), ())), preferred_element_type=jnp.float32
        )

    back_real = turned(qr, cos) + turned(qi, sin)
    back_imag = turned(qi, cos) - turned(qr, sin)

    @pl.when(step == 0)
    def _():
        real_ref[...] = back_real
        imag_ref[...] = back_imag

    @pl.when(step != 0)
    def _():
        real_ref[...] += back_real
        imag_ref[...] += back_imag

    @pl.when(step == pl.num_programs(0) - 1)
    def _():
        out_ref[0] = real_ref[...].astype(jnp.bfloat16)
        out_ref[1] = imag_ref[...].astype(jnp.bfloat16)


def params():
    return pltpu.CompilerParams(vmem_limit_bytes=vmem_bytes)


def forward(info, spectrum, weight, bt):
    _, tile_rows, slab_columns = spectrum.shape
    crop_width = weight.shape[1]
    band = bt.shape[1] // 2
    width = crop_width + lane
    count = info.shape[1]
    window = tile_rows + sublane
    return pl.pallas_call(
        functools.partial(forward_kernel, tile_rows=tile_rows, crop_width=crop_width, band=band),
        grid_spec=pltpu.PrefetchScalarGridSpec(
            num_scalar_prefetch=1,
            grid=(count,),
            in_specs=[
                pl.BlockSpec(
                    (pl.Element(2), pl.Element(tile_rows), pl.Element(width)),
                    lambda i, info: (0, 0, pl.multiple_of(info[2, i], lane)),
                ),
                pl.BlockSpec(
                    (pl.Element(window), pl.Element(crop_width)),
                    lambda i, info: (pl.multiple_of(info[0, i], sublane), 0),
                ),
                pl.BlockSpec(
                    (pl.Element(window), pl.Element(2 * band)),
                    lambda i, info: (pl.multiple_of(info[0, i], sublane), 0),
                ),
            ],
            out_specs=pl.BlockSpec((1, 2, band, crop_width), lambda i, info: (i, 0, 0, 0)),
        ),
        out_shape=jax.ShapeDtypeStruct((count, 2, band, crop_width), jnp.bfloat16),
        compiler_params=params(),
        name="forward",
    )(info, spectrum, weight, bt)


def backward(info, spectrum, back, weight, bt):
    _, tile_rows, slab_columns = spectrum.shape
    crop_width = weight.shape[1]
    band = bt.shape[1] // 2
    width = crop_width + lane
    count = info.shape[1]
    window = tile_rows + sublane
    whole = pl.BlockSpec(
        spectrum.shape, lambda i, info: (0, 0, 0), pipeline_mode=pl.Buffered(1)
    )
    return pl.pallas_call(
        functools.partial(
            backward_kernel, tile_rows=tile_rows, crop_width=crop_width, band=band, width=width
        ),
        grid_spec=pltpu.PrefetchScalarGridSpec(
            num_scalar_prefetch=1,
            grid=(count,),
            in_specs=[
                whole,
                pl.BlockSpec((1, 2, band, crop_width), lambda i, info: (i, 0, 0, 0)),
                pl.BlockSpec(
                    (pl.Element(window), pl.Element(crop_width)),
                    lambda i, info: (pl.multiple_of(info[0, i], sublane), 0),
                ),
                pl.BlockSpec(
                    (pl.Element(window), pl.Element(2 * band)),
                    lambda i, info: (pl.multiple_of(info[0, i], sublane), 0),
                ),
            ],
            out_specs=pl.BlockSpec(spectrum.shape, lambda i, info: (0, 0, 0)),
        ),
        out_shape=jax.ShapeDtypeStruct(spectrum.shape, jnp.float32),
        compiler_params=params(),
        name="backward",
    )(info, spectrum, back, weight, bt)


def middle(mid, image, cos_table, sin_table):
    _, band, crop_width = mid.shape
    block = min(256, crop_width)
    table = pl.BlockSpec((crop_width, block), lambda j: (0, j))
    return pl.pallas_call(
        middle_kernel,
        grid=(crop_width // block,),
        in_specs=[
            pl.BlockSpec((2, band, crop_width), lambda j: (0, 0, 0)),
            pl.BlockSpec((1, band, block), lambda j: (0, 0, j)),
            table,
            table,
        ],
        out_specs=pl.BlockSpec((2, band, crop_width), lambda j: (0, 0, 0)),
        out_shape=jax.ShapeDtypeStruct((2, band, crop_width), jnp.bfloat16),
        scratch_shapes=[pltpu.VMEM((band, crop_width), jnp.float32)] * 2,
        compiler_params=params(),
        name="middle",
    )(mid, image, cos_table, sin_table)


def image_info(position, tile_rows, slab_columns, crop_width, centre_rows, centre_cols):
    tops = centre_rows - crop_width // 2
    lefts = centre_cols - crop_width // 2
    begin = position * tile_rows - tops + tile_rows
    active = (begin > 0) & (begin < crop_width + tile_rows)
    begin = jnp.clip(begin, 0, crop_width + tile_rows)
    aligned = begin // sublane * sublane
    col_start = jnp.minimum(lefts // lane * lane, slab_columns - crop_width - lane)
    return jnp.stack(
        [aligned, begin - aligned, col_start, lefts - col_start, active.astype(jnp.int32)]
    ).astype(jnp.int32)


def per_device(spectrum, pupil, measured, centre_rows, centre_cols):
    position = lax.axis_index("ty")
    _, tile_rows, slab_columns = spectrum.shape
    crop_width = pupil.shape[0]
    band = measured.shape[1]
    band_start = (crop_width - band) // 2
    cos_table, sin_table = fourier_tables(crop_width)
    pads = ((tile_rows, tile_rows + sublane), (0, 0))
    band_table = np.concatenate(
        [
            cos_table[:, band_start : band_start + band],
            sin_table[:, band_start : band_start + band],
        ],
        axis=1,
    ).astype(np.float32)
    bt = jnp.asarray(np.pad(band_table, pads))
    weight = jnp.pad(pupil_weight(pupil), pads)
    info = image_info(position, tile_rows, slab_columns, crop_width, centre_rows, centre_cols)
    partial = forward(info, spectrum, weight, bt)
    mid = lax.psum_scatter(partial, "ty", scatter_dimension=0, tiled=True)[0]
    back = middle(mid, measured, jnp.asarray(cos_table), jnp.asarray(sin_table))
    gathered = lax.all_gather(back, "ty")
    return backward(info, spectrum, gathered, weight, bt)


def solution(mesh):
    return jax.shard_map(
        per_device,
        mesh=mesh,
        in_specs=(
            P(None, ("groups", "ty"), None),
            P(),
            P(("groups", "ty"), None, None),
            P("groups"),
            P("groups"),
        ),
        out_specs=P(None, ("groups", "ty"), None),
        check_vma=False,
    )
```

time: 1010 us -> 390 us (0.39); the launches traced: 995 us -> 386 us
  local copies, waits for them, and re-layouts: 243 us -> 3.39 us
  blocking collectives: 190 us -> 0 us
  matrix products: 139 us -> 0 us
  other arithmetic: 111 us -> 3.53 us
  waiting for transfers between devices: 236 us -> 303 us
  Pallas kernels: 0 us -> 63.2 us
  loops' own time: 62.3 us -> 0 us
  starting transfers between devices: 11.5 us -> 0.04 us
  between operations: 2.26 us -> 13.4 us
    all_to_all x1 -> x0, blocking collectives: 190 us -> none  [per_device(): lax.all_to_all(outgoing.astype(jnp.bfloat16), 'ty', split_axis=1, concat_...]
    reduce_scatter x0 -> x1, waiting for transfers between devices: none -> 177 us  [per_device(): mid = lax.psum_scatter(partial, 'ty', scatter_dimension=0, tiled=True)[0]]
    all_to_all x1 -> x0, waiting for transfers between devices: 143 us -> none  [per_device(): lax.all_to_all(pieces, 'ty', split_axis=1, concat_axis=1, tiled=True)]
    dynamic_update_slice x16 -> x0, local copies, waits for them, and re-layouts: 142 us -> none  [place_unit(): return lax.dynamic_update_slice(accumulated, current + piece, corner)]
    dot_general x16 -> x0, matrix products: 139 us -> none  [the longest x4 35.7 us: product_pair(): jnp.dot(left_imag, right_imag, preferred_element_type=jnp.float32)]
    all_gather x0 -> x1, waiting for transfers between devices: none -> 126 us  [per_device(): gathered = lax.all_gather(back, 'ty')]
    ppermute x2 -> x0, waiting for transfers between devices: 92.9 us -> none  [shifted(): return lax.ppermute(value, axis, pairs)]
    gather x48 -> x0, local copies, waits for them, and re-layouts: 63.5 us -> none
  transfers between devices with their start and end apart: 3 -> 2, of which waited for: 3 -> 2; matrix products, arithmetic and copies ran while one was open for 4% -> 0% of each run, Pallas kernels for 0% -> 0%
where the time goes in v1:
time: 390 us; the launch traced here: 386 us
  waiting for transfers between devices  303 us (78%)
  Pallas kernels  63.2 us (16%)
  between operations  13.4 us (3%)
    reduce_scatter x1, waiting for transfers between devices, per_device(): mid = lax.psum_scatter(partial, 'ty', scatter_dimension=0, tiled=True)[0]  177 us
    all_gather x1, waiting for transfers between devices, per_device(): gathered = lax.all_gather(back, 'ty')  126 us
    pallas_call x1, Pallas kernels, backward(): pl.pallas_call(functools.partial(backward_kernel, tile_rows=tile_rows, cr...  25.9 us
    pallas_call x1, Pallas kernels, forward(): pl.pallas_call(functools.partial(forward_kernel, tile_rows=tile_rows, cro...  25.8 us
    pallas_call x1, Pallas kernels, middle(): pl.pallas_call(middle_kernel, grid=(crop_width // block,), in_specs=[pl.B...  11.5 us
  transfers between devices with their start and end apart: 2, of which 2 were waited for; matrix products, arithmetic and copies ran while one was open for 0% of the time, Pallas kernels for 0%

profile of v1, /device:TPU:11, one launch (start us, length us, event | category | flops | bytes accessed | tf_op | source)
XLA Modules:
  0.0 386.4 jit_solution(16864937108760482247)
XLA Ops:
  6.5 0.0 reduce-scatter.2.cloned.1.call-start
  6.5 0.7 fusion
  7.2 0.7 subtract_bitcast_fusion
  7.9 2.2 convert_select_fusion
  10.1 2.8 pad.4.weight_ref
  12.9 0.6 stack.27.info_ref
  13.5 25.8 %forward.1 = bf16[16,2,256,1024]{3,2,1,0:T(8,128)(2,1)} custom-call(s32[5,16]{1,0:T(8,128)} %stack.27.info_ref, f32[2,128,8192]{2,1,0:T(8,128)} %spec_ref.3, f32[1288,1024]{1,0:T(8,128)} %pad.4.weight_ref, f32[1288,512]{1,0:T(8,128)} %constant.64.clone.bt_ref), custom_call_target="tpu_custom_call" | custom-call | tf_op jit(solution)/shard_map/forward/pallas_call | solution.py:151
  39.3 0.0 reduce-scatter.2.cloned.1.call-update
  39.3 0.0 all-gather.3.cloned.1.call-start
  39.3 176.7 %reduce-scatter.2.cloned.1.call-done = bf16[1,2,256,1024]{3,2,1,0:T(8,128)(2,1)} async-done(((bf16[16,2,256,1024]{3,2,1,0:T(8,128)(2,1)}), bf16[1,2,256,1024]{3,2,1,0:T(8,128)(2,1)}) %reduce-scatter.2.cloned.1.call-update) | async-done | bytes 1048592 | tf_op jit(solution)/shard_map/reduce_scatter | solution.py:268
  216.0 11.5 %middle.1 = bf16[2,256,1024]{2,1,0:T(8,128)(2,1)} custom-call(bf16[2,256,1024]{2,1,0:T(8,128)(2,1)} %bitcast.11, bf16[1,256,1024]{2,1,0:T(8,128)(2,1)} %image_ref.1, bf16[1024,1024]{1,0:T(8,128)(2,1)} %constant.65.clone.cos_ref, bf16[1024,1024]{1,0:T(8,128)(2,1)} %constant.66.clone.sin_ref), custom_call_target="tpu_custom_call" | custom-call | tf_op jit(solution)/shard_map/middle/pallas_call | solution.py:219
  227.5 0.0 all-gather.3.cloned.1.call-update
  227.5 126.2 %all-gather.3.cloned.1.call-done = bf16[32,256,1024]{2,1,0:T(8,128)(2,1)} async-done(((bf16[2,256,1024]{2,1,0:T(8,128)(2,1)}), bf16[32,256,1024]{2,1,0:T(8,128)(2,1)}) %all-gather.3.cloned.1.call-update) | async-done | bytes 16777232 | tf_op jit(solution)/shard_map/all_gather | solution.py:270
  353.7 25.9 %backward.1 = f32[2,128,8192]{2,1,0:T(8,128)} custom-call(s32[5,16]{1,0:T(8,128)} %stack.27.info_ref, f32[2,128,8192]{2,1,0:T(8,128)} %spec_ref.3, bf16[16,2,256,1024]{3,2,1,0:T(8,128)(2,1)} %bitcast.10, f32[1288,1024]{1,0:T(8,128)} %pad.4.weight_ref, f32[1288,512]{1,0:T(8,128)} %constant.64.clone.bt_ref), custom_call_target="tpu_custom_call" | custom-call | tf_op jit(solution)/shard_map/backward/pallas_call | solution.py:188
  (1 shorter events, 0.0 us)
Async XLA Ops:
  6.5 209.5 %reduce-scatter.2.cloned.1.call-start = ((), (), s32[]{:S(2)}) async-start(), calls=%async_computation.1 | async-start | bytes 17825792 | tf_op jit(solution)/shard_map/reduce_scatter | solution.py:268
  39.3 314.4 %all-gather.3.cloned.1.call-start = ((), (), s32[]{:S(2)}) async-start(), calls=%async_computation.2 | async-start | bytes 17825792 | tf_op jit(solution)/shard_map/all_gather | solution.py:270
Sparse Core Ops, SparseCore 0:
  39.4 176.5 reduce-scatter.1
  227.6 126.0 all-gather.2

commit v2 on v1

v2 whole, which is shorter than its diff:
```python
import functools
import math

import jax
import jax.numpy as jnp
import numpy as np
from jax import lax
from jax.experimental import pallas as pl
from jax.experimental.pallas import tpu as pltpu
from jax.sharding import PartitionSpec as P

step_size = 0.5
lane = 128
row_tile = 16
vmem_bytes = 56 * 1024 * 1024


def fourier_tables(crop_width):
    counter = np.arange(crop_width, dtype=np.int64)
    angle = (counter[:, None] * counter[None, :] % crop_width) * (2.0 * math.pi / crop_width)
    factor = 1.0 / math.sqrt(crop_width)
    cos_table = (np.cos(angle) * factor).astype(np.float32).astype(jnp.bfloat16)
    sin_table = (np.sin(angle) * factor).astype(np.float32).astype(jnp.bfloat16)
    return cos_table, sin_table


def tile_weight(pupil_ref, first_row, shift, tile_rows):
    window, crop_width = pupil_ref.shape
    rows = pltpu.roll(pupil_ref[...].astype(jnp.float32), (2 * window - shift) % window, 0)
    shape = (tile_rows, crop_width)
    row = 2 * (first_row + lax.broadcasted_iota(jnp.int32, shape, 0)) - crop_width + 1
    column = 2 * lax.broadcasted_iota(jnp.int32, shape, 1) - crop_width + 1
    inside = row * row + column * column <= crop_width * crop_width
    return jnp.where(inside, rows[:tile_rows], 0.0)


def tile_band(band_ref, shift, tile_rows):
    window, both = band_ref.shape
    rows = pltpu.roll(band_ref[...].astype(jnp.float32), (2 * window - shift) % window, 0)
    rows = rows[:tile_rows]
    turned = jnp.concatenate([-rows[:, both // 2 :], rows[:, : both // 2]], axis=1)
    return jnp.concatenate([rows, turned], axis=0).astype(jnp.bfloat16)


class Windows:
    def __init__(self, tile_rows, slab_columns, crop_width):
        self.tile_rows = tile_rows
        self.crop_width = crop_width
        self.rows = tile_rows + row_tile
        self.columns = crop_width + lane
        self.last_row = crop_width - self.rows
        self.last_column = slab_columns - self.columns

    def row(self, first_row):
        start = jnp.clip(first_row, 0, self.last_row) // row_tile * row_tile
        return pl.multiple_of(start, row_tile)

    def column(self, left):
        start = jnp.minimum(left // lane * lane, self.last_column)
        return pl.multiple_of(start, lane)

    def active(self, first_row):
        return (first_row > -self.tile_rows) & (first_row < self.crop_width)


def forward_kernel(meta_ref, spec_ref, pupil_ref, band_ref, out_ref, *, base, win):
    slot = base + pl.program_id(0)
    first_row, left = meta_ref[0, slot], meta_ref[1, slot]
    active = win.active(first_row)
    tile_rows, crop_width = win.tile_rows, win.crop_width

    @pl.when(jnp.logical_not(active))
    def _():
        out_ref[...] = jnp.zeros_like(out_ref)

    @pl.when(active)
    def _():
        row_shift = first_row - win.row(first_row)
        col_shift = left - win.column(left)
        weight = tile_weight(pupil_ref, first_row, row_shift, tile_rows)
        parts = []
        for part in range(2):
            low = spec_ref[part].astype(jnp.bfloat16).astype(jnp.float32)
            low = pltpu.roll(low, (win.columns - col_shift) % win.columns, 1)[:, :crop_width]
            parts.append((weight * low).astype(jnp.bfloat16))
        pupiled = jnp.concatenate(parts, axis=0)
        table = tile_band(band_ref, row_shift, tile_rows)
        mid = lax.dot_general(
            table, pupiled, (((0,), (0,)), ((), ())), preferred_element_type=jnp.float32
        )
        out_ref[...] = mid.astype(jnp.bfloat16).reshape(out_ref.shape)


def backward_kernel(meta_ref, spec_ref, pupil_ref, band_ref, *refs, slots, win):
    back_refs = refs[: len(slots)]
    out_ref, held, sems = refs[len(slots) :]
    step = pl.program_id(0)
    count = len(slots)
    tile_rows, crop_width = win.tile_rows, win.crop_width

    def fetch(index, buffer):
        for number, back_ref in enumerate(back_refs):

            @pl.when(index == number)
            def _():
                pltpu.make_async_copy(back_ref, held.at[buffer], sems.at[buffer]).start()

    @pl.when(step == 0)
    def _():
        fetch(0, 0)
        out_ref[...] = spec_ref[...]

    @pl.when(step + 1 < count)
    def _():
        fetch(step + 1, (step + 1) % 2)

    buffer = step % 2
    pltpu.make_async_copy(back_refs[0], held.at[buffer], sems.at[buffer]).wait()
    slot = pick(slots, step)
    first_row, left = meta_ref[0, slot], meta_ref[1, slot]

    @pl.when(win.active(first_row))
    def _():
        row_shift = first_row - win.row(first_row)
        col_start = win.column(left)
        weight = tile_weight(pupil_ref, first_row, row_shift, tile_rows) * step_size
        table = tile_band(band_ref, row_shift, tile_rows)
        back = held[buffer].reshape(table.shape[1], crop_width)
        grad = jnp.dot(table, back, preferred_element_type=jnp.float32)
        columns = pl.ds(col_start, win.columns)
        pad = jnp.zeros((tile_rows, win.columns - crop_width), jnp.float32)
        for part in range(2):
            piece = grad[part * tile_rows : (part + 1) * tile_rows] * weight
            piece = pltpu.roll(jnp.concatenate([piece, pad], axis=1), left - col_start, 1)
            out_ref[part, :, columns] = out_ref[part, :, columns] - piece


def pick(values, index):
    result = jnp.int32(values[0])
    for number, value in enumerate(values[1:], 1):
        result = jnp.where(index == number, jnp.int32(value), result)
    return result


def middle_kernel(own_ref, up_ref, down_ref, image_ref, cos_ref, sin_ref, out_ref, mid_ref, sum_ref):
    step = pl.program_id(0)
    _, band, crop_width = own_ref.shape

    @pl.when(step == 0)
    def _():
        total = own_ref[...].astype(jnp.float32) + up_ref[...].astype(jnp.float32)
        total = total + down_ref[...].astype(jnp.float32)
        mid_ref[...] = total.astype(jnp.bfloat16).reshape(2 * band, crop_width)
        sum_ref[...] = jnp.zeros_like(sum_ref)

    dot = functools.partial(jnp.dot, preferred_element_type=jnp.float32)
    mid = mid_ref[...]
    by_cos, by_sin = dot(mid, cos_ref[...]), dot(mid, sin_ref[...])
    field_real = by_cos[:band] - by_sin[band:]
    field_imag = by_sin[:band] + by_cos[band:]
    magnitude = jnp.sqrt(field_real * field_real + field_imag * field_imag)
    keeping = 1.0 - image_ref[0].astype(jnp.float32) / jnp.maximum(magnitude, 1.0)
    resid = jnp.concatenate([field_real * keeping, field_imag * keeping], axis=0)
    resid = resid.astype(jnp.bfloat16)

    def turned(table):
        return lax.dot_general(
            resid, table, (((1,), (1,)), ((), ())), preferred_element_type=jnp.float32
        )

    by_cos, by_sin = turned(cos_ref[...]), turned(sin_ref[...])
    sum_ref[0] += by_cos[:band] + by_sin[band:]
    sum_ref[1] += by_cos[band:] - by_sin[:band]

    @pl.when(step == pl.num_programs(0) - 1)
    def _():
        out_ref[...] = sum_ref[...].astype(jnp.bfloat16)


def params():
    return pltpu.CompilerParams(vmem_limit_bytes=vmem_bytes)


def cost(count, win, band, moved):
    flops = 16 * count * win.tile_rows * band * win.crop_width
    return pl.CostEstimate(flops=flops, bytes_accessed=moved, transcendentals=0)


def forward(meta, spectrum, pupil, band_table, base, count):
    _, tile_rows, slab_columns = spectrum.shape
    crop_width = pupil.shape[1]
    band = band_table.shape[1] // 2
    win = Windows(tile_rows, slab_columns, crop_width)

    def row(i, meta):
        return (win.row(meta[0, base + i]), 0)

    return pl.pallas_call(
        functools.partial(forward_kernel, base=base, win=win),
        grid_spec=pltpu.PrefetchScalarGridSpec(
            num_scalar_prefetch=1,
            grid=(count,),
            in_specs=[
                pl.BlockSpec(
                    (pl.Element(2), pl.Element(tile_rows), pl.Element(win.columns)),
                    lambda i, meta: (0, 0, win.column(meta[1, base + i])),
                ),
                pl.BlockSpec((pl.Element(win.rows), pl.Element(crop_width)), row),
                pl.BlockSpec((pl.Element(win.rows), pl.Element(2 * band)), row),
            ],
            out_specs=pl.BlockSpec((1, 2, band, crop_width), lambda i, meta: (i, 0, 0, 0)),
        ),
        out_shape=jax.ShapeDtypeStruct((count, 2, band, crop_width), jnp.bfloat16),
        compiler_params=params(),
        cost_estimate=cost(count, win, band, count * 3000000),
        name="forward",
    )(meta, spectrum, pupil, band_table)


def backward(meta, spectrum, pupil, band_table, slots, backs):
    _, tile_rows, slab_columns = spectrum.shape
    crop_width = pupil.shape[1]
    band = band_table.shape[1] // 2
    win = Windows(tile_rows, slab_columns, crop_width)
    count = len(slots)

    def row(i, meta):
        return (win.row(meta[0, pick(slots, i)]), 0)

    return pl.pallas_call(
        functools.partial(backward_kernel, slots=slots, win=win),
        grid_spec=pltpu.PrefetchScalarGridSpec(
            num_scalar_prefetch=1,
            grid=(count,),
            in_specs=[
                pl.BlockSpec(
                    spectrum.shape, lambda i, meta: (0, 0, 0), pipeline_mode=pl.Buffered(1)
                ),
                pl.BlockSpec((pl.Element(win.rows), pl.Element(crop_width)), row),
                pl.BlockSpec((pl.Element(win.rows), pl.Element(2 * band)), row),
            ]
            + [pl.BlockSpec(memory_space=pl.ANY)] * count,
            out_specs=pl.BlockSpec(spectrum.shape, lambda i, meta: (0, 0, 0)),
            scratch_shapes=[
                pltpu.VMEM((2, 2, band, crop_width), jnp.bfloat16),
                pltpu.SemaphoreType.DMA((2,)),
            ],
        ),
        out_shape=jax.ShapeDtypeStruct(spectrum.shape, jnp.float32),
        compiler_params=params(),
        cost_estimate=cost(count, win, band, count * 3000000 + 16 * 1024 * 1024),
        name="backward",
    )(meta, spectrum, pupil, band_table, *backs)


def middle(own, up, down, image, cos_table, sin_table):
    _, band, crop_width = own.shape
    block = min(256, crop_width)
    table = pl.BlockSpec((crop_width, block), lambda j: (0, j))
    whole = pl.BlockSpec((2, band, crop_width), lambda j: (0, 0, 0))
    return pl.pallas_call(
        middle_kernel,
        grid=(crop_width // block,),
        in_specs=[
            whole,
            whole,
            whole,
            pl.BlockSpec((1, band, block), lambda j: (0, 0, j)),
            table,
            table,
        ],
        out_specs=whole,
        out_shape=jax.ShapeDtypeStruct((2, band, crop_width), jnp.bfloat16),
        scratch_shapes=[
            pltpu.VMEM((2 * band, crop_width), jnp.bfloat16),
            pltpu.VMEM((2, band, crop_width), jnp.float32),
        ],
        compiler_params=params(),
        name="middle",
    )(own, up, down, image, cos_table, sin_table)


def total(*terms):
    return sum(term.astype(jnp.float32) for term in terms).astype(jnp.bfloat16)


def far_first(planes):
    rows = []
    for z in range(planes):
        upward = 2 * z < planes
        rows.append(
            sorted(range(planes), key=lambda q: (-abs(q - z), (q < z) if upward else (q > z)))
        )
    return rows


def chosen(plane, options):
    groups = []
    for z, value in options.items():
        for entry in groups:
            if entry[0] is value:
                entry[1].append(z)
                break
        else:
            groups.append((value, [z]))
    result = groups[0][0]
    for value, members in groups[1:]:
        here = functools.reduce(jnp.logical_or, [plane == z for z in members])
        result = jnp.where(here, value, result)
    return result


def per_device(spectrum, pupil, measured, centre_rows, centre_cols):
    count = lax.axis_size("ty")
    planes = count // 4
    position = lax.axis_index("ty")
    plane, corner = position // 4, position % 4
    _, tile_rows, slab_columns = spectrum.shape
    crop_width = pupil.shape[0]
    band = measured.shape[1]
    band_start = (crop_width - band) // 2
    cos_table, sin_table = fourier_tables(crop_width)
    chosen_rows = slice(band_start, band_start + band)
    band_table = jnp.asarray(
        np.concatenate([cos_table[:, chosen_rows], sin_table[:, chosen_rows]], axis=1)
    )
    cos_table, sin_table = jnp.asarray(cos_table), jnp.asarray(sin_table)

    order = far_first(planes)
    flips = jnp.asarray([3, 1, 2, 0], jnp.int32)
    my_order = lax.dynamic_index_in_dim(jnp.asarray(order, jnp.int32), plane, keepdims=False)
    ids = (my_order[:, None] * 4 + (corner ^ flips)[None, :]).reshape(-1)
    match = ids[:, None] == jnp.arange(count, dtype=jnp.int32)[None, :]
    half = crop_width // 2
    tops = jnp.sum(jnp.where(match, centre_rows[None, :], 0), axis=1) - half
    lefts = jnp.sum(jnp.where(match, centre_cols[None, :], 0), axis=1) - half
    meta = jnp.stack([position * tile_rows - tops, lefts]).astype(jnp.int32)

    def sibling(value):
        return lax.ppermute(value, "ty", [(i, i ^ 1) for i in range(count)])

    def across(value):
        return lax.ppermute(value, "ty", [(i, i ^ 2) for i in range(count)])

    def along(value, sources, by):
        pairs = [(4 * z + i, 4 * (z + by) + i) for z in sources for i in range(4)]
        return lax.ppermute(value, "ty", pairs)

    def partial(base, number):
        return forward(meta, spectrum, pupil, band_table, base, number)

    summed = []
    received = []
    up = down = None
    up_total = down_total = None

    def z_step(s):
        nonlocal up, down
        sources = [z for z in range(planes - 1) if z < s]
        value = chosen(plane, {z: summed[order[z].index(planes - s + z)] for z in sources})
        up = along(total(value, up) if up is not None else value, sources, 1)
        sources = [z for z in range(1, planes) if planes - 1 - z < s]
        value = chosen(plane, {z: summed[order[z].index(s - planes + z)] for z in sources})
        down = along(total(value, down) if down is not None else value, sources, -1)

    for j in range(planes):
        if j == 0:
            theirs = [partial(0, 1)[0], partial(1, 1)[0]]
            mine = [partial(2, 1)[0], partial(3, 1)[0]]
            came = [sibling(theirs[0]), sibling(theirs[1])]
        else:
            theirs = partial(4 * j, 2)
            mine = partial(4 * j + 2, 2)
            came = sibling(theirs)
        outgoing = total(mine[0], came[0])
        if j >= 2:
            outgoing, received[j - 2] = lax.optimization_barrier((outgoing, received[j - 2]))
        received.append(across(outgoing))
        if j >= 1:
            z_step(j)
        summed.append(total(mine[1], came[1], received[j]))
    band_back = middle(summed[-1], up, down, measured, cos_table, sin_table)

    near = [list(reversed(row)) for row in order]
    from_below, from_above = [band_back], [band_back]
    column = [band_back]
    other = [across(band_back)]
    result = spectrum
    for s in range(1, planes):
        from_below.append(along(from_below[-1], range(s - 1, planes - 1), 1))
        from_above.append(along(from_above[-1], range(1, planes - s + 1), -1))
        options = {}
        for z in range(planes):
            q = near[z][s]
            options[z] = from_below[z - q] if q < z else from_above[q - z]
        value = chosen(plane, options)
        column.append(value)
        other.append(across(value))

    def slot(j, kind):
        return 4 * (planes - 1 - j) + kind

    slots, backs = [], []
    for j in range(planes):
        slots += [slot(j, 3), slot(j, 1)]
        backs += [column[j], sibling(column[j])]
        if j < planes - 1:
            slots += [slot(j, 2), slot(j, 0)]
            backs += [other[j], sibling(other[j])]
    result = backward(meta, result, pupil, band_table, slots, backs)
    slots = [slot(planes - 1, 2), slot(planes - 1, 0)]
    backs = [other[-1], sibling(other[-1])]
    return backward(meta, result, pupil, band_table, slots, backs)


def solution(mesh):
    return jax.shard_map(
        per_device,
        mesh=mesh,
        in_specs=(
            P(None, ("groups", "ty"), None),
            P(),
            P(("groups", "ty"), None, None),
            P("groups"),
            P("groups"),
        ),
        out_specs=P(None, ("groups", "ty"), None),
        check_vma=False,
    )
```

time: 390 us -> 332 us (0.85)
  waiting for transfers between devices: 303 us -> 101 us
  starting transfers between devices: 0.04 us -> 101 us
  Pallas kernels: 63.2 us -> 94.8 us
  other arithmetic: 3.53 us -> 28.1 us
  between operations: 13.4 us -> 0.53 us
    reduce_scatter x1 -> x0, waiting for transfers between devices: 177 us -> none  [per_device(): mid = lax.psum_scatter(partial, 'ty', scatter_dimension=0, tiled=True)[0]]
    all_gather x1 -> x0, waiting for transfers between devices: 126 us -> none  [per_device(): gathered = lax.all_gather(back, 'ty')]
    ppermute x0 -> x33, waiting for transfers between devices: none -> 101 us  [the longest x12 66 us: along(): return lax.ppermute(value, 'ty', pairs)]
    ppermute x0 -> x33, starting transfers between devices: none -> 101 us  [the longest x13 63.5 us: sibling(): return lax.ppermute(value, 'ty', [(i, i ^ 1) for i in range(count)])]
    pallas_call x3 -> x13, Pallas kernels: 63.2 us -> 94.8 us  [the longest x10 46.4 us: forward(): pl.pallas_call(functools.partial(forward_kernel, base=base, win=win), gri...]
    convert_element_type x0 -> x9, other arithmetic: none -> 23.1 us  [total(): sum((term.astype(jnp.float32) for term in terms)).astype(jnp.bfloat16)]
    unnamed x0 -> x50, local copies, waits for them, and re-layouts: none -> 4.02 us
  transfers between devices with their start and end apart: 2 -> 33, of which waited for: 2 -> 15; matrix products, arithmetic and copies ran while one was open for 0% -> 8% of each run, Pallas kernels for 0% -> 20%
where the time goes in v2:
time: 332 us; the launch traced here: 329 us
  starting transfers between devices  101 us (30%)
  waiting for transfers between devices  101 us (30%)
  Pallas kernels  94.8 us (29%)
  other arithmetic  28.1 us (8%)
  local copies, waits for them, and re-layouts  4.11 us (1%)
    ppermute x12, waiting for transfers between devices, along(): return lax.ppermute(value, 'ty', pairs)  66 us
    ppermute x13, starting transfers between devices, sibling(): return lax.ppermute(value, 'ty', [(i, i ^ 1) for i in range(count)])  63.5 us
    pallas_call x10, Pallas kernels, forward(): pl.pallas_call(functools.partial(forward_kernel, base=base, win=win), gri...  46.4 us
    ppermute x8, waiting for transfers between devices, across(): return lax.ppermute(value, 'ty', [(i, i ^ 2) for i in range(count)])  34.9 us
    pallas_call x2, Pallas kernels, backward(): pl.pallas_call(functools.partial(backward_kernel, slots=slots, win=win),...  34.5 us
    ppermute x12, starting transfers between devices, along(): return lax.ppermute(value, 'ty', pairs)  30.8 us
    convert_element_type x9, other arithmetic, total(): sum((term.astype(jnp.float32) for term in terms)).astype(jnp.bfloat16)  23.1 us
    pallas_call x1, Pallas kernels, middle(): pl.pallas_call(middle_kernel, grid=(crop_width // block,), in_specs=[whol...  14 us
  transfers between devices with their start and end apart: 33, of which 15 were waited for; matrix products, arithmetic and copies ran while one was open for 8% of the time, Pallas kernels for 20%

profile of v2, /device:TPU:11, one launch (start us, length us, event | category | flops | bytes accessed | tf_op | source)
XLA Modules:
  0.0 329.1 jit_solution(240897497833238475)
XLA Ops:
  2.9 4.2 %forward.17 = bf16[1,2,256,1024]{3,2,1,0:T(8,128)(2,1)} custom-call(s32[2,16]{1,0:T(2,128)} %pad_add_fusion.meta_ref, f32[2,128,8192]{2,1,0:T(8,128)} %spec_ref.21, bf16[1024,1024]{1,0:T(8,128)(2,1)} %pupil_ref.23, bf16[1024,512]{1,0:T(8,128)(2,1)} %constant.55.clone.band_ref), custom_call_target="tpu_custom_call" | custom-call | flops 536870912 | bytes 3000000 | tf_op jit(solution)/shard_map/forward/pallas_call | solution.py:198
  7.1 5.4 %forward.13 = bf16[2,2,256,1024]{3,2,1,0:T(8,128)(2,1)} custom-call(s32[2,16]{1,0:T(2,128)} %pad_add_fusion.meta_ref, f32[2,128,8192]{2,1,0:T(8,128)} %spec_ref.21, bf16[1024,1024]{1,0:T(8,128)(2,1)} %pupil_ref.23, bf16[1024,512]{1,0:T(8,128)(2,1)} %constant.55.clone.band_ref), custom_call_target="tpu_custom_call" | custom-call | flops 1073741824 | bytes 6000000 | tf_op jit(solution)/shard_map/forward/pallas_call | solution.py:198
  12.5 4.2 %forward.19 = bf16[1,2,256,1024]{3,2,1,0:T(8,128)(2,1)} custom-call(s32[2,16]{1,0:T(2,128)} %pad_add_fusion.meta_ref, f32[2,128,8192]{2,1,0:T(8,128)} %spec_ref.21, bf16[1024,1024]{1,0:T(8,128)(2,1)} %pupil_ref.23, bf16[1024,512]{1,0:T(8,128)(2,1)} %constant.55.clone.band_ref), custom_call_target="tpu_custom_call" | custom-call | flops 536870912 | bytes 3000000 | tf_op jit(solution)/shard_map/forward/pallas_call | solution.py:198
  16.8 3.2 forward.16
  20.0 1.6 fusion.2
  21.6 3.0 collective-permute-start.6
  24.6 4.6 %forward.15 = bf16[2,2,256,1024]{3,2,1,0:T(8,128)(2,1)} custom-call(s32[2,16]{1,0:T(2,128)} %pad_add_fusion.meta_ref, f32[2,128,8192]{2,1,0:T(8,128)} %spec_ref.21, bf16[1024,1024]{1,0:T(8,128)(2,1)} %pupil_ref.23, bf16[1024,512]{1,0:T(8,128)(2,1)} %constant.55.clone.band_ref), custom_call_target="tpu_custom_call" | custom-call | flops 1073741824 | bytes 6000000 | tf_op jit(solution)/shard_map/forward/pallas_call | solution.py:198
  29.2 1.0 collective-permute-start.4
  30.1 4.2 %forward.18 = bf16[1,2,256,1024]{3,2,1,0:T(8,128)(2,1)} custom-call(s32[2,16]{1,0:T(2,128)} %pad_add_fusion.meta_ref, f32[2,128,8192]{2,1,0:T(8,128)} %spec_ref.21, bf16[1024,1024]{1,0:T(8,128)(2,1)} %pupil_ref.23, bf16[1024,512]{1,0:T(8,128)(2,1)} %constant.55.clone.band_ref), custom_call_target="tpu_custom_call" | custom-call | flops 536870912 | bytes 3000000 | tf_op jit(solution)/shard_map/forward/pallas_call | solution.py:198
  34.4 4.8 %forward.12 = bf16[2,2,256,1024]{3,2,1,0:T(8,128)(2,1)} custom-call(s32[2,16]{1,0:T(2,128)} %pad_add_fusion.meta_ref, f32[2,128,8192]{2,1,0:T(8,128)} %spec_ref.21, bf16[1024,1024]{1,0:T(8,128)(2,1)} %pupil_ref.23, bf16[1024,512]{1,0:T(8,128)(2,1)} %constant.55.clone.band_ref), custom_call_target="tpu_custom_call" | custom-call | flops 1073741824 | bytes 6000000 | tf_op jit(solution)/shard_map/forward/pallas_call | solution.py:198
  39.2 1.0 copy-done.24
  40.2 7.6 %collective-permute-done.6 = bf16[2,256,1024]{2,1,0:T(8,128)(2,1)} collective-permute-done((bf16[2,256,1024]{2,1,0:T(8,128)(2,1)S(1)}, bf16[2,256,1024]{2,1,0:T(8,128)(2,1)}, u32[]{:S(2)}, u32[]{:S(2)}) %collective-permute-start.6) | collective-permute-done | bytes 1048608 | tf_op jit(solution)/shard_map/ppermute | solution.py:343
  47.8 2.2 fusion.1
  50.0 1.6 collective-permute-start.12
  51.6 1.6 fusion.7
  53.3 1.1 collective-permute-start.2
  54.4 1.5 collective-permute-start.9
  55.9 5.4 %forward.11 = bf16[2,2,256,1024]{3,2,1,0:T(8,128)(2,1)} custom-call(s32[2,16]{1,0:T(2,128)} %pad_add_fusion.meta_ref, f32[2,128,8192]{2,1,0:T(8,128)} %spec_ref.21, bf16[1024,1024]{1,0:T(8,128)(2,1)} %pupil_ref.23, bf16[1024,512]{1,0:T(8,128)(2,1)} %constant.55.clone.band_ref), custom_call_target="tpu_custom_call" | custom-call | flops 1073741824 | bytes 6000000 | tf_op jit(solution)/shard_map/forward/pallas_call | solution.py:198
  61.3 0.9 collective-permute-start
  62.2 5.5 %forward.14 = bf16[2,2,256,1024]{3,2,1,0:T(8,128)(2,1)} custom-call(s32[2,16]{1,0:T(2,128)} %pad_add_fusion.meta_ref, f32[2,128,8192]{2,1,0:T(8,128)} %spec_ref.21, bf16[1024,1024]{1,0:T(8,128)(2,1)} %pupil_ref.23, bf16[1024,512]{1,0:T(8,128)(2,1)} %constant.55.clone.band_ref), custom_call_target="tpu_custom_call" | custom-call | flops 1073741824 | bytes 6000000 | tf_op jit(solution)/shard_map/forward/pallas_call | solution.py:198
  67.7 3.4 %fusion.8 = bf16[2,256,1024]{2,1,0:T(8,128)(2,1)} fusion(bf16[2,2,256,1024]{3,2,1,0:T(8,128)(2,1)S(1)} %collective-permute-done.4, bf16[2,2,256,1024]{3,2,1,0:T(8,128)(2,1)} %forward.14), kind=kLoop, calls=%fused_computation.20 | loop fusion | flops 2097152 | bytes 3145728 | tf_op jit(solution)/shard_map/convert_element_type | solution.py:284
  71.2 6.0 %collective-permute-done.2 = bf16[2,256,1024]{2,1,0:T(8,128)(2,1)} collective-permute-done((bf16[2,256,1024]{2,1,0:T(8,128)(2,1)}, bf16[2,256,1024]{2,1,0:T(8,128)(2,1)}, u32[]{:S(2)}, u32[]{:S(2)}) %collective-permute-start.2) | collective-permute-done | bytes 1048608 | tf_op jit(solution)/shard_map/ppermute | solution.py:343
  77.2 3.7 %add_convert_fusion.1 = (bf16[2,256,1024]{2,1,0:T(8,128)(2,1)}, bf16[2,256,1024]{2,1,0:T(8,128)(2,1)S(1)}) fusion(bf16[2,256,1024]{2,1,0:T(8,128)(2,1)} %collective-permute-done.12, bf16[2,256,1024]{2,1,0:T(8,128)(2,1)S(1)} %fusion.1, pred[]{:T(512)S(6)} %eq.19, bf16[2,256,1024]{2,1,0:T(8,128)(2,1)} %collective-permute-done.2, ...), kind=kLoop, calls=%fused_computation.12 | loop fusion | flops 5767168 | bytes 7340033 | tf_op jit(solution)/shard_map/convert_element_type | solution.py:284
  80.9 2.8 add_convert_fusion.3
  83.8 4.1 %collective-permute-start.10 = (bf16[2,256,1024]{2,1,0:T(8,128)(2,1)}, bf16[2,256,1024]{2,1,0:T(8,128)(2,1)S(1)}, u32[]{:S(2)}, u32[]{:S(2)}) collective-permute-start(bf16[2,256,1024]{2,1,0:T(8,128)(2,1)} %add_convert_fusion.3), channel_id=1, source_target_pairs={{0,4},{1,5},{2,6},{3,7},{4,8},{5,9},{6,10},{7,11},{16,20},{17,21},... | collective-permute-start | bytes 3145736 | tf_op jit(solution)/shard_map/ppermute | solution.py:347
  87.9 1.3 collective-permute-start.13
  89.2 4.8 %forward.10 = bf16[2,2,256,1024]{3,2,1,0:T(8,128)(2,1)} custom-call(s32[2,16]{1,0:T(2,128)} %pad_add_fusion.meta_ref, f32[2,128,8192]{2,1,0:T(8,128)} %spec_ref.21, bf16[1024,1024]{1,0:T(8,128)(2,1)} %pupil_ref.23, bf16[1024,512]{1,0:T(8,128)(2,1)} %constant.55.clone.band_ref), custom_call_target="tpu_custom_call" | custom-call | flops 1073741824 | bytes 6000000 | tf_op jit(solution)/shard_map/forward/pallas_call | solution.py:198
  94.0 2.1 fusion.6
  96.7 3.0 collective-permute-done.7
  99.7 8.0 %collective-permute-done.10 = bf16[2,256,1024]{2,1,0:T(8,128)(2,1)S(1)} collective-permute-done((bf16[2,256,1024]{2,1,0:T(8,128)(2,1)}, bf16[2,256,1024]{2,1,0:T(8,128)(2,1)S(1)}, u32[]{:S(2)}, u32[]{:S(2)}) %collective-permute-start.10) | collective-permute-done | bytes 1048608 | tf_op jit(solution)/shard_map/ppermute | solution.py:347
  107.7 3.7 %collective-permute-done.13 = bf16[2,256,1024]{2,1,0:T(8,128)(2,1)S(1)} collective-permute-done((bf16[2,256,1024]{2,1,0:T(8,128)(2,1)}, bf16[2,256,1024]{2,1,0:T(8,128)(2,1)S(1)}, u32[]{:S(2)}, u32[]{:S(2)}) %collective-permute-start.13) | collective-permute-done | bytes 1048608 | tf_op jit(solution)/shard_map/ppermute | solution.py:347
  111.4 2.7 add_convert_fusion
  114.2 1.9 collective-permute-start.11
  116.1 3.6 %collective-permute-start.14 = (bf16[2,256,1024]{2,1,0:T(8,128)(2,1)S(1)}, bf16[2,256,1024]{2,1,0:T(8,128)(2,1)S(1)}, u32[]{:S(2)}, u32[]{:S(2)}) collective-permute-start(bf16[2,256,1024]{2,1,0:T(8,128)(2,1)S(1)} %get-tuple-element.13), channel_id=1, source_target_pairs={{4,0},{5,1},{6,2},{7,3},{8,4},{9,5},{10,6},{11,7},{12,8},{13,9},{1... | collective-permute-start | bytes 3145736 | tf_op jit(solution)/shard_map/ppermute | solution.py:347
  119.7 1.6 collective-permute-done.3
  121.3 2.8 fusion.5.own_ref
  124.2 12.4 %collective-permute-done.11.up_ref = bf16[2,256,1024]{2,1,0:T(8,128)(2,1)S(1)} collective-permute-done((bf16[2,256,1024]{2,1,0:T(8,128)(2,1)S(1)}, bf16[2,256,1024]{2,1,0:T(8,128)(2,1)S(1)}, u32[]{:S(2)}, u32[]{:S(2)}) %collective-permute-start.11) | collective-permute-done | bytes 1048608 | tf_op jit(solution)/shard_map/ppermute | solution.py:347
  136.6 1.9 collective-permute-done.14.down_ref
  138.5 1.0 copy-done.23
  139.5 14.0 %middle.1.refs_0_ = bf16[2,256,1024]{2,1,0:T(8,128)(2,1)} custom-call(bf16[2,256,1024]{2,1,0:T(8,128)(2,1)} %fusion.5.own_ref, bf16[2,256,1024]{2,1,0:T(8,128)(2,1)} %copy-done.22, bf16[2,256,1024]{2,1,0:T(8,128)(2,1)} %copy-done.23, bf16[1,256,1024]{2,1,0:T(8,128)(2,1)} %image_ref.1, bf16[1024,1024]{1,0:T(8,128)(2,1)} %constant.56.clone.cos_ref, ...), custom_call_target="tpu_custom_call" | custom-call | tf_op jit(solution)/shard_map/middle/pallas_call | solution.py:261
  153.4 1.9 collective-permute-start.18
  155.3 3.4 %collective-permute-start.19 = (bf16[2,256,1024]{2,1,0:T(8,128)(2,1)}, bf16[2,256,1024]{2,1,0:T(8,128)(2,1)S(1)}, u32[]{:S(2)}, u32[]{:S(2)}) collective-permute-start(bf16[2,256,1024]{2,1,0:T(8,128)(2,1)} %middle.1.refs_0_), channel_id=1, source_target_pairs={{4,0},{5,1},{6,2},{7,3},{8,4},{9,5},{10,6},{11,7},{12,8},{13,9},{1... | collective-permute-start | bytes 3145736 | tf_op jit(solution)/shard_map/ppermute | solution.py:347
  158.8 16.3 %collective-permute-done.18 = bf16[2,256,1024]{2,1,0:T(8,128)(2,1)S(1)} collective-permute-done((bf16[2,256,1024]{2,1,0:T(8,128)(2,1)}, bf16[2,256,1024]{2,1,0:T(8,128)(2,1)S(1)}, u32[]{:S(2)}, u32[]{:S(2)}) %collective-permute-start.18) | collective-permute-done | bytes 1048608 | tf_op jit(solution)/shard_map/ppermute | solution.py:347
  175.1 3.2 collective-permute-start.23
  178.3 1.9 collective-permute-start.24
  180.3 14.6 %collective-permute-done.23 = bf16[2,256,1024]{2,1,0:T(8,128)(2,1)} collective-permute-done((bf16[2,256,1024]{2,1,0:T(8,128)(2,1)S(1)}, bf16[2,256,1024]{2,1,0:T(8,128)(2,1)}, u32[]{:S(2)}, u32[]{:S(2)}) %collective-permute-start.23) | collective-permute-done | bytes 1048608 | tf_op jit(solution)/shard_map/ppermute | solution.py:347
  194.8 1.7 collective-permute-start.28
  196.5 1.8 collective-permute-done.24
  198.3 4.6 %collective-permute-start.29 = (bf16[2,256,1024]{2,1,0:T(8,128)(2,1)}, bf16[2,256,1024]{2,1,0:T(8,128)(2,1)}, u32[]{:S(2)}, u32[]{:S(2)}) collective-permute-start(bf16[2,256,1024]{2,1,0:T(8,128)(2,1)} %collective-permute-done.24), channel_id=1, source_target_pairs={{4,0},{5,1},{6,2},{7,3},{20,16},{21,17},{22,18},{23,19}} | collective-permute-start | bytes 3145736 | tf_op jit(solution)/shard_map/ppermute | solution.py:347
  202.9 9.1 %collective-permute-start.15 = (bf16[2,256,1024]{2,1,0:T(8,128)(2,1)}, bf16[2,256,1024]{2,1,0:T(8,128)(2,1)S(1)}, u32[]{:S(2)}, u32[]{:S(2)}) collective-permute-start(bf16[2,256,1024]{2,1,0:T(8,128)(2,1)} %middle.1.refs_0_), channel_id=1, source_target_pairs={{0,1},{1,0},{2,3},{3,2},{4,5},{5,4},{6,7},{7,6},{8,9},{9,8},{10,11... | collective-permute-start | bytes 3145736 | tf_op jit(solution)/shard_map/ppermute | solution.py:340
  212.1 7.3 %collective-permute-done.29 = bf16[2,256,1024]{2,1,0:T(8,128)(2,1)} collective-permute-done((bf16[2,256,1024]{2,1,0:T(8,128)(2,1)}, bf16[2,256,1024]{2,1,0:T(8,128)(2,1)}, u32[]{:S(2)}, u32[]{:S(2)}) %collective-permute-start.29) | collective-permute-done | bytes 1048608 | tf_op jit(solution)/shard_map/ppermute | solution.py:347
  219.4 2.2 select_select_fusion
  221.7 1.5 collective-permute-start.26
  223.2 8.5 %collective-permute-start.20 = (bf16[2,256,1024]{2,1,0:T(8,128)(2,1)S(1)}, bf16[2,256,1024]{2,1,0:T(8,128)(2,1)S(1)}, u32[]{:S(2)}, u32[]{:S(2)}) collective-permute-start(bf16[2,256,1024]{2,1,0:T(8,128)(2,1)S(1)} %get-tuple-element.17.refs_4_), channel_id=1, source_target_pairs={{0,1},{1,0},{2,3},{3,2},{4,5},{5,4},{6,7},{7,6},{8,9},{9,8},{10,11... | collective-permute-start | bytes 3145736 | tf_op jit(solution)/shard_map/ppermute | solution.py:340
  231.9 6.5 %collective-permute-done.21.refs_6_ = bf16[2,256,1024]{2,1,0:T(8,128)(2,1)S(1)} collective-permute-done((bf16[2,256,1024]{2,1,0:T(8,128)(2,1)S(1)}, bf16[2,256,1024]{2,1,0:T(8,128)(2,1)S(1)}, u32[]{:S(2)}, u32[]{:S(2)}) %collective-permute-start.21) | collective-permute-done | bytes 1048608 | tf_op jit(solution)/shard_map/ppermute | solution.py:343
  238.4 17.4 %collective-permute-start.30 = (bf16[2,256,1024]{2,1,0:T(8,128)(2,1)S(1)}, bf16[2,256,1024]{2,1,0:T(8,128)(2,1)S(1)}, u32[]{:S(2)}, u32[]{:S(2)}) collective-permute-start(bf16[2,256,1024]{2,1,0:T(8,128)(2,1)S(1)} %get-tuple-element.15.refs_12_), channel_id=1, source_target_pairs={{0,1},{1,0},{2,3},{3,2},{4,5},{5,4},{6,7},{7,6},{8,9},{9,8},{10,11... | collective-permute-start | bytes 3145736 | tf_op jit(solution)/shard_map/ppermute | solution.py:340
  255.8 5.1 %collective-permute-done.26.refs_10_ = bf16[2,256,1024]{2,1,0:T(8,128)(2,1)S(1)} collective-permute-done((bf16[2,256,1024]{2,1,0:T(8,128)(2,1)S(1)}, bf16[2,256,1024]{2,1,0:T(8,128)(2,1)S(1)}, u32[]{:S(2)}, u32[]{:S(2)}) %collective-permute-start.26) | collective-permute-done | bytes 1048608 | tf_op jit(solution)/shard_map/ppermute | solution.py:343
  260.9 17.4 %collective-permute-start.22 = (bf16[2,256,1024]{2,1,0:T(8,128)(2,1)S(1)}, bf16[2,256,1024]{2,1,0:T(8,128)(2,1)S(1)}, u32[]{:S(2)}, u32[]{:S(2)}) collective-permute-start(bf16[2,256,1024]{2,1,0:T(8,128)(2,1)S(1)} %collective-permute-done.21.refs_6_), channel_id=1, source_target_pairs={{0,1},{1,0},{2,3},{3,2},{4,5},{5,4},{6,7},{7,6},{8,9},{9,8},{10,11... | collective-permute-start | bytes 3145736 | tf_op jit(solution)/shard_map/ppermute | solution.py:340
  278.3 5.1 %collective-permute-done.31.refs_0_ = bf16[2,256,1024]{2,1,0:T(8,128)(2,1)} collective-permute-done((bf16[2,256,1024]{2,1,0:T(8,128)(2,1)S(1)}, bf16[2,256,1024]{2,1,0:T(8,128)(2,1)}, u32[]{:S(2)}, u32[]{:S(2)}) %collective-permute-start.31) | collective-permute-done | bytes 1048608 | tf_op jit(solution)/shard_map/ppermute | solution.py:343
  283.4 8.9 %collective-permute-start.32 = (bf16[2,256,1024]{2,1,0:T(8,128)(2,1)}, bf16[2,256,1024]{2,1,0:T(8,128)(2,1)}, u32[]{:S(2)}, u32[]{:S(2)}) collective-permute-start(bf16[2,256,1024]{2,1,0:T(8,128)(2,1)} %collective-permute-done.31.refs_0_), channel_id=1, source_target_pairs={{0,1},{1,0},{2,3},{3,2},{4,5},{5,4},{6,7},{7,6},{8,9},{9,8},{10,11... | collective-permute-start | bytes 3145736 | tf_op jit(solution)/shard_map/ppermute | solution.py:340
  292.4 1.0 copy-done.20
  293.3 1.0 copy-done.21
  294.4 24.1 %backward.2.spec_ref = f32[2,128,8192]{2,1,0:T(8,128)} custom-call(s32[2,16]{1,0:T(2,128)} %pad_add_fusion.meta_ref, f32[2,128,8192]{2,1,0:T(8,128)} %spec_ref.21, bf16[1024,1024]{1,0:T(8,128)(2,1)} %pupil_ref.23, bf16[1024,512]{1,0:T(8,128)(2,1)} %constant.55.clone.band_ref, bf16[2,256,1024]{2,1,0:T(8,128)(2,1)} %middle.1.refs_0_, ...), custom_call_target="tpu_custom_call" | custom-call | flops 7516192768 | bytes 58777216 | tf_op jit(solution)/shard_map/backward/pallas_call | solution.py:230
  318.5 10.4 %backward.3 = f32[2,128,8192]{2,1,0:T(8,128)} custom-call(s32[2,16]{1,0:T(2,128)} %pad_add_fusion.meta_ref, f32[2,128,8192]{2,1,0:T(8,128)} %backward.2.spec_ref, bf16[1024,1024]{1,0:T(8,128)(2,1)} %pupil_ref.23, bf16[1024,512]{1,0:T(8,128)(2,1)} %constant.55.clone.band_ref, bf16[2,256,1024]{2,1,0:T(8,128)(2,1)} %collective-permute-done.31.refs_0_, ...), custom_call_target="tpu_custom_call" | custom-call | flops 1073741824 | bytes 22777216 | tf_op jit(solution)/shard_map/backward/pallas_call | solution.py:230
  (82 shorter events, 4.0 us)
Async XLA Ops:
  7.1 12.8 %collective-permute-start.5 = (bf16[2,256,1024]{2,1,0:T(8,128)(2,1)}, bf16[2,256,1024]{2,1,0:T(8,128)(2,1)S(1)}, u32[]{:S(2)}, u32[]{:S(2)}) collective-permute-start(bf16[2,256,1024]{2,1,0:T(8,128)(2,1)} %bitcast.38), channel_id=1, source_target_pairs={{0,1},{1,0},{2,3},{3,2},{4,5},{5,4},{6,7},{7,6},{8,9},{9,8},{10,11... | collective-permute-start | bytes 3145736 | tf_op jit(solution)/shard_map/ppermute | solution.py:340
  12.5 39.1 %collective-permute-start.1 = (bf16[2,2,256,1024]{3,2,1,0:T(8,128)(2,1)}, bf16[2,2,256,1024]{3,2,1,0:T(8,128)(2,1)S(1)}, u32[]{:S(2)}, u32[]{:S(2)}) collective-permute-start(bf16[2,2,256,1024]{3,2,1,0:T(8,128)(2,1)} %forward.13), channel_id=1, source_target_pairs={{0,1},{1,0},{2,3},{3,2},{4,5},{5,4},{6,7},{7,6},{8,9},{9,8},{10,11... | collective-permute-start | bytes 6291464 | tf_op jit(solution)/shard_map/ppermute | solution.py:340
  16.8 22.4 %collective-permute-start.8 = (bf16[2,256,1024]{2,1,0:T(8,128)(2,1)}, bf16[2,256,1024]{2,1,0:T(8,128)(2,1)S(1)}, u32[]{:S(2)}, u32[]{:S(2)}) collective-permute-start(bf16[2,256,1024]{2,1,0:T(8,128)(2,1)} %bitcast.37), channel_id=1, source_target_pairs={{0,1},{1,0},{2,3},{3,2},{4,5},{5,4},{6,7},{7,6},{8,9},{9,8},{10,11... | collective-permute-start | bytes 3145736 | tf_op jit(solution)/shard_map/ppermute | solution.py:340
  21.6 26.2 %collective-permute-start.6 = (bf16[2,256,1024]{2,1,0:T(8,128)(2,1)S(1)}, bf16[2,256,1024]{2,1,0:T(8,128)(2,1)}, u32[]{:S(2)}, u32[]{:S(2)}) collective-permute-start(bf16[2,256,1024]{2,1,0:T(8,128)(2,1)S(1)} %fusion.2), channel_id=1, source_target_pairs={{0,2},{1,3},{2,0},{3,1},{4,6},{5,7},{6,4},{7,5},{8,10},{9,11},{10,... | collective-permute-start | bytes 3145736 | tf_op jit(solution)/shard_map/ppermute | solution.py:343
  29.2 38.5 %collective-permute-start.4 = (bf16[2,2,256,1024]{3,2,1,0:T(8,128)(2,1)}, bf16[2,2,256,1024]{3,2,1,0:T(8,128)(2,1)S(1)}, u32[]{:S(2)}, u32[]{:S(2)}) collective-permute-start(bf16[2,2,256,1024]{3,2,1,0:T(8,128)(2,1)} %forward.15), channel_id=1, source_target_pairs={{0,1},{1,0},{2,3},{3,2},{4,5},{5,4},{6,7},{7,6},{8,9},{9,8},{10,11... | collective-permute-start | bytes 6291464 | tf_op jit(solution)/shard_map/ppermute | solution.py:340
  34.4 13.4 %copy-start.7 = (bf16[1,2,256,1024]{3,2,1,0:T(8,128)(2,1)S(1)}, bf16[1,2,256,1024]{3,2,1,0:T(8,128)(2,1)}, u32[]{:S(2)}) copy-start(bf16[1,2,256,1024]{3,2,1,0:T(8,128)(2,1)} %forward.18) | copy-start | bytes 3145732
  39.2 12.4 %copy-start.2 = (bf16[2,2,256,1024]{3,2,1,0:T(8,128)(2,1)S(1)}, bf16[2,2,256,1024]{3,2,1,0:T(8,128)(2,1)}, u32[]{:S(2)}) copy-start(bf16[2,2,256,1024]{3,2,1,0:T(8,128)(2,1)} %forward.12) | copy-start | bytes 6291460
  39.2 1.0 copy-start.24
  50.0 21.2 %collective-permute-start.12 = (bf16[2,256,1024]{2,1,0:T(8,128)(2,1)S(1)}, bf16[2,256,1024]{2,1,0:T(8,128)(2,1)}, u32[]{:S(2)}, u32[]{:S(2)}) collective-permute-start(bf16[2,256,1024]{2,1,0:T(8,128)(2,1)S(1)} %fusion.1), channel_id=1, source_target_pairs={{12,8},{13,9},{14,10},{15,11},{28,24},{29,25},{30,26},{31,27}} | collective-permute-start | bytes 3145736 | tf_op jit(solution)/shard_map/ppermute | solution.py:347
  51.6 9.6 %copy-start.10 = (bf16[2,2,256,1024]{3,2,1,0:T(8,128)(2,1)}, bf16[2,2,256,1024]{3,2,1,0:T(8,128)(2,1)S(1)}, u32[]{:S(2)}) copy-start(bf16[2,2,256,1024]{3,2,1,0:T(8,128)(2,1)S(1)} %collective-permute-done.1) | copy-start | bytes 6291460
  53.3 23.9 %collective-permute-start.2 = (bf16[2,256,1024]{2,1,0:T(8,128)(2,1)}, bf16[2,256,1024]{2,1,0:T(8,128)(2,1)}, u32[]{:S(2)}, u32[]{:S(2)}) collective-permute-start(bf16[2,256,1024]{2,1,0:T(8,128)(2,1)} %fusion.7), channel_id=1, source_target_pairs={{0,2},{1,3},{2,0},{3,1},{4,6},{5,7},{6,4},{7,5},{8,10},{9,11},{10,... | collective-permute-start | bytes 3145736 | tf_op jit(solution)/shard_map/ppermute | solution.py:343
  54.4 26.5 %collective-permute-start.9 = (bf16[2,256,1024]{2,1,0:T(8,128)(2,1)S(1)}, bf16[2,256,1024]{2,1,0:T(8,128)(2,1)}, u32[]{:S(2)}, u32[]{:S(2)}) collective-permute-start(bf16[2,256,1024]{2,1,0:T(8,128)(2,1)S(1)} %fusion.1), channel_id=1, source_target_pairs={{0,4},{1,5},{2,6},{3,7},{16,20},{17,21},{18,22},{19,23}} | collective-permute-start | bytes 3145736 | tf_op jit(solution)/shard_map/ppermute | solution.py:347
  61.3 32.7 %collective-permute-start = (bf16[2,2,256,1024]{3,2,1,0:T(8,128)(2,1)}, bf16[2,2,256,1024]{3,2,1,0:T(8,128)(2,1)}, u32[]{:S(2)}, u32[]{:S(2)}) collective-permute-start(bf16[2,2,256,1024]{3,2,1,0:T(8,128)(2,1)} %forward.11), channel_id=1, source_target_pairs={{0,1},{1,0},{2,3},{3,2},{4,5},{5,4},{6,7},{7,6},{8,9},{9,8},{10,11... | collective-permute-start | bytes 6291464 | tf_op jit(solution)/shard_map/ppermute | solution.py:340
  62.2 15.0 %copy-start.11 = (bf16[2,2,256,1024]{3,2,1,0:T(8,128)(2,1)S(1)}, bf16[2,2,256,1024]{3,2,1,0:T(8,128)(2,1)}, u32[]{:S(2)}) copy-start(bf16[2,2,256,1024]{3,2,1,0:T(8,128)(2,1)} %copy-done.10) | copy-start | bytes 6291460
  67.7 9.5 %copy-start.3 = (bf16[2,2,256,1024]{3,2,1,0:T(8,128)(2,1)S(1)}, bf16[2,2,256,1024]{3,2,1,0:T(8,128)(2,1)}, u32[]{:S(2)}) copy-start(bf16[2,2,256,1024]{3,2,1,0:T(8,128)(2,1)} %forward.12) | copy-start | bytes 6291460
  67.7 3.5 %copy-start.8 = (bf16[2,2,256,1024]{3,2,1,0:T(8,128)(2,1)}, bf16[2,2,256,1024]{3,2,1,0:T(8,128)(2,1)S(1)}, u32[]{:S(2)}) copy-start(bf16[2,2,256,1024]{3,2,1,0:T(8,128)(2,1)S(1)} %collective-permute-done.4) | copy-start | bytes 6291460
  71.2 28.5 %collective-permute-start.7 = (bf16[2,256,1024]{2,1,0:T(8,128)(2,1)}, bf16[2,256,1024]{2,1,0:T(8,128)(2,1)}, u32[]{:S(2)}, u32[]{:S(2)}) collective-permute-start(bf16[2,256,1024]{2,1,0:T(8,128)(2,1)} %fusion.8), channel_id=1, source_target_pairs={{0,2},{1,3},{2,0},{3,1},{4,6},{5,7},{6,4},{7,5},{8,10},{9,11},{10,... | collective-permute-start | bytes 3145736 | tf_op jit(solution)/shard_map/ppermute | solution.py:343
  83.8 23.9 %collective-permute-start.10 = (bf16[2,256,1024]{2,1,0:T(8,128)(2,1)}, bf16[2,256,1024]{2,1,0:T(8,128)(2,1)S(1)}, u32[]{:S(2)}, u32[]{:S(2)}) collective-permute-start(bf16[2,256,1024]{2,1,0:T(8,128)(2,1)} %add_convert_fusion.3), channel_id=1, source_target_pairs={{0,4},{1,5},{2,6},{3,7},{4,8},{5,9},{6,10},{7,11},{16,20},{17,21},... | collective-permute-start | bytes 3145736 | tf_op jit(solution)/shard_map/ppermute | solution.py:347
  87.9 23.5 %collective-permute-start.13 = (bf16[2,256,1024]{2,1,0:T(8,128)(2,1)}, bf16[2,256,1024]{2,1,0:T(8,128)(2,1)S(1)}, u32[]{:S(2)}, u32[]{:S(2)}) collective-permute-start(bf16[2,256,1024]{2,1,0:T(8,128)(2,1)} %get-tuple-element.11), channel_id=1, source_target_pairs={{8,4},{9,5},{10,6},{11,7},{12,8},{13,9},{14,10},{15,11},{24,20},{2... | collective-permute-start | bytes 3145736 | tf_op jit(solution)/shard_map/ppermute | solution.py:347
  89.2 22.2 %copy-start.9 = (bf16[2,2,256,1024]{3,2,1,0:T(8,128)(2,1)S(1)}, bf16[2,2,256,1024]{3,2,1,0:T(8,128)(2,1)}, u32[]{:S(2)}) copy-start(bf16[2,2,256,1024]{3,2,1,0:T(8,128)(2,1)} %copy-done.8) | copy-start | bytes 6291460
  94.0 17.4 %copy-start = (bf16[2,2,256,1024]{3,2,1,0:T(8,128)(2,1)S(1)}, bf16[2,2,256,1024]{3,2,1,0:T(8,128)(2,1)}, u32[]{:S(2)}) copy-start(bf16[2,2,256,1024]{3,2,1,0:T(8,128)(2,1)} %forward.14) | copy-start | bytes 6291460
  96.1 25.2 %copy-start.1 = (bf16[2,2,256,1024]{3,2,1,0:T(8,128)(2,1)S(1)}, bf16[2,2,256,1024]{3,2,1,0:T(8,128)(2,1)}, u32[]{:S(2)}) copy-start(bf16[2,2,256,1024]{3,2,1,0:T(8,128)(2,1)} %forward.10) | copy-start | bytes 6291460
  96.1 25.2 %collective-permute-start.3 = (bf16[2,256,1024]{2,1,0:T(8,128)(2,1)S(1)}, bf16[2,256,1024]{2,1,0:T(8,128)(2,1)S(1)}, u32[]{:S(2)}, u32[]{:S(2)}) collective-permute-start(bf16[2,256,1024]{2,1,0:T(8,128)(2,1)S(1)} %fusion.6), channel_id=1, source_target_pairs={{0,2},{1,3},{2,0},{3,1},{4,6},{5,7},{6,4},{7,5},{8,10},{9,11},{10,... | collective-permute-start | bytes 3145736 | tf_op jit(solution)/shard_map/ppermute | solution.py:343
  114.2 22.4 %collective-permute-start.11 = (bf16[2,256,1024]{2,1,0:T(8,128)(2,1)S(1)}, bf16[2,256,1024]{2,1,0:T(8,128)(2,1)S(1)}, u32[]{:S(2)}, u32[]{:S(2)}) collective-permute-start(bf16[2,256,1024]{2,1,0:T(8,128)(2,1)S(1)} %get-tuple-element.14), channel_id=1, source_target_pairs={{0,4},{1,5},{2,6},{3,7},{4,8},{5,9},{6,10},{7,11},{8,12},{9,13},{1... | collective-permute-start | bytes 3145736 | tf_op jit(solution)/shard_map/ppermute | solution.py:347
  116.1 22.4 %collective-permute-start.14 = (bf16[2,256,1024]{2,1,0:T(8,128)(2,1)S(1)}, bf16[2,256,1024]{2,1,0:T(8,128)(2,1)S(1)}, u32[]{:S(2)}, u32[]{:S(2)}) collective-permute-start(bf16[2,256,1024]{2,1,0:T(8,128)(2,1)S(1)} %get-tuple-element.13), channel_id=1, source_target_pairs={{4,0},{5,1},{6,2},{7,3},{8,4},{9,5},{10,6},{11,7},{12,8},{13,9},{1... | collective-permute-start | bytes 3145736 | tf_op jit(solution)/shard_map/ppermute | solution.py:347
  136.6 1.9 copy-start.22
  138.5 1.0 copy-start.23
  153.4 21.7 %collective-permute-start.18 = (bf16[2,256,1024]{2,1,0:T(8,128)(2,1)}, bf16[2,256,1024]{2,1,0:T(8,128)(2,1)S(1)}, u32[]{:S(2)}, u32[]{:S(2)}) collective-permute-start(bf16[2,256,1024]{2,1,0:T(8,128)(2,1)} %middle.1.refs_0_), channel_id=1, source_target_pairs={{0,4},{1,5},{2,6},{3,7},{4,8},{5,9},{6,10},{7,11},{8,12},{9,13},{1... | collective-permute-start | bytes 3145736 | tf_op jit(solution)/shard_map/ppermute | solution.py:347
  155.3 22.9 %collective-permute-start.19 = (bf16[2,256,1024]{2,1,0:T(8,128)(2,1)}, bf16[2,256,1024]{2,1,0:T(8,128)(2,1)S(1)}, u32[]{:S(2)}, u32[]{:S(2)}) collective-permute-start(bf16[2,256,1024]{2,1,0:T(8,128)(2,1)} %middle.1.refs_0_), channel_id=1, source_target_pairs={{4,0},{5,1},{6,2},{7,3},{8,4},{9,5},{10,6},{11,7},{12,8},{13,9},{1... | collective-permute-start | bytes 3145736 | tf_op jit(solution)/shard_map/ppermute | solution.py:347
  175.1 19.7 %collective-permute-start.23 = (bf16[2,256,1024]{2,1,0:T(8,128)(2,1)S(1)}, bf16[2,256,1024]{2,1,0:T(8,128)(2,1)}, u32[]{:S(2)}, u32[]{:S(2)}) collective-permute-start(bf16[2,256,1024]{2,1,0:T(8,128)(2,1)S(1)} %collective-permute-done.18), channel_id=1, source_target_pairs={{4,8},{5,9},{6,10},{7,11},{8,12},{9,13},{10,14},{11,15},{20,24},{2... | collective-permute-start | bytes 3145736 | tf_op jit(solution)/shard_map/ppermute | solution.py:347
  178.3 33.8 %copy-start.18 = (bf16[2,256,1024]{2,1,0:T(8,128)(2,1)}, bf16[2,256,1024]{2,1,0:T(8,128)(2,1)S(1)}, u32[]{:S(2)}) copy-start(bf16[2,256,1024]{2,1,0:T(8,128)(2,1)S(1)} %collective-permute-done.19) | copy-start | bytes 3145732
  178.3 20.0 %collective-permute-start.24 = (bf16[2,256,1024]{2,1,0:T(8,128)(2,1)S(1)}, bf16[2,256,1024]{2,1,0:T(8,128)(2,1)}, u32[]{:S(2)}, u32[]{:S(2)}) collective-permute-start(bf16[2,256,1024]{2,1,0:T(8,128)(2,1)S(1)} %collective-permute-done.19), channel_id=1, source_target_pairs={{4,0},{5,1},{6,2},{7,3},{8,4},{9,5},{10,6},{11,7},{20,16},{21,17},... | collective-permute-start | bytes 3145736 | tf_op jit(solution)/shard_map/ppermute | solution.py:347
  180.2 31.8 %collective-permute-start.16 = (bf16[2,256,1024]{2,1,0:T(8,128)(2,1)}, bf16[2,256,1024]{2,1,0:T(8,128)(2,1)S(1)}, u32[]{:S(2)}, u32[]{:S(2)}) collective-permute-start(bf16[2,256,1024]{2,1,0:T(8,128)(2,1)} %middle.1.refs_0_), channel_id=1, source_target_pairs={{0,2},{1,3},{2,0},{3,1},{4,6},{5,7},{6,4},{7,5},{8,10},{9,11},{10,... | collective-permute-start | bytes 3145736 | tf_op jit(solution)/shard_map/ppermute | solution.py:343
  194.8 17.3 %collective-permute-start.28 = (bf16[2,256,1024]{2,1,0:T(8,128)(2,1)}, bf16[2,256,1024]{2,1,0:T(8,128)(2,1)}, u32[]{:S(2)}, u32[]{:S(2)}) collective-permute-start(bf16[2,256,1024]{2,1,0:T(8,128)(2,1)} %collective-permute-done.23), channel_id=1, source_target_pairs={{8,12},{9,13},{10,14},{11,15},{24,28},{25,29},{26,30},{27,31}} | collective-permute-start | bytes 3145736 | tf_op jit(solution)/shard_map/ppermute | solution.py:347
  198.3 21.1 %collective-permute-start.29 = (bf16[2,256,1024]{2,1,0:T(8,128)(2,1)}, bf16[2,256,1024]{2,1,0:T(8,128)(2,1)}, u32[]{:S(2)}, u32[]{:S(2)}) collective-permute-start(bf16[2,256,1024]{2,1,0:T(8,128)(2,1)} %collective-permute-done.24), channel_id=1, source_target_pairs={{4,0},{5,1},{6,2},{7,3},{20,16},{21,17},{22,18},{23,19}} | collective-permute-start | bytes 3145736 | tf_op jit(solution)/shard_map/ppermute | solution.py:347
  202.9 28.8 %collective-permute-start.15 = (bf16[2,256,1024]{2,1,0:T(8,128)(2,1)}, bf16[2,256,1024]{2,1,0:T(8,128)(2,1)S(1)}, u32[]{:S(2)}, u32[]{:S(2)}) collective-permute-start(bf16[2,256,1024]{2,1,0:T(8,128)(2,1)} %middle.1.refs_0_), channel_id=1, source_target_pairs={{0,1},{1,0},{2,3},{3,2},{4,5},{5,4},{6,7},{7,6},{8,9},{9,8},{10,11... | collective-permute-start | bytes 3145736 | tf_op jit(solution)/shard_map/ppermute | solution.py:340
  212.0 9.6 %copy-start.12 = (bf16[2,256,1024]{2,1,0:T(8,128)(2,1)}, bf16[2,256,1024]{2,1,0:T(8,128)(2,1)S(1)}, u32[]{:S(2)}) copy-start(bf16[2,256,1024]{2,1,0:T(8,128)(2,1)S(1)} %collective-permute-done.16.refs_2_) | copy-start | bytes 3145732
  212.0 19.7 %collective-permute-start.17 = (bf16[2,256,1024]{2,1,0:T(8,128)(2,1)S(1)}, bf16[2,256,1024]{2,1,0:T(8,128)(2,1)S(1)}, u32[]{:S(2)}, u32[]{:S(2)}) collective-permute-start(bf16[2,256,1024]{2,1,0:T(8,128)(2,1)S(1)} %collective-permute-done.16.refs_2_), channel_id=1, source_target_pairs={{0,1},{1,0},{2,3},{3,2},{4,5},{5,4},{6,7},{7,6},{8,9},{9,8},{10,11... | collective-permute-start | bytes 3145736 | tf_op jit(solution)/shard_map/ppermute | solution.py:340
  221.6 72.7 %copy-start.4 = (bf16[2,256,1024]{2,1,0:T(8,128)(2,1)}, bf16[2,256,1024]{2,1,0:T(8,128)(2,1)S(1)}, u32[]{:S(2)}) copy-start(bf16[2,256,1024]{2,1,0:T(8,128)(2,1)S(1)} %get-tuple-element.15.refs_12_) | copy-start | bytes 3145732
  221.6 72.7 %copy-start.5 = (bf16[2,256,1024]{2,1,0:T(8,128)(2,1)}, bf16[2,256,1024]{2,1,0:T(8,128)(2,1)S(1)}, u32[]{:S(2)}) copy-start(bf16[2,256,1024]{2,1,0:T(8,128)(2,1)S(1)} %get-tuple-element.16.refs_8_) | copy-start | bytes 3145732
  221.6 72.7 %copy-start.6 = (bf16[2,256,1024]{2,1,0:T(8,128)(2,1)}, bf16[2,256,1024]{2,1,0:T(8,128)(2,1)S(1)}, u32[]{:S(2)}) copy-start(bf16[2,256,1024]{2,1,0:T(8,128)(2,1)S(1)} %get-tuple-element.17.refs_4_) | copy-start | bytes 3145732
  221.6 16.7 %collective-permute-start.21 = (bf16[2,256,1024]{2,1,0:T(8,128)(2,1)S(1)}, bf16[2,256,1024]{2,1,0:T(8,128)(2,1)S(1)}, u32[]{:S(2)}, u32[]{:S(2)}) collective-permute-start(bf16[2,256,1024]{2,1,0:T(8,128)(2,1)S(1)} %get-tuple-element.17.refs_4_), channel_id=1, source_target_pairs={{0,2},{1,3},{2,0},{3,1},{4,6},{5,7},{6,4},{7,5},{8,10},{9,11},{10,... | collective-permute-start | bytes 3145736 | tf_op jit(solution)/shard_map/ppermute | solution.py:343
  221.7 39.1 %collective-permute-start.26 = (bf16[2,256,1024]{2,1,0:T(8,128)(2,1)S(1)}, bf16[2,256,1024]{2,1,0:T(8,128)(2,1)S(1)}, u32[]{:S(2)}, u32[]{:S(2)}) collective-permute-start(bf16[2,256,1024]{2,1,0:T(8,128)(2,1)S(1)} %get-tuple-element.16.refs_8_), channel_id=1, source_target_pairs={{0,2},{1,3},{2,0},{3,1},{4,6},{5,7},{6,4},{7,5},{8,10},{9,11},{10,... | collective-permute-start | bytes 3145736 | tf_op jit(solution)/shard_map/ppermute | solution.py:343
  223.2 55.1 %collective-permute-start.20 = (bf16[2,256,1024]{2,1,0:T(8,128)(2,1)S(1)}, bf16[2,256,1024]{2,1,0:T(8,128)(2,1)S(1)}, u32[]{:S(2)}, u32[]{:S(2)}) collective-permute-start(bf16[2,256,1024]{2,1,0:T(8,128)(2,1)S(1)} %get-tuple-element.17.refs_4_), channel_id=1, source_target_pairs={{0,1},{1,0},{2,3},{3,2},{4,5},{5,4},{6,7},{7,6},{8,9},{9,8},{10,11... | collective-permute-start | bytes 3145736 | tf_op jit(solution)/shard_map/ppermute | solution.py:340
  231.7 62.7 %copy-start.13 = (bf16[2,256,1024]{2,1,0:T(8,128)(2,1)}, bf16[2,256,1024]{2,1,0:T(8,128)(2,1)S(1)}, u32[]{:S(2)}) copy-start(bf16[2,256,1024]{2,1,0:T(8,128)(2,1)S(1)} %collective-permute-done.15.refs_1_) | copy-start | bytes 3145732
  231.7 51.7 %collective-permute-start.31 = (bf16[2,256,1024]{2,1,0:T(8,128)(2,1)S(1)}, bf16[2,256,1024]{2,1,0:T(8,128)(2,1)}, u32[]{:S(2)}, u32[]{:S(2)}) collective-permute-start(bf16[2,256,1024]{2,1,0:T(8,128)(2,1)S(1)} %get-tuple-element.15.refs_12_), channel_id=1, source_target_pairs={{0,2},{1,3},{2,0},{3,1},{4,6},{5,7},{6,4},{7,5},{8,10},{9,11},{10,... | collective-permute-start | bytes 3145736 | tf_op jit(solution)/shard_map/ppermute | solution.py:343
  231.7 62.6 %copy-start.14 = (bf16[2,256,1024]{2,1,0:T(8,128)(2,1)}, bf16[2,256,1024]{2,1,0:T(8,128)(2,1)S(1)}, u32[]{:S(2)}) copy-start(bf16[2,256,1024]{2,1,0:T(8,128)(2,1)S(1)} %collective-permute-done.17.refs_3_) | copy-start | bytes 3145732
  231.7 60.6 %collective-permute-start.25 = (bf16[2,256,1024]{2,1,0:T(8,128)(2,1)S(1)}, bf16[2,256,1024]{2,1,0:T(8,128)(2,1)S(1)}, u32[]{:S(2)}, u32[]{:S(2)}) collective-permute-start(bf16[2,256,1024]{2,1,0:T(8,128)(2,1)S(1)} %get-tuple-element.16.refs_8_), channel_id=1, source_target_pairs={{0,1},{1,0},{2,3},{3,2},{4,5},{5,4},{6,7},{7,6},{8,9},{9,8},{10,11... | collective-permute-start | bytes 3145736 | tf_op jit(solution)/shard_map/ppermute | solution.py:340
  238.4 56.0 %copy-start.15 = (bf16[2,256,1024]{2,1,0:T(8,128)(2,1)}, bf16[2,256,1024]{2,1,0:T(8,128)(2,1)S(1)}, u32[]{:S(2)}) copy-start(bf16[2,256,1024]{2,1,0:T(8,128)(2,1)S(1)} %collective-permute-done.21.refs_6_) | copy-start | bytes 3145732
  238.4 53.9 %collective-permute-start.30 = (bf16[2,256,1024]{2,1,0:T(8,128)(2,1)S(1)}, bf16[2,256,1024]{2,1,0:T(8,128)(2,1)S(1)}, u32[]{:S(2)}, u32[]{:S(2)}) collective-permute-start(bf16[2,256,1024]{2,1,0:T(8,128)(2,1)S(1)} %get-tuple-element.15.refs_12_), channel_id=1, source_target_pairs={{0,1},{1,0},{2,3},{3,2},{4,5},{5,4},{6,7},{7,6},{8,9},{9,8},{10,11... | collective-permute-start | bytes 3145736 | tf_op jit(solution)/shard_map/ppermute | solution.py:340
  260.8 31.5 %copy-start.16 = (bf16[2,256,1024]{2,1,0:T(8,128)(2,1)}, bf16[2,256,1024]{2,1,0:T(8,128)(2,1)S(1)}, u32[]{:S(2)}) copy-start(bf16[2,256,1024]{2,1,0:T(8,128)(2,1)S(1)} %collective-permute-done.26.refs_10_) | copy-start | bytes 3145732
  260.9 31.5 %collective-permute-start.22 = (bf16[2,256,1024]{2,1,0:T(8,128)(2,1)S(1)}, bf16[2,256,1024]{2,1,0:T(8,128)(2,1)S(1)}, u32[]{:S(2)}, u32[]{:S(2)}) collective-permute-start(bf16[2,256,1024]{2,1,0:T(8,128)(2,1)S(1)} %collective-permute-done.21.refs_6_), channel_id=1, source_target_pairs={{0,1},{1,0},{2,3},{3,2},{4,5},{5,4},{6,7},{7,6},{8,9},{9,8},{10,11... | collective-permute-start | bytes 3145736 | tf_op jit(solution)/shard_map/ppermute | solution.py:340
  278.2 14.1 %copy-start.17 = (bf16[2,256,1024]{2,1,0:T(8,128)(2,1)}, bf16[2,256,1024]{2,1,0:T(8,128)(2,1)S(1)}, u32[]{:S(2)}) copy-start(bf16[2,256,1024]{2,1,0:T(8,128)(2,1)S(1)} %collective-permute-done.20.refs_5_) | copy-start | bytes 3145732
  278.2 16.1 %collective-permute-start.27 = (bf16[2,256,1024]{2,1,0:T(8,128)(2,1)S(1)}, bf16[2,256,1024]{2,1,0:T(8,128)(2,1)}, u32[]{:S(2)}, u32[]{:S(2)}) collective-permute-start(bf16[2,256,1024]{2,1,0:T(8,128)(2,1)S(1)} %collective-permute-done.26.refs_10_), channel_id=1, source_target_pairs={{0,1},{1,0},{2,3},{3,2},{4,5},{5,4},{6,7},{7,6},{8,9},{9,8},{10,11... | collective-permute-start | bytes 3145736 | tf_op jit(solution)/shard_map/ppermute | solution.py:340
  283.4 35.0 %collective-permute-start.32 = (bf16[2,256,1024]{2,1,0:T(8,128)(2,1)}, bf16[2,256,1024]{2,1,0:T(8,128)(2,1)}, u32[]{:S(2)}, u32[]{:S(2)}) collective-permute-start(bf16[2,256,1024]{2,1,0:T(8,128)(2,1)} %collective-permute-done.31.refs_0_), channel_id=1, source_target_pairs={{0,1},{1,0},{2,3},{3,2},{4,5},{5,4},{6,7},{7,6},{8,9},{9,8},{10,11... | collective-permute-start | bytes 3145736 | tf_op jit(solution)/shard_map/ppermute | solution.py:340
  292.3 2.1 copy-start.19
  292.3 1.0 copy-start.20
  293.3 1.0 copy-start.21

commit v3 on v2

--- a/solution.py
+++ b/solution.py
@@ -63,15 +63,28 @@
         return (first_row > -self.tile_rows) & (first_row < self.crop_width)
 
 
-def forward_kernel(meta_ref, spec_ref, pupil_ref, band_ref, out_ref, *, base, win):
-    slot = base + pl.program_id(0)
+def forward_kernel(meta_ref, spec_ref, pupil_ref, band_ref, *refs, base, win, adding):
+    came_ref, out_refs = (refs[0], refs[1:]) if adding else (None, refs)
+    step = pl.program_id(0)
+    slot = base + step
     first_row, left = meta_ref[0, slot], meta_ref[1, slot]
     active = win.active(first_row)
     tile_rows, crop_width = win.tile_rows, win.crop_width
+    shape = out_refs[0].shape
+
+    def store(value):
+        if not adding:
+            out_refs[0][...] = value.reshape(shape)
+            return
+        for number, out_ref in enumerate(out_refs):
+
+            @pl.when(step == number)
+            def _():
+                out_ref[...] = value.reshape(shape)
 
     @pl.when(jnp.logical_not(active))
     def _():
-        out_ref[...] = jnp.zeros_like(out_ref)
+        store(came_ref[...] if adding else jnp.zeros(shape, jnp.bfloat16))
 
     @pl.when(active)
     def _():
@@ -88,7 +101,9 @@
         mid = lax.dot_general(
             table, pupiled, (((0,), (0,)), ((), ())), preferred_element_type=jnp.float32
         )
-        out_ref[...] = mid.astype(jnp.bfloat16).reshape(out_ref.shape)
+        if adding:
+            mid = mid + came_ref[...].reshape(mid.shape).astype(jnp.float32)
+        store(mid.astype(jnp.bfloat16))
 
 
 def backward_kernel(meta_ref, spec_ref, pupil_ref, band_ref, *refs, slots, win):
@@ -142,39 +157,40 @@
     return result
 
 
-def middle_kernel(own_ref, up_ref, down_ref, image_ref, cos_ref, sin_ref, out_ref, mid_ref, sum_ref):
+def middle_kernel(
+    own_ref, up_ref, down_ref, image_ref, cos_ref, sin_ref, out_ref, mid_ref, resid_ref
+):
     step = pl.program_id(0)
     _, band, crop_width = own_ref.shape
+    block = cos_ref.shape[1]
+    blocks = crop_width // block
 
     @pl.when(step == 0)
     def _():
         total = own_ref[...].astype(jnp.float32) + up_ref[...].astype(jnp.float32)
         total = total + down_ref[...].astype(jnp.float32)
         mid_ref[...] = total.astype(jnp.bfloat16).reshape(2 * band, crop_width)
-        sum_ref[...] = jnp.zeros_like(sum_ref)
-
-    dot = functools.partial(jnp.dot, preferred_element_type=jnp.float32)
-    mid = mid_ref[...]
-    by_cos, by_sin = dot(mid, cos_ref[...]), dot(mid, sin_ref[...])
-    field_real = by_cos[:band] - by_sin[band:]
-    field_imag = by_sin[:band] + by_cos[band:]
-    magnitude = jnp.sqrt(field_real * field_real + field_imag * field_imag)
-    keeping = 1.0 - image_ref[0].astype(jnp.float32) / jnp.maximum(magnitude, 1.0)
-    resid = jnp.concatenate([field_real * keeping, field_imag * keeping], axis=0)
-    resid = resid.astype(jnp.bfloat16)
-
-    def turned(table):
-        return lax.dot_general(
-            resid, table, (((1,), (1,)), ((), ())), preferred_element_type=jnp.float32
-        )
-
-    by_cos, by_sin = turned(cos_ref[...]), turned(sin_ref[...])
-    sum_ref[0] += by_cos[:band] + by_sin[band:]
-    sum_ref[1] += by_cos[band:] - by_sin[:band]
-
-    @pl.when(step == pl.num_programs(0) - 1)
-    def _():
-        out_ref[...] = sum_ref[...].astype(jnp.bfloat16)
+
+    def products(left):
+        dot = functools.partial(jnp.dot, preferred_element_type=jnp.float32)
+        return dot(left, cos_ref[...]), dot(left, sin_ref[...])
+
+    @pl.when(step < blocks)
+    def _():
+        by_cos, by_sin = products(mid_ref[...])
+        field_real = by_cos[:band] - by_sin[band:]
+        field_imag = by_sin[:band] + by_cos[band:]
+        magnitude = jnp.sqrt(field_real * field_real + field_imag * field_imag)
+        keeping = 1.0 - image_ref[0].astype(jnp.float32) / jnp.maximum(magnitude, 1.0)
+        resid = jnp.concatenate([field_real * keeping, field_imag * keeping], axis=0)
+        columns = pl.ds(pl.multiple_of(step * block, block), block)
+        resid_ref[:, columns] = resid.astype(jnp.bfloat16)
+
+    @pl.when(step >= blocks)
+    def _():
+        by_cos, by_sin = products(resid_ref[...])
+        out_ref[0] = (by_cos[:band] + by_sin[band:]).astype(jnp.bfloat16)
+        out_ref[1] = (by_cos[band:] - by_sin[:band]).astype(jnp.bfloat16)
 
 
 def params():
@@ -186,17 +202,26 @@
     return pl.CostEstimate(flops=flops, bytes_accessed=moved, transcendentals=0)
 
 
-def forward(meta, spectrum, pupil, band_table, base, count):
+def forward(meta, spectrum, pupil, band_table, base, count, came=None):
     _, tile_rows, slab_columns = spectrum.shape
     crop_width = pupil.shape[1]
     band = band_table.shape[1] // 2
     win = Windows(tile_rows, slab_columns, crop_width)
+    adding = came is not None
 
     def row(i, meta):
         return (win.row(meta[0, base + i]), 0)
 
+    stacked = pl.BlockSpec((1, 2, band, crop_width), lambda i, meta: (i, 0, 0, 0))
+    single = pl.BlockSpec((2, band, crop_width), lambda i, meta: (0, 0, 0))
+    if adding:
+        out_specs = [single] * count
+        out_shape = [jax.ShapeDtypeStruct((2, band, crop_width), jnp.bfloat16)] * count
+    else:
+        out_specs = stacked
+        out_shape = jax.ShapeDtypeStruct((count, 2, band, crop_width), jnp.bfloat16)
     return pl.pallas_call(
-        functools.partial(forward_kernel, base=base, win=win),
+        functools.partial(forward_kernel, base=base, win=win, adding=adding),
         grid_spec=pltpu.PrefetchScalarGridSpec(
             num_scalar_prefetch=1,
             grid=(count,),
@@ -207,14 +232,15 @@
                 ),
                 pl.BlockSpec((pl.Element(win.rows), pl.Element(crop_width)), row),
                 pl.BlockSpec((pl.Element(win.rows), pl.Element(2 * band)), row),
-            ],
-            out_specs=pl.BlockSpec((1, 2, band, crop_width), lambda i, meta: (i, 0, 0, 0)),
+            ]
+            + [stacked] * adding,
+            out_specs=out_specs,
         ),
-        out_shape=jax.ShapeDtypeStruct((count, 2, band, crop_width), jnp.bfloat16),
+        out_shape=out_shape,
         compiler_params=params(),
         cost_estimate=cost(count, win, band, count * 3000000),
         name="forward",
-    )(meta, spectrum, pupil, band_table)
+    )(meta, spectrum, pupil, band_table, *([came] if adding else []))
 
 
 def backward(meta, spectrum, pupil, band_table, slots, backs):
@@ -256,26 +282,29 @@
 def middle(own, up, down, image, cos_table, sin_table):
     _, band, crop_width = own.shape
     block = min(256, crop_width)
-    table = pl.BlockSpec((crop_width, block), lambda j: (0, j))
+    blocks = crop_width // block
+    table = pl.BlockSpec((crop_width, block), lambda j: (0, j % blocks))
     whole = pl.BlockSpec((2, band, crop_width), lambda j: (0, 0, 0))
     return pl.pallas_call(
         middle_kernel,
-        grid=(crop_width // block,),
+        grid=(2 * blocks,),
         in_specs=[
             whole,
             whole,
             whole,
-            pl.BlockSpec((1, band, block), lambda j: (0, 0, j)),
+            pl.BlockSpec((1, band, block), lambda j: (0, 0, jnp.minimum(j, blocks - 1))),
             table,
             table,
         ],
-        out_specs=whole,
+        out_specs=pl.BlockSpec((2, band, block), lambda j: (0, 0, jnp.maximum(j - blocks, 0))),
         out_shape=jax.ShapeDtypeStruct((2, band, crop_width), jnp.bfloat16),
-        scratch_shapes=[
-            pltpu.VMEM((2 * band, crop_width), jnp.bfloat16),
-            pltpu.VMEM((2, band, crop_width), jnp.float32),
-        ],
+        scratch_shapes=[pltpu.VMEM((2 * band, crop_width), jnp.bfloat16)] * 2,
         compiler_params=params(),
+        cost_estimate=pl.CostEstimate(
+            flops=16 * band * crop_width * crop_width,
+            bytes_accessed=14 * band * crop_width * 2 + 8 * crop_width * crop_width,
+            transcendentals=0,
+        ),
         name="middle",
     )(own, up, down, image, cos_table, sin_table)
 
@@ -314,7 +343,7 @@
     count = lax.axis_size("ty")
     planes = count // 4
     position = lax.axis_index("ty")
-    plane, corner = position // 4, position % 4
+    plane = position // 4
     _, tile_rows, slab_columns = spectrum.shape
     crop_width = pupil.shape[0]
     band = measured.shape[1]
@@ -327,10 +356,20 @@
     cos_table, sin_table = jnp.asarray(cos_table), jnp.asarray(sin_table)
 
     order = far_first(planes)
-    flips = jnp.asarray([3, 1, 2, 0], jnp.int32)
-    my_order = lax.dynamic_index_in_dim(jnp.asarray(order, jnp.int32), plane, keepdims=False)
-    ids = (my_order[:, None] * 4 + (corner ^ flips)[None, :]).reshape(-1)
-    match = ids[:, None] == jnp.arange(count, dtype=jnp.int32)[None, :]
+    first = [(0, 2)]
+    second = [(0, 0), (1, 2), (1, 0)]
+    others = [(j, y) for j in range(2, planes) for y in (2, 0)]
+    groups = [first, second, others]
+    slots = {}
+    for core in (1, 0):
+        for group in groups:
+            for j, y in group:
+                slots[j, y + core] = len(slots)
+    ids = [
+        [order[i // 4][j] * 4 + (i % 4 ^ flip) for (j, flip) in slots] for i in range(count)
+    ]
+    my_ids = lax.dynamic_index_in_dim(jnp.asarray(ids, jnp.int32), position, keepdims=False)
+    match = my_ids[:, None] == jnp.arange(count, dtype=jnp.int32)[None, :]
     half = crop_width // 2
     tops = jnp.sum(jnp.where(match, centre_rows[None, :], 0), axis=1) - half
     lefts = jnp.sum(jnp.where(match, centre_cols[None, :], 0), axis=1) - half
@@ -346,71 +385,88 @@
         pairs = [(4 * z + i, 4 * (z + by) + i) for z in sources for i in range(4)]
         return lax.ppermute(value, "ty", pairs)
 
-    def partial(base, number):
-        return forward(meta, spectrum, pupil, band_table, base, number)
-
+    def theirs(group, after):
+        known = meta if after is None else lax.optimization_barrier((meta, after))[0]
+        j, y = group[0]
+        return forward(known, spectrum, pupil, band_table, slots[j, y + 1], len(group))
+
+    def mine(group, came, after):
+        known = meta if after is None else lax.optimization_barrier((meta, after))[0]
+        j, y = group[0]
+        return forward(known, spectrum, pupil, band_table, slots[j, y], len(group), came)
+
+    sent = theirs(first, None)
+    came_first = sibling(sent)
+    sent = theirs(second, sent)
+    came_second = sibling(sent)
+    (leaving,) = mine(first, came_first, sent)
+    received = {0: across(leaving)}
+    kept = {}
+    sent = theirs(others, leaving)
+    came_others = sibling(sent)
+    made = mine(second, came_second, sent)
+    kept[0], leaving, kept[1] = made
+    received[1] = across(leaving)
+    made = mine(others, came_others, made[0])
+    for (j, y), value in zip(others, made):
+        if y:
+            received[j] = across(value)
+        else:
+            kept[j] = value
+
+    up = down = None
     summed = []
-    received = []
-    up = down = None
-    up_total = down_total = None
-
-    def z_step(s):
-        nonlocal up, down
+    for s in range(1, planes + 1):
+        summed.append(total(kept[s - 1], received[s - 1]))
+        if s == planes:
+            break
         sources = [z for z in range(planes - 1) if z < s]
         value = chosen(plane, {z: summed[order[z].index(planes - s + z)] for z in sources})
-        up = along(total(value, up) if up is not None else value, sources, 1)
-        sources = [z for z in range(1, planes) if planes - 1 - z < s]
-        value = chosen(plane, {z: summed[order[z].index(s - planes + z)] for z in sources})
-        down = along(total(value, down) if down is not None else value, sources, -1)
-
-    for j in range(planes):
-        if j == 0:
-            theirs = [partial(0, 1)[0], partial(1, 1)[0]]
-            mine = [partial(2, 1)[0], partial(3, 1)[0]]
-            came = [sibling(theirs[0]), sibling(theirs[1])]
-        else:
-            theirs = partial(4 * j, 2)
-            mine = partial(4 * j + 2, 2)
-            came = sibling(theirs)
-        outgoing = total(mine[0], came[0])
-        if j >= 2:
-            outgoing, received[j - 2] = lax.optimization_barrier((outgoing, received[j - 2]))
-        received.append(across(outgoing))
-        if j >= 1:
-            z_step(j)
-        summed.append(total(mine[1], came[1], received[j]))
+        going_up = value if up is None else total(value, up)
+        sources_down = [z for z in range(1, planes) if planes - 1 - z < s]
+        value = chosen(plane, {z: summed[order[z].index(s - planes + z)] for z in sources_down})
+        going_down = value if down is None else total(value, down)
+        up, down = along(going_up, sources, 1), along(going_down, sources_down, -1)
     band_back = middle(summed[-1], up, down, measured, cos_table, sin_table)
 
     near = [list(reversed(row)) for row in order]
+    result = spectrum
     from_below, from_above = [band_back], [band_back]
-    column = [band_back]
-    other = [across(band_back)]
-    result = spectrum
-    for s in range(1, planes):
-        from_below.append(along(from_below[-1], range(s - 1, planes - 1), 1))
-        from_above.append(along(from_above[-1], range(1, planes - s + 1), -1))
-        options = {}
-        for z in range(planes):
-            q = near[z][s]
-            options[z] = from_below[z - q] if q < z else from_above[q - z]
-        value = chosen(plane, options)
-        column.append(value)
-        other.append(across(value))
-
-    def slot(j, kind):
-        return 4 * (planes - 1 - j) + kind
-
-    slots, backs = [], []
-    for j in range(planes):
-        slots += [slot(j, 3), slot(j, 1)]
-        backs += [column[j], sibling(column[j])]
-        if j < planes - 1:
-            slots += [slot(j, 2), slot(j, 0)]
-            backs += [other[j], sibling(other[j])]
-    result = backward(meta, result, pupil, band_table, slots, backs)
-    slots = [slot(planes - 1, 2), slot(planes - 1, 0)]
-    backs = [other[-1], sibling(other[-1])]
-    return backward(meta, result, pupil, band_table, slots, backs)
+    waiting = []
+    value, turned = band_back, None
+    for s in range(planes):
+        j = planes - 1 - s
+        new_slots, arrived = [slots[j, 0]], [value]
+        started = [across(value), sibling(value)]
+        next_slots = [slots[j, 2], slots[j, 1]]
+        if turned is not None:
+            started.append(sibling(turned))
+            next_slots.append(slots[j + 1, 3])
+        if s < planes - 1:
+            started.append(along(from_below[-1], range(s, planes - 1), 1))
+            started.append(along(from_above[-1], range(1, planes - s), -1))
+        waiting.append((slots[j, 0], value))
+        if s > 0:
+            result = backward(
+                meta, result, pupil, band_table, [k for k, _ in waiting], [v for _, v in waiting]
+            )
+            waiting = []
+        started = list(lax.optimization_barrier(tuple([result] + started)))
+        result, started = started[0], started[1:]
+        waiting += list(zip(next_slots, started))
+        turned = started[0]
+        if s < planes - 1:
+            from_below.append(started[-2])
+            from_above.append(started[-1])
+            options = {}
+            for z in range(planes):
+                q = near[z][s + 1]
+                options[z] = from_below[z - q] if q < z else from_above[q - z]
+            value = chosen(plane, options)
+    waiting.append((slots[0, 3], sibling(turned)))
+    return backward(
+        meta, result, pupil, band_table, [k for k, _ in waiting], [v for _, v in waiting]
+    )
 
 
 def solution(mesh):

time: 332 us -> 307 us (0.925)
  starting transfers between devices: 101 us -> 52.6 us
  waiting for transfers between devices: 101 us -> 126 us
  other arithmetic: 28.1 us -> 13.5 us
  Pallas kernels: 94.8 us -> 103 us
    ppermute x8, waiting for transfers between devices: 34.9 us -> 95.4 us  [across(): return lax.ppermute(value, 'ty', [(i, i ^ 2) for i in range(count)])]
    ppermute x13 -> x11, starting transfers between devices: 63.5 us -> 14.3 us  [sibling(): return lax.ppermute(value, 'ty', [(i, i ^ 1) for i in range(count)])]
    ppermute x12, waiting for transfers between devices: 66 us -> 28.4 us  [along(): return lax.ppermute(value, 'ty', pairs)]
    pallas_call x2 -> x4, Pallas kernels: 34.5 us -> 50.9 us  [backward(): pl.pallas_call(functools.partial(backward_kernel, slots=slots, win=win),...]
    convert_element_type x9 -> x5, other arithmetic: 23.1 us -> 11.6 us  [total(): sum((term.astype(jnp.float32) for term in terms)).astype(jnp.bfloat16)]
    pallas_call x11 -> x7, Pallas kernels: 60.3 us -> 52.2 us  [the longest x6 40.7 us: forward(): pl.pallas_call(functools.partial(forward_kernel, base=base, win=win, addi...]
  transfers between devices with their start and end apart: 33 -> 31, of which waited for: 15 -> 18; matrix products, arithmetic and copies ran while one was open for 8% -> 4% of each run, Pallas kernels for 20% -> 25%
where the time goes in v3:
time: 307 us; the launch traced here: 303 us
  waiting for transfers between devices  126 us (41%)
  Pallas kernels  103 us (34%)
  starting transfers between devices  52.6 us (17%)
  other arithmetic  13.5 us (4%)
  local copies, waits for them, and re-layouts  7.27 us (2%)
    ppermute x8, waiting for transfers between devices, across(): return lax.ppermute(value, 'ty', [(i, i ^ 2) for i in range(count)])  95.4 us
    pallas_call x4, Pallas kernels, backward(): pl.pallas_call(functools.partial(backward_kernel, slots=slots, win=win),...  50.9 us
    pallas_call x6, Pallas kernels, forward(): pl.pallas_call(functools.partial(forward_kernel, base=base, win=win, addi...  40.7 us
    ppermute x12, starting transfers between devices, along(): return lax.ppermute(value, 'ty', pairs)  31.3 us
    ppermute x12, waiting for transfers between devices, along(): return lax.ppermute(value, 'ty', pairs)  28.4 us
    ppermute x11, starting transfers between devices, sibling(): return lax.ppermute(value, 'ty', [(i, i ^ 1) for i in range(count)])  14.3 us
    convert_element_type x5, other arithmetic, total(): sum((term.astype(jnp.float32) for term in terms)).astype(jnp.bfloat16)  11.6 us
    pallas_call x1, Pallas kernels, middle(): pl.pallas_call(middle_kernel, grid=(2 * blocks,), in_specs=[whole, whole,...  11.5 us
  transfers between devices with their start and end apart: 31, of which 18 were waited for; matrix products, arithmetic and copies ran while one was open for 4% of the time, Pallas kernels for 25%

profile of v3, /device:TPU:11, one launch (start us, length us, event | category | flops | bytes accessed | tf_op | source)
XLA Modules:
  0.0 303.2 jit_solution(14641279044198261494)
XLA Ops:
  0.0 0.7 dynamic-slice_bitcast_fusion
  0.7 0.9 select_reduce_fusion.1
  2.1 4.2 %forward.6 = bf16[1,2,256,1024]{3,2,1,0:T(8,128)(2,1)} custom-call(s32[2,16]{1,0:T(2,128)} %pad_add_fusion.meta_ref, f32[2,128,8192]{2,1,0:T(8,128)} %spec_ref.12, bf16[1024,1024]{1,0:T(8,128)(2,1)} %pupil_ref.19, bf16[1024,512]{1,0:T(8,128)(2,1)} %constant.43.clone.band_ref), custom_call_target="tpu_custom_call" | custom-call | flops 536870912 | bytes 3000000 | tf_op jit(solution)/shard_map/forward/pallas_call | solution.py:223
  6.3 0.7 collective-permute-start
  7.0 7.0 %forward.7 = bf16[3,2,256,1024]{3,2,1,0:T(8,128)(2,1)} custom-call(s32[2,16]{1,0:T(2,128)} %pad_add_fusion.meta_ref, f32[2,128,8192]{2,1,0:T(8,128)} %spec_ref.12, bf16[1024,1024]{1,0:T(8,128)(2,1)} %pupil_ref.19, bf16[1024,512]{1,0:T(8,128)(2,1)} %constant.43.clone.band_ref), custom_call_target="tpu_custom_call" | custom-call | flops 1610612736 | bytes 9000000 | tf_op jit(solution)/shard_map/forward/pallas_call | solution.py:223
  14.1 1.0 copy-done.19
  15.0 4.6 %forward.8 = bf16[2,256,1024]{2,1,0:T(8,128)(2,1)} custom-call(s32[2,16]{1,0:T(2,128)} %pad_add_fusion.meta_ref, f32[2,128,8192]{2,1,0:T(8,128)} %spec_ref.12, bf16[1024,1024]{1,0:T(8,128)(2,1)} %pupil_ref.19, bf16[1024,512]{1,0:T(8,128)(2,1)} %constant.43.clone.band_ref, bf16[1,2,256,1024]{3,2,1,0:T(8,128)(2,1)} %copy-done.19), custom_call_target="tpu_custom_call" | custom-call | flops 536870912 | bytes 3000000 | tf_op jit(solution)/shard_map/forward/pallas_call | solution.py:223
  19.6 7.7 %forward.9 = bf16[4,2,256,1024]{3,2,1,0:T(8,128)(2,1)} custom-call(s32[2,16]{1,0:T(2,128)} %pad_add_fusion.meta_ref, f32[2,128,8192]{2,1,0:T(8,128)} %spec_ref.12, bf16[1024,1024]{1,0:T(8,128)(2,1)} %pupil_ref.19, bf16[1024,512]{1,0:T(8,128)(2,1)} %constant.43.clone.band_ref), custom_call_target="tpu_custom_call" | custom-call | flops 2147483648 | bytes 12000000 | tf_op jit(solution)/shard_map/forward/pallas_call | solution.py:223
  27.9 1.9 collective-permute-start.6
  29.8 1.6 copy-done.3
  31.4 7.2 %forward.10 = (bf16[2,256,1024]{2,1,0:T(8,128)(2,1)}, bf16[2,256,1024]{2,1,0:T(8,128)(2,1)}, bf16[2,256,1024]{2,1,0:T(8,128)(2,1)}) custom-call(s32[2,16]{1,0:T(2,128)} %pad_add_fusion.meta_ref, f32[2,128,8192]{2,1,0:T(8,128)} %spec_ref.12, bf16[1024,1024]{1,0:T(8,128)(2,1)} %pupil_ref.19, bf16[1024,512]{1,0:T(8,128)(2,1)} %constant.43.clone.band_ref, ...), custom_call_target="tpu_custom_call" | custom-call | flops 1610612736 | bytes 9000000 | tf_op jit(solution)/shard_map/forward/pallas_call | solution.py:223
  38.7 1.1 collective-permute-start.4
  39.7 13.3 %collective-permute-done.6 = bf16[2,256,1024]{2,1,0:T(8,128)(2,1)S(1)} collective-permute-done((bf16[2,256,1024]{2,1,0:T(8,128)(2,1)S(1)}, bf16[2,256,1024]{2,1,0:T(8,128)(2,1)S(1)}, u32[]{:S(2)}, u32[]{:S(2)}) %collective-permute-start.6) | collective-permute-done | bytes 1048608 | tf_op jit(solution)/shard_map/ppermute | solution.py:382
  53.0 1.6 add_convert_fusion.4
  54.7 1.6 collective-permute-start.10
  56.3 1.3 collective-permute-start.7
  57.6 18.0 %collective-permute-done.4 = bf16[2,256,1024]{2,1,0:T(8,128)(2,1)S(1)} collective-permute-done((bf16[2,256,1024]{2,1,0:T(8,128)(2,1)}, bf16[2,256,1024]{2,1,0:T(8,128)(2,1)S(1)}, u32[]{:S(2)}, u32[]{:S(2)}) %collective-permute-start.4) | collective-permute-done | bytes 1048608 | tf_op jit(solution)/shard_map/ppermute | solution.py:382
  75.6 1.0 copy-done.5
  76.6 3.5 %add_convert_fusion.1 = (bf16[2,256,1024]{2,1,0:T(8,128)(2,1)}, bf16[2,256,1024]{2,1,0:T(8,128)(2,1)S(1)}) fusion(bf16[2,256,1024]{2,1,0:T(8,128)(2,1)} %collective-permute-done.10, bf16[2,256,1024]{2,1,0:T(8,128)(2,1)S(1)} %add_convert_fusion.4, pred[]{:T(512)S(6)} %eq.39, bf16[2,256,1024]{2,1,0:T(8,128)(2,1)} %copy-done.5, ...), kind=kLoop, calls=%fused_computation.1 | loop fusion | flops 4718592 | bytes 6291457 | tf_op jit(solution)/shard_map/convert_element_type | solution.py:313
  80.1 1.3 collective-permute-start.11
  81.6 1.9 add_convert_fusion.3
  83.4 7.5 %collective-permute-start.8 = (bf16[2,256,1024]{2,1,0:T(8,128)(2,1)S(1)}, bf16[2,256,1024]{2,1,0:T(8,128)(2,1)S(1)}, u32[]{:S(2)}, u32[]{:S(2)}) collective-permute-start(bf16[2,256,1024]{2,1,0:T(8,128)(2,1)S(1)} %add_convert_fusion.3), channel_id=1, source_target_pairs={{0,4},{1,5},{2,6},{3,7},{4,8},{5,9},{6,10},{7,11},{16,20},{17,21},... | collective-permute-start | bytes 3145736 | tf_op jit(solution)/shard_map/ppermute | solution.py:386
  90.9 10.0 %forward.11 = (bf16[2,256,1024]{2,1,0:T(8,128)(2,1)}, bf16[2,256,1024]{2,1,0:T(8,128)(2,1)}, bf16[2,256,1024]{2,1,0:T(8,128)(2,1)}, bf16[2,256,1024]{2,1,0:T(8,128)(2,1)}) custom-call(s32[2,16]{1,0:T(2,128)} %pad_add_fusion.meta_ref, f32[2,128,8192]{2,1,0:T(8,128)} %spec_ref.12, bf16[1024,1024]{1,0:T(8,128)(2,1)} %pupil_ref.19, ...), custom_call_target="tpu_custom_call" | custom-call | flops 2147483648 | bytes 12000000 | tf_op jit(solution)/shard_map/forward/pallas_call | solution.py:223
  100.9 0.7 collective-permute-start.5
  101.6 0.8 collective-permute-start.3
  102.4 6.1 %collective-permute-done.11 = bf16[2,256,1024]{2,1,0:T(8,128)(2,1)} collective-permute-done((bf16[2,256,1024]{2,1,0:T(8,128)(2,1)}, bf16[2,256,1024]{2,1,0:T(8,128)(2,1)}, u32[]{:S(2)}, u32[]{:S(2)}) %collective-permute-start.11) | collective-permute-done | bytes 1048608 | tf_op jit(solution)/shard_map/ppermute | solution.py:386
  108.5 2.5 collective-permute-done.8
  110.9 13.0 %collective-permute-done.5 = bf16[2,256,1024]{2,1,0:T(8,128)(2,1)} collective-permute-done((bf16[2,256,1024]{2,1,0:T(8,128)(2,1)}, bf16[2,256,1024]{2,1,0:T(8,128)(2,1)}, u32[]{:S(2)}, u32[]{:S(2)}) %collective-permute-start.5) | collective-permute-done | bytes 1048608 | tf_op jit(solution)/shard_map/ppermute | solution.py:382
  123.9 3.2 %add_convert_fusion = (bf16[2,256,1024]{2,1,0:T(8,128)(2,1)S(1)}, bf16[2,256,1024]{2,1,0:T(8,128)(2,1)S(1)}) fusion(bf16[2,256,1024]{2,1,0:T(8,128)(2,1)} %collective-permute-done.11, bf16[2,256,1024]{2,1,0:T(8,128)(2,1)S(1)} %get-tuple-element.74, pred[]{:T(512)S(6)} %eq.38, bf16[2,256,1024]{2,1,0:T(8,128)(2,1)} %collective-permute-done.5, ...), kind=kLoop, calls=%fused_computation | loop fusion | flops 7340032 | bytes 7340034 | tf_op jit(solution)/shard_map/convert_element_type | solution.py:313
  127.1 1.9 collective-permute-start.12
  129.0 3.4 %collective-permute-start.9 = (bf16[2,256,1024]{2,1,0:T(8,128)(2,1)S(1)}, bf16[2,256,1024]{2,1,0:T(8,128)(2,1)S(1)}, u32[]{:S(2)}, u32[]{:S(2)}) collective-permute-start(bf16[2,256,1024]{2,1,0:T(8,128)(2,1)S(1)} %get-tuple-element.76), channel_id=1, source_target_pairs={{0,4},{1,5},{2,6},{3,7},{4,8},{5,9},{6,10},{7,11},{8,12},{9,13},{1... | collective-permute-start | bytes 3145736 | tf_op jit(solution)/shard_map/ppermute | solution.py:386
  132.4 13.9 %collective-permute-done.3 = bf16[2,256,1024]{2,1,0:T(8,128)(2,1)S(1)} collective-permute-done((bf16[2,256,1024]{2,1,0:T(8,128)(2,1)}, bf16[2,256,1024]{2,1,0:T(8,128)(2,1)S(1)}, u32[]{:S(2)}, u32[]{:S(2)}) %collective-permute-start.3) | collective-permute-done | bytes 1048608 | tf_op jit(solution)/shard_map/ppermute | solution.py:382
  146.3 1.4 add_convert_fusion.7.own_ref
  148.3 1.9 collective-permute-done.9.up_ref
  150.2 1.0 copy-done.21
  151.2 11.5 %middle.1.refs_0_ = bf16[2,256,1024]{2,1,0:T(8,128)(2,1)} custom-call(bf16[2,256,1024]{2,1,0:T(8,128)(2,1)} %add_convert_fusion.7.own_ref, bf16[2,256,1024]{2,1,0:T(8,128)(2,1)} %copy-done.21, bf16[2,256,1024]{2,1,0:T(8,128)(2,1)} %copy-done.20, bf16[1,256,1024]{2,1,0:T(8,128)(2,1)} %image_ref.1, bf16[1024,1024]{1,0:T(8,128)(2,1)} %constant.44.clone.cos_ref, ...), custom_call_target="tpu_custom_call" | custom-call | flops 4294967296 | bytes 15728640 | tf_op jit(solution)/shard_map/middle/pallas_call | solution.py:288
  162.7 1.9 collective-permute-start.16
  164.6 3.4 %collective-permute-start.15 = (bf16[2,256,1024]{2,1,0:T(8,128)(2,1)}, bf16[2,256,1024]{2,1,0:T(8,128)(2,1)S(1)}, u32[]{:S(2)}, u32[]{:S(2)}) collective-permute-start(bf16[2,256,1024]{2,1,0:T(8,128)(2,1)} %middle.1.refs_0_), channel_id=1, source_target_pairs={{0,4},{1,5},{2,6},{3,7},{4,8},{5,9},{6,10},{7,11},{8,12},{9,13},{1... | collective-permute-start | bytes 3145736 | tf_op jit(solution)/shard_map/ppermute | solution.py:386
  168.0 6.9 %collective-permute-start.14 = (bf16[2,256,1024]{2,1,0:T(8,128)(2,1)}, bf16[2,256,1024]{2,1,0:T(8,128)(2,1)}, u32[]{:S(2)}, u32[]{:S(2)}) collective-permute-start(bf16[2,256,1024]{2,1,0:T(8,128)(2,1)} %middle.1.refs_0_), channel_id=1, source_target_pairs={{0,1},{1,0},{2,3},{3,2},{4,5},{5,4},{6,7},{7,6},{8,9},{9,8},{10,11... | collective-permute-start | bytes 3145736 | tf_op jit(solution)/shard_map/ppermute | solution.py:379
  175.5 7.7 %collective-permute-done.16 = bf16[2,256,1024]{2,1,0:T(8,128)(2,1)S(1)} collective-permute-done((bf16[2,256,1024]{2,1,0:T(8,128)(2,1)}, bf16[2,256,1024]{2,1,0:T(8,128)(2,1)S(1)}, u32[]{:S(2)}, u32[]{:S(2)}) %collective-permute-start.16) | collective-permute-done | bytes 1048608 | tf_op jit(solution)/shard_map/ppermute | solution.py:386
  183.2 1.9 collective-permute-done.15
  185.1 14.8 %collective-permute-done.13.refs_1_ = bf16[2,256,1024]{2,1,0:T(8,128)(2,1)S(1)} collective-permute-done((bf16[2,256,1024]{2,1,0:T(8,128)(2,1)}, bf16[2,256,1024]{2,1,0:T(8,128)(2,1)S(1)}, u32[]{:S(2)}, u32[]{:S(2)}) %collective-permute-start.13) | collective-permute-done | bytes 1048608 | tf_op jit(solution)/shard_map/ppermute | solution.py:382
  200.0 0.9 collective-permute-start.18
  201.5 1.1 collective-permute-start.19
  202.5 3.5 %collective-permute-start.20 = (bf16[2,256,1024]{2,1,0:T(8,128)(2,1)S(1)}, bf16[2,256,1024]{2,1,0:T(8,128)(2,1)S(1)}, u32[]{:S(2)}, u32[]{:S(2)}) collective-permute-start(bf16[2,256,1024]{2,1,0:T(8,128)(2,1)S(1)} %collective-permute-done.15), channel_id=1, source_target_pairs={{4,8},{5,9},{6,10},{7,11},{8,12},{9,13},{10,14},{11,15},{20,24},{2... | collective-permute-start | bytes 3145736 | tf_op jit(solution)/shard_map/ppermute | solution.py:386
  206.0 1.9 collective-permute-start.21
  208.0 13.0 %backward.4.spec_ref = f32[2,128,8192]{2,1,0:T(8,128)} custom-call(s32[2,16]{1,0:T(2,128)} %pad_add_fusion.meta_ref, f32[2,128,8192]{2,1,0:T(8,128)} %spec_ref.12, bf16[1024,1024]{1,0:T(8,128)(2,1)} %pupil_ref.19, bf16[1024,512]{1,0:T(8,128)(2,1)} %constant.43.clone.band_ref, bf16[2,256,1024]{2,1,0:T(8,128)(2,1)} %middle.1.refs_0_, ...), custom_call_target="tpu_custom_call" | custom-call | flops 2147483648 | bytes 28777216 | tf_op jit(solution)/shard_map/backward/pallas_call | solution.py:256
  221.0 3.9 %collective-permute-done.17.refs_0_ = bf16[2,256,1024]{2,1,0:T(8,128)(2,1)} collective-permute-done((bf16[2,256,1024]{2,1,0:T(8,128)(2,1)S(1)}, bf16[2,256,1024]{2,1,0:T(8,128)(2,1)}, u32[]{:S(2)}, u32[]{:S(2)}) %collective-permute-start.17) | collective-permute-done | bytes 1048608 | tf_op jit(solution)/shard_map/ppermute | solution.py:382
  224.9 3.6 %collective-permute-done.20 = bf16[2,256,1024]{2,1,0:T(8,128)(2,1)S(1)} collective-permute-done((bf16[2,256,1024]{2,1,0:T(8,128)(2,1)S(1)}, bf16[2,256,1024]{2,1,0:T(8,128)(2,1)S(1)}, u32[]{:S(2)}, u32[]{:S(2)}) %collective-permute-start.20) | collective-permute-done | bytes 1048608 | tf_op jit(solution)/shard_map/ppermute | solution.py:386
  228.5 3.9 %collective-permute-done.21 = bf16[2,256,1024]{2,1,0:T(8,128)(2,1)S(1)} collective-permute-done((bf16[2,256,1024]{2,1,0:T(8,128)(2,1)S(1)}, bf16[2,256,1024]{2,1,0:T(8,128)(2,1)S(1)}, u32[]{:S(2)}, u32[]{:S(2)}) %collective-permute-start.21) | collective-permute-done | bytes 1048608 | tf_op jit(solution)/shard_map/ppermute | solution.py:386
  232.4 1.1 collective-permute-start.24
  233.8 1.0 collective-permute-start.22
  234.8 0.7 collective-permute-start.25
  235.5 2.9 collective-permute-start.26
  238.4 12.1 %backward.5.spec_ref = f32[2,128,8192]{2,1,0:T(8,128)} custom-call(s32[2,16]{1,0:T(2,128)} %pad_add_fusion.meta_ref, f32[2,128,8192]{2,1,0:T(8,128)} %backward.4.spec_ref, bf16[1024,1024]{1,0:T(8,128)(2,1)} %pupil_ref.19, bf16[1024,512]{1,0:T(8,128)(2,1)} %constant.43.clone.band_ref, bf16[2,256,1024]{2,1,0:T(8,128)(2,1)} %collective-permute-done.17.refs_0_, ...), custom_call_target="tpu_custom_call" | custom-call | flops 2147483648 | bytes 28777216 | tf_op jit(solution)/shard_map/backward/pallas_call | solution.py:256
  250.5 7.6 %collective-permute-done.22.refs_0_ = bf16[2,256,1024]{2,1,0:T(8,128)(2,1)S(1)} collective-permute-done((bf16[2,256,1024]{2,1,0:T(8,128)(2,1)S(1)}, bf16[2,256,1024]{2,1,0:T(8,128)(2,1)S(1)}, u32[]{:S(2)}, u32[]{:S(2)}) %collective-permute-start.22) | collective-permute-done | bytes 1048608 | tf_op jit(solution)/shard_map/ppermute | solution.py:382
  258.1 1.0 copy-done.17
  259.4 1.7 collective-permute-start.28
  262.0 12.8 %backward.6.spec_ref = f32[2,128,8192]{2,1,0:T(8,128)} custom-call(s32[2,16]{1,0:T(2,128)} %pad_add_fusion.meta_ref, f32[2,128,8192]{2,1,0:T(8,128)} %backward.5.spec_ref, bf16[1024,1024]{1,0:T(8,128)(2,1)} %pupil_ref.19, bf16[1024,512]{1,0:T(8,128)(2,1)} %constant.43.clone.band_ref, bf16[2,256,1024]{2,1,0:T(8,128)(2,1)} %copy-done.8, ...), custom_call_target="tpu_custom_call" | custom-call | flops 2147483648 | bytes 28777216 | tf_op jit(solution)/shard_map/backward/pallas_call | solution.py:256
  274.8 11.0 %collective-permute-done.27.refs_0_ = bf16[2,256,1024]{2,1,0:T(8,128)(2,1)S(1)} collective-permute-done((bf16[2,256,1024]{2,1,0:T(8,128)(2,1)S(1)}, bf16[2,256,1024]{2,1,0:T(8,128)(2,1)S(1)}, u32[]{:S(2)}, u32[]{:S(2)}) %collective-permute-start.27) | collective-permute-done | bytes 1048608 | tf_op jit(solution)/shard_map/ppermute | solution.py:382
  285.8 0.9 collective-permute-start.30
  286.7 2.3 collective-permute-done.30.refs_3_
  289.0 1.0 copy-done.16
  290.0 13.0 %backward.7 = f32[2,128,8192]{2,1,0:T(8,128)} custom-call(s32[2,16]{1,0:T(2,128)} %pad_add_fusion.meta_ref, f32[2,128,8192]{2,1,0:T(8,128)} %backward.6.spec_ref, bf16[1024,1024]{1,0:T(8,128)(2,1)} %pupil_ref.19, bf16[1024,512]{1,0:T(8,128)(2,1)} %constant.43.clone.band_ref, bf16[2,256,1024]{2,1,0:T(8,128)(2,1)} %copy-done.14, ...), custom_call_target="tpu_custom_call" | custom-call | flops 2147483648 | bytes 28777216 | tf_op jit(solution)/shard_map/backward/pallas_call | solution.py:256
  (65 shorter events, 4.8 us)
Async XLA Ops:
  6.3 7.7 %collective-permute-start = (bf16[1,2,256,1024]{3,2,1,0:T(8,128)(2,1)}, bf16[1,2,256,1024]{3,2,1,0:T(8,128)(2,1)S(1)}, u32[]{:S(2)}, u32[]{:S(2)}) collective-permute-start(bf16[1,2,256,1024]{3,2,1,0:T(8,128)(2,1)} %forward.6), channel_id=1, source_target_pairs={{0,1},{1,0},{2,3},{3,2},{4,5},{5,4},{6,7},{7,6},{8,9},{9,8},{10,11... | collective-permute-start | bytes 3145736 | tf_op jit(solution)/shard_map/ppermute | solution.py:379
  14.0 15.8 %collective-permute-start.1 = (bf16[3,2,256,1024]{3,2,1,0:T(8,128)(2,1)}, bf16[3,2,256,1024]{3,2,1,0:T(8,128)(2,1)S(1)}, u32[]{:S(2)}, u32[]{:S(2)}) collective-permute-start(bf16[3,2,256,1024]{3,2,1,0:T(8,128)(2,1)} %forward.7), channel_id=1, source_target_pairs={{0,1},{1,0},{2,3},{3,2},{4,5},{5,4},{6,7},{7,6},{8,9},{9,8},{10,11... | collective-permute-start | bytes 9437192 | tf_op jit(solution)/shard_map/ppermute | solution.py:379
  14.0 1.0 copy-start.19
  19.6 8.3 %copy-start.18 = (bf16[2,256,1024]{2,1,0:T(8,128)(2,1)S(1)}, bf16[2,256,1024]{2,1,0:T(8,128)(2,1)}, u32[]{:S(2)}) copy-start(bf16[2,256,1024]{2,1,0:T(8,128)(2,1)} %forward.8) | copy-start | bytes 3145732
  27.3 63.6 %collective-permute-start.2 = (bf16[4,2,256,1024]{3,2,1,0:T(8,128)(2,1)}, bf16[4,2,256,1024]{3,2,1,0:T(8,128)(2,1)}, u32[]{:S(2)}, u32[]{:S(2)}) collective-permute-start(bf16[4,2,256,1024]{3,2,1,0:T(8,128)(2,1)} %forward.9), channel_id=1, source_target_pairs={{0,1},{1,0},{2,3},{3,2},{4,5},{5,4},{6,7},{7,6},{8,9},{9,8},{10,11... | collective-permute-start | bytes 12582920 | tf_op jit(solution)/shard_map/ppermute | solution.py:379
  27.9 25.1 %collective-permute-start.6 = (bf16[2,256,1024]{2,1,0:T(8,128)(2,1)S(1)}, bf16[2,256,1024]{2,1,0:T(8,128)(2,1)S(1)}, u32[]{:S(2)}, u32[]{:S(2)}) collective-permute-start(bf16[2,256,1024]{2,1,0:T(8,128)(2,1)S(1)} %copy-done.18), channel_id=1, source_target_pairs={{0,2},{1,3},{2,0},{3,1},{4,6},{5,7},{6,4},{7,5},{8,10},{9,11},{10,... | collective-permute-start | bytes 3145736 | tf_op jit(solution)/shard_map/ppermute | solution.py:382
  29.8 1.6 copy-start.3
  38.7 37.9 %copy-start.4 = (bf16[2,256,1024]{2,1,0:T(8,128)(2,1)S(1)}, bf16[2,256,1024]{2,1,0:T(8,128)(2,1)}, u32[]{:S(2)}) copy-start(bf16[2,256,1024]{2,1,0:T(8,128)(2,1)} %get-tuple-element.46) | copy-start | bytes 3145732
  38.7 36.9 %collective-permute-start.4 = (bf16[2,256,1024]{2,1,0:T(8,128)(2,1)}, bf16[2,256,1024]{2,1,0:T(8,128)(2,1)S(1)}, u32[]{:S(2)}, u32[]{:S(2)}) collective-permute-start(bf16[2,256,1024]{2,1,0:T(8,128)(2,1)} %get-tuple-element.47), channel_id=1, source_target_pairs={{0,2},{1,3},{2,0},{3,1},{4,6},{5,7},{6,4},{7,5},{8,10},{9,11},{10,... | collective-permute-start | bytes 3145736 | tf_op jit(solution)/shard_map/ppermute | solution.py:382
  54.7 20.9 %collective-permute-start.10 = (bf16[2,256,1024]{2,1,0:T(8,128)(2,1)S(1)}, bf16[2,256,1024]{2,1,0:T(8,128)(2,1)}, u32[]{:S(2)}, u32[]{:S(2)}) collective-permute-start(bf16[2,256,1024]{2,1,0:T(8,128)(2,1)S(1)} %add_convert_fusion.4), channel_id=1, source_target_pairs={{12,8},{13,9},{14,10},{15,11},{28,24},{29,25},{30,26},{31,27}} | collective-permute-start | bytes 3145736 | tf_op jit(solution)/shard_map/ppermute | solution.py:386
  56.3 25.3 %collective-permute-start.7 = (bf16[2,256,1024]{2,1,0:T(8,128)(2,1)S(1)}, bf16[2,256,1024]{2,1,0:T(8,128)(2,1)}, u32[]{:S(2)}, u32[]{:S(2)}) collective-permute-start(bf16[2,256,1024]{2,1,0:T(8,128)(2,1)S(1)} %add_convert_fusion.4), channel_id=1, source_target_pairs={{0,4},{1,5},{2,6},{3,7},{16,20},{17,21},{18,22},{19,23}} | collective-permute-start | bytes 3145736 | tf_op jit(solution)/shard_map/ppermute | solution.py:386
  75.6 1.0 copy-start.5
  80.1 28.4 %collective-permute-start.11 = (bf16[2,256,1024]{2,1,0:T(8,128)(2,1)}, bf16[2,256,1024]{2,1,0:T(8,128)(2,1)}, u32[]{:S(2)}, u32[]{:S(2)}) collective-permute-start(bf16[2,256,1024]{2,1,0:T(8,128)(2,1)} %get-tuple-element.73), channel_id=1, source_target_pairs={{8,4},{9,5},{10,6},{11,7},{12,8},{13,9},{14,10},{15,11},{24,20},{2... | collective-permute-start | bytes 3145736 | tf_op jit(solution)/shard_map/ppermute | solution.py:386
  83.4 27.5 %collective-permute-start.8 = (bf16[2,256,1024]{2,1,0:T(8,128)(2,1)S(1)}, bf16[2,256,1024]{2,1,0:T(8,128)(2,1)S(1)}, u32[]{:S(2)}, u32[]{:S(2)}) collective-permute-start(bf16[2,256,1024]{2,1,0:T(8,128)(2,1)S(1)} %add_convert_fusion.3), channel_id=1, source_target_pairs={{0,4},{1,5},{2,6},{3,7},{4,8},{5,9},{6,10},{7,11},{16,20},{17,21},... | collective-permute-start | bytes 3145736 | tf_op jit(solution)/shard_map/ppermute | solution.py:386
  100.9 23.0 %collective-permute-start.5 = (bf16[2,256,1024]{2,1,0:T(8,128)(2,1)}, bf16[2,256,1024]{2,1,0:T(8,128)(2,1)}, u32[]{:S(2)}, u32[]{:S(2)}) collective-permute-start(bf16[2,256,1024]{2,1,0:T(8,128)(2,1)} %get-tuple-element.49), channel_id=1, source_target_pairs={{0,2},{1,3},{2,0},{3,1},{4,6},{5,7},{6,4},{7,5},{8,10},{9,11},{10,... | collective-permute-start | bytes 3145736 | tf_op jit(solution)/shard_map/ppermute | solution.py:382
  101.6 44.7 %collective-permute-start.3 = (bf16[2,256,1024]{2,1,0:T(8,128)(2,1)}, bf16[2,256,1024]{2,1,0:T(8,128)(2,1)S(1)}, u32[]{:S(2)}, u32[]{:S(2)}) collective-permute-start(bf16[2,256,1024]{2,1,0:T(8,128)(2,1)} %get-tuple-element.45), channel_id=1, source_target_pairs={{0,2},{1,3},{2,0},{3,1},{4,6},{5,7},{6,4},{7,5},{8,10},{9,11},{10,... | collective-permute-start | bytes 3145736 | tf_op jit(solution)/shard_map/ppermute | solution.py:382
  123.9 22.4 %copy-start.11 = (bf16[2,256,1024]{2,1,0:T(8,128)(2,1)S(1)}, bf16[2,256,1024]{2,1,0:T(8,128)(2,1)}, u32[]{:S(2)}) copy-start(bf16[2,256,1024]{2,1,0:T(8,128)(2,1)} %get-tuple-element.44) | copy-start | bytes 3145732
  127.1 21.2 %collective-permute-start.12 = (bf16[2,256,1024]{2,1,0:T(8,128)(2,1)S(1)}, bf16[2,256,1024]{2,1,0:T(8,128)(2,1)S(1)}, u32[]{:S(2)}, u32[]{:S(2)}) collective-permute-start(bf16[2,256,1024]{2,1,0:T(8,128)(2,1)S(1)} %get-tuple-element.75), channel_id=1, source_target_pairs={{4,0},{5,1},{6,2},{7,3},{8,4},{9,5},{10,6},{11,7},{12,8},{13,9},{1... | collective-permute-start | bytes 3145736 | tf_op jit(solution)/shard_map/ppermute | solution.py:386
  129.0 21.2 %collective-permute-start.9 = (bf16[2,256,1024]{2,1,0:T(8,128)(2,1)S(1)}, bf16[2,256,1024]{2,1,0:T(8,128)(2,1)S(1)}, u32[]{:S(2)}, u32[]{:S(2)}) collective-permute-start(bf16[2,256,1024]{2,1,0:T(8,128)(2,1)S(1)} %get-tuple-element.76), channel_id=1, source_target_pairs={{0,4},{1,5},{2,6},{3,7},{4,8},{5,9},{6,10},{7,11},{8,12},{9,13},{1... | collective-permute-start | bytes 3145736 | tf_op jit(solution)/shard_map/ppermute | solution.py:386
  148.3 1.9 copy-start.20
  150.2 1.0 copy-start.21
  162.7 20.4 %collective-permute-start.16 = (bf16[2,256,1024]{2,1,0:T(8,128)(2,1)}, bf16[2,256,1024]{2,1,0:T(8,128)(2,1)S(1)}, u32[]{:S(2)}, u32[]{:S(2)}) collective-permute-start(bf16[2,256,1024]{2,1,0:T(8,128)(2,1)} %middle.1.refs_0_), channel_id=1, source_target_pairs={{4,0},{5,1},{6,2},{7,3},{8,4},{9,5},{10,6},{11,7},{12,8},{13,9},{1... | collective-permute-start | bytes 3145736 | tf_op jit(solution)/shard_map/ppermute | solution.py:386
  164.6 20.5 %collective-permute-start.15 = (bf16[2,256,1024]{2,1,0:T(8,128)(2,1)}, bf16[2,256,1024]{2,1,0:T(8,128)(2,1)S(1)}, u32[]{:S(2)}, u32[]{:S(2)}) collective-permute-start(bf16[2,256,1024]{2,1,0:T(8,128)(2,1)} %middle.1.refs_0_), channel_id=1, source_target_pairs={{0,4},{1,5},{2,6},{3,7},{4,8},{5,9},{6,10},{7,11},{8,12},{9,13},{1... | collective-permute-start | bytes 3145736 | tf_op jit(solution)/shard_map/ppermute | solution.py:386
  168.0 17.1 %collective-permute-start.14 = (bf16[2,256,1024]{2,1,0:T(8,128)(2,1)}, bf16[2,256,1024]{2,1,0:T(8,128)(2,1)}, u32[]{:S(2)}, u32[]{:S(2)}) collective-permute-start(bf16[2,256,1024]{2,1,0:T(8,128)(2,1)} %middle.1.refs_0_), channel_id=1, source_target_pairs={{0,1},{1,0},{2,3},{3,2},{4,5},{5,4},{6,7},{7,6},{8,9},{9,8},{10,11... | collective-permute-start | bytes 3145736 | tf_op jit(solution)/shard_map/ppermute | solution.py:379
  174.9 24.9 %collective-permute-start.13 = (bf16[2,256,1024]{2,1,0:T(8,128)(2,1)}, bf16[2,256,1024]{2,1,0:T(8,128)(2,1)S(1)}, u32[]{:S(2)}, u32[]{:S(2)}) collective-permute-start(bf16[2,256,1024]{2,1,0:T(8,128)(2,1)} %middle.1.refs_0_), channel_id=1, source_target_pairs={{0,2},{1,3},{2,0},{3,1},{4,6},{5,7},{6,4},{7,5},{8,10},{9,11},{10,... | collective-permute-start | bytes 3145736 | tf_op jit(solution)/shard_map/ppermute | solution.py:382
  199.9 1.0 copy-start.12
  200.0 7.9 %copy-start = (bf16[2,256,1024]{2,1,0:T(8,128)(2,1)}, bf16[2,256,1024]{2,1,0:T(8,128)(2,1)S(1)}, u32[]{:S(2)}) copy-start(bf16[2,256,1024]{2,1,0:T(8,128)(2,1)S(1)} %broadcast_select_fusion.refs_3_) | copy-start | bytes 3145732
  200.0 21.0 %collective-permute-start.18 = (bf16[2,256,1024]{2,1,0:T(8,128)(2,1)S(1)}, bf16[2,256,1024]{2,1,0:T(8,128)(2,1)S(1)}, u32[]{:S(2)}, u32[]{:S(2)}) collective-permute-start(bf16[2,256,1024]{2,1,0:T(8,128)(2,1)S(1)} %broadcast_select_fusion.refs_3_), channel_id=1, source_target_pairs={{0,1},{1,0},{2,3},{3,2},{4,5},{5,4},{6,7},{7,6},{8,9},{9,8},{10,11... | collective-permute-start | bytes 3145736 | tf_op jit(solution)/shard_map/ppermute | solution.py:379
  200.9 24.0 %collective-permute-start.17 = (bf16[2,256,1024]{2,1,0:T(8,128)(2,1)S(1)}, bf16[2,256,1024]{2,1,0:T(8,128)(2,1)}, u32[]{:S(2)}, u32[]{:S(2)}) collective-permute-start(bf16[2,256,1024]{2,1,0:T(8,128)(2,1)S(1)} %broadcast_select_fusion.refs_3_), channel_id=1, source_target_pairs={{0,2},{1,3},{2,0},{3,1},{4,6},{5,7},{6,4},{7,5},{8,10},{9,11},{10,... | collective-permute-start | bytes 3145736 | tf_op jit(solution)/shard_map/ppermute | solution.py:382
  201.5 23.5 %collective-permute-start.19 = (bf16[2,256,1024]{2,1,0:T(8,128)(2,1)}, bf16[2,256,1024]{2,1,0:T(8,128)(2,1)S(1)}, u32[]{:S(2)}, u32[]{:S(2)}) collective-permute-start(bf16[2,256,1024]{2,1,0:T(8,128)(2,1)} %copy-done.12), channel_id=1, source_target_pairs={{0,1},{1,0},{2,3},{3,2},{4,5},{5,4},{6,7},{7,6},{8,9},{9,8},{10,11... | collective-permute-start | bytes 3145736 | tf_op jit(solution)/shard_map/ppermute | solution.py:379
  202.5 26.0 %collective-permute-start.20 = (bf16[2,256,1024]{2,1,0:T(8,128)(2,1)S(1)}, bf16[2,256,1024]{2,1,0:T(8,128)(2,1)S(1)}, u32[]{:S(2)}, u32[]{:S(2)}) collective-permute-start(bf16[2,256,1024]{2,1,0:T(8,128)(2,1)S(1)} %collective-permute-done.15), channel_id=1, source_target_pairs={{4,8},{5,9},{6,10},{7,11},{8,12},{9,13},{10,14},{11,15},{20,24},{2... | collective-permute-start | bytes 3145736 | tf_op jit(solution)/shard_map/ppermute | solution.py:386
  206.0 26.4 %collective-permute-start.21 = (bf16[2,256,1024]{2,1,0:T(8,128)(2,1)S(1)}, bf16[2,256,1024]{2,1,0:T(8,128)(2,1)S(1)}, u32[]{:S(2)}, u32[]{:S(2)}) collective-permute-start(bf16[2,256,1024]{2,1,0:T(8,128)(2,1)S(1)} %collective-permute-done.16), channel_id=1, source_target_pairs={{4,0},{5,1},{6,2},{7,3},{8,4},{9,5},{10,6},{11,7},{20,16},{21,17},... | collective-permute-start | bytes 3145736 | tf_op jit(solution)/shard_map/ppermute | solution.py:386
  221.0 12.7 %copy-start.7 = (bf16[2,256,1024]{2,1,0:T(8,128)(2,1)}, bf16[2,256,1024]{2,1,0:T(8,128)(2,1)S(1)}, u32[]{:S(2)}) copy-start(bf16[2,256,1024]{2,1,0:T(8,128)(2,1)S(1)} %collective-permute-done.18.refs_1_) | copy-start | bytes 3145732
  224.9 7.4 %copy-start.10 = (bf16[2,256,1024]{2,1,0:T(8,128)(2,1)}, bf16[2,256,1024]{2,1,0:T(8,128)(2,1)S(1)}, u32[]{:S(2)}) copy-start(bf16[2,256,1024]{2,1,0:T(8,128)(2,1)S(1)} %collective-permute-done.19.refs_2_) | copy-start | bytes 3145732
  232.4 18.1 %collective-permute-start.24 = (bf16[2,256,1024]{2,1,0:T(8,128)(2,1)}, bf16[2,256,1024]{2,1,0:T(8,128)(2,1)S(1)}, u32[]{:S(2)}, u32[]{:S(2)}) collective-permute-start(bf16[2,256,1024]{2,1,0:T(8,128)(2,1)} %collective-permute-done.17.refs_0_), channel_id=1, source_target_pairs={{0,1},{1,0},{2,3},{3,2},{4,5},{5,4},{6,7},{7,6},{8,9},{9,8},{10,11... | collective-permute-start | bytes 3145736 | tf_op jit(solution)/shard_map/ppermute | solution.py:379
  233.7 4.7 %copy-start.1 = (bf16[2,256,1024]{2,1,0:T(8,128)(2,1)}, bf16[2,256,1024]{2,1,0:T(8,128)(2,1)S(1)}, u32[]{:S(2)}) copy-start(bf16[2,256,1024]{2,1,0:T(8,128)(2,1)S(1)} %select_select_fusion.1.refs_3_) | copy-start | bytes 3145732
  233.7 16.8 %collective-permute-start.23 = (bf16[2,256,1024]{2,1,0:T(8,128)(2,1)S(1)}, bf16[2,256,1024]{2,1,0:T(8,128)(2,1)S(1)}, u32[]{:S(2)}, u32[]{:S(2)}) collective-permute-start(bf16[2,256,1024]{2,1,0:T(8,128)(2,1)S(1)} %select_select_fusion.1.refs_3_), channel_id=1, source_target_pairs={{0,1},{1,0},{2,3},{3,2},{4,5},{5,4},{6,7},{7,6},{8,9},{9,8},{10,11... | collective-permute-start | bytes 3145736 | tf_op jit(solution)/shard_map/ppermute | solution.py:379
  233.8 24.4 %collective-permute-start.22 = (bf16[2,256,1024]{2,1,0:T(8,128)(2,1)S(1)}, bf16[2,256,1024]{2,1,0:T(8,128)(2,1)S(1)}, u32[]{:S(2)}, u32[]{:S(2)}) collective-permute-start(bf16[2,256,1024]{2,1,0:T(8,128)(2,1)S(1)} %select_select_fusion.1.refs_3_), channel_id=1, source_target_pairs={{0,2},{1,3},{2,0},{3,1},{4,6},{5,7},{6,4},{7,5},{8,10},{9,11},{10,... | collective-permute-start | bytes 3145736 | tf_op jit(solution)/shard_map/ppermute | solution.py:382
  234.8 23.4 %collective-permute-start.25 = (bf16[2,256,1024]{2,1,0:T(8,128)(2,1)S(1)}, bf16[2,256,1024]{2,1,0:T(8,128)(2,1)S(1)}, u32[]{:S(2)}, u32[]{:S(2)}) collective-permute-start(bf16[2,256,1024]{2,1,0:T(8,128)(2,1)S(1)} %collective-permute-done.20), channel_id=1, source_target_pairs={{8,12},{9,13},{10,14},{11,15},{24,28},{25,29},{26,30},{27,31}} | collective-permute-start | bytes 3145736 | tf_op jit(solution)/shard_map/ppermute | solution.py:386
  235.5 23.7 %collective-permute-start.26 = (bf16[2,256,1024]{2,1,0:T(8,128)(2,1)S(1)}, bf16[2,256,1024]{2,1,0:T(8,128)(2,1)}, u32[]{:S(2)}, u32[]{:S(2)}) collective-permute-start(bf16[2,256,1024]{2,1,0:T(8,128)(2,1)S(1)} %collective-permute-done.21), channel_id=1, source_target_pairs={{4,0},{5,1},{6,2},{7,3},{20,16},{21,17},{22,18},{23,19}} | collective-permute-start | bytes 3145736 | tf_op jit(solution)/shard_map/ppermute | solution.py:386
  250.5 8.9 %copy-start.6 = (bf16[2,256,1024]{2,1,0:T(8,128)(2,1)}, bf16[2,256,1024]{2,1,0:T(8,128)(2,1)S(1)}, u32[]{:S(2)}) copy-start(bf16[2,256,1024]{2,1,0:T(8,128)(2,1)S(1)} %collective-permute-done.24.refs_2_) | copy-start | bytes 3145732
  250.5 8.8 %copy-start.9 = (bf16[2,256,1024]{2,1,0:T(8,128)(2,1)}, bf16[2,256,1024]{2,1,0:T(8,128)(2,1)S(1)}, u32[]{:S(2)}) copy-start(bf16[2,256,1024]{2,1,0:T(8,128)(2,1)S(1)} %collective-permute-done.23.refs_1_) | copy-start | bytes 3145732
  258.1 3.5 %copy-start.8 = (bf16[2,256,1024]{2,1,0:T(8,128)(2,1)}, bf16[2,256,1024]{2,1,0:T(8,128)(2,1)S(1)}, u32[]{:S(2)}) copy-start(bf16[2,256,1024]{2,1,0:T(8,128)(2,1)S(1)} %collective-permute-done.22.refs_0_) | copy-start | bytes 3145732
  258.1 1.0 copy-start.17
  259.4 2.6 copy-start.2
  259.4 15.4 %collective-permute-start.28 = (bf16[2,256,1024]{2,1,0:T(8,128)(2,1)S(1)}, bf16[2,256,1024]{2,1,0:T(8,128)(2,1)S(1)}, u32[]{:S(2)}, u32[]{:S(2)}) collective-permute-start(bf16[2,256,1024]{2,1,0:T(8,128)(2,1)S(1)} %select_select_fusion.refs_3_), channel_id=1, source_target_pairs={{0,1},{1,0},{2,3},{3,2},{4,5},{5,4},{6,7},{7,6},{8,9},{9,8},{10,11... | collective-permute-start | bytes 3145736 | tf_op jit(solution)/shard_map/ppermute | solution.py:379
  261.1 24.7 %collective-permute-start.27 = (bf16[2,256,1024]{2,1,0:T(8,128)(2,1)S(1)}, bf16[2,256,1024]{2,1,0:T(8,128)(2,1)S(1)}, u32[]{:S(2)}, u32[]{:S(2)}) collective-permute-start(bf16[2,256,1024]{2,1,0:T(8,128)(2,1)S(1)} %select_select_fusion.refs_3_), channel_id=1, source_target_pairs={{0,2},{1,3},{2,0},{3,1},{4,6},{5,7},{6,4},{7,5},{8,10},{9,11},{10,... | collective-permute-start | bytes 3145736 | tf_op jit(solution)/shard_map/ppermute | solution.py:382
  261.6 24.2 %collective-permute-start.29 = (bf16[2,256,1024]{2,1,0:T(8,128)(2,1)S(1)}, bf16[2,256,1024]{2,1,0:T(8,128)(2,1)S(1)}, u32[]{:S(2)}, u32[]{:S(2)}) collective-permute-start(bf16[2,256,1024]{2,1,0:T(8,128)(2,1)S(1)} %collective-permute-done.22.refs_0_), channel_id=1, source_target_pairs={{0,1},{1,0},{2,3},{3,2},{4,5},{5,4},{6,7},{7,6},{8,9},{9,8},{10,11... | collective-permute-start | bytes 3145736 | tf_op jit(solution)/shard_map/ppermute | solution.py:379
  274.8 14.2 %copy-start.13 = (bf16[2,256,1024]{2,1,0:T(8,128)(2,1)}, bf16[2,256,1024]{2,1,0:T(8,128)(2,1)S(1)}, u32[]{:S(2)}) copy-start(bf16[2,256,1024]{2,1,0:T(8,128)(2,1)S(1)} %collective-permute-done.28.refs_1_) | copy-start | bytes 3145732
  285.8 3.2 %copy-start.14 = (bf16[2,256,1024]{2,1,0:T(8,128)(2,1)}, bf16[2,256,1024]{2,1,0:T(8,128)(2,1)S(1)}, u32[]{:S(2)}) copy-start(bf16[2,256,1024]{2,1,0:T(8,128)(2,1)S(1)} %collective-permute-done.27.refs_0_) | copy-start | bytes 3145732
  285.8 3.2 %copy-start.15 = (bf16[2,256,1024]{2,1,0:T(8,128)(2,1)}, bf16[2,256,1024]{2,1,0:T(8,128)(2,1)S(1)}, u32[]{:S(2)}) copy-start(bf16[2,256,1024]{2,1,0:T(8,128)(2,1)S(1)} %collective-permute-done.29.refs_2_) | copy-start | bytes 3145732
  285.8 3.2 %collective-permute-start.30 = (bf16[2,256,1024]{2,1,0:T(8,128)(2,1)S(1)}, bf16[2,256,1024]{2,1,0:T(8,128)(2,1)S(1)}, u32[]{:S(2)}, u32[]{:S(2)}) collective-permute-start(bf16[2,256,1024]{2,1,0:T(8,128)(2,1)S(1)} %collective-permute-done.27.refs_0_), channel_id=1, source_target_pairs={{0,1},{1,0},{2,3},{3,2},{4,5},{5,4},{6,7},{7,6},{8,9},{9,8},{10,11... | collective-permute-start | bytes 3145736 | tf_op jit(solution)/shard_map/ppermute | solution.py:379
  289.0 1.0 copy-start.16

commit v4 on v3

--- a/solution.py
+++ b/solution.py
@@ -12,7 +12,7 @@
 step_size = 0.5
 lane = 128
 row_tile = 16
-vmem_bytes = 56 * 1024 * 1024
+vmem_bytes = 64 * 1024 * 1024 - 512 * 1024
 
 
 def fourier_tables(crop_width):
@@ -107,19 +107,23 @@
 
 
 def backward_kernel(meta_ref, spec_ref, pupil_ref, band_ref, *refs, slots, win):
-    back_refs = refs[: len(slots)]
-    out_ref, held, sems = refs[len(slots) :]
+    back_refs, (out_ref, held, sems) = refs[:-3], refs[-3:]
+    stacked = len(back_refs) < len(slots)
     step = pl.program_id(0)
     count = len(slots)
     tile_rows, crop_width = win.tile_rows, win.crop_width
 
     def fetch(index, buffer):
-        for number, back_ref in enumerate(back_refs):
+        for number, back_ref in enumerate([] if stacked else back_refs):
 
             @pl.when(index == number)
             def _():
                 pltpu.make_async_copy(back_ref, held.at[buffer], sems.at[buffer]).start()
 
+        if stacked:
+            source = back_refs[0].at[index]
+            pltpu.make_async_copy(source, held.at[buffer], sems.at[buffer]).start()
+
     @pl.when(step == 0)
     def _():
         fetch(0, 0)
@@ -130,7 +134,8 @@
         fetch(step + 1, (step + 1) % 2)
 
     buffer = step % 2
-    pltpu.make_async_copy(back_refs[0], held.at[buffer], sems.at[buffer]).wait()
+    sample = back_refs[0].at[0] if stacked else back_refs[0]
+    pltpu.make_async_copy(sample, held.at[buffer], sems.at[buffer]).wait()
     slot = pick(slots, step)
     first_row, left = meta_ref[0, slot], meta_ref[1, slot]
 
@@ -151,24 +156,24 @@
 
 
 def pick(values, index):
+    if list(values) == list(range(len(values))):
+        return index
     result = jnp.int32(values[0])
     for number, value in enumerate(values[1:], 1):
         result = jnp.where(index == number, jnp.int32(value), result)
     return result
 
 
-def middle_kernel(
-    own_ref, up_ref, down_ref, image_ref, cos_ref, sin_ref, out_ref, mid_ref, resid_ref
-):
+def middle_kernel(*refs, terms):
+    term_refs, (image_ref, cos_ref, sin_ref, out_ref, mid_ref, resid_ref) = refs[:terms], refs[terms:]
     step = pl.program_id(0)
-    _, band, crop_width = own_ref.shape
+    _, band, crop_width = term_refs[0].shape
     block = cos_ref.shape[1]
     blocks = crop_width // block
 
     @pl.when(step == 0)
     def _():
-        total = own_ref[...].astype(jnp.float32) + up_ref[...].astype(jnp.float32)
-        total = total + down_ref[...].astype(jnp.float32)
+        total = sum(ref[...].astype(jnp.float32) for ref in term_refs)
         mid_ref[...] = total.astype(jnp.bfloat16).reshape(2 * band, crop_width)
 
     def products(left):
@@ -180,8 +185,8 @@
         by_cos, by_sin = products(mid_ref[...])
         field_real = by_cos[:band] - by_sin[band:]
         field_imag = by_sin[:band] + by_cos[band:]
-        magnitude = jnp.sqrt(field_real * field_real + field_imag * field_imag)
-        keeping = 1.0 - image_ref[0].astype(jnp.float32) / jnp.maximum(magnitude, 1.0)
+        power = field_real * field_real + field_imag * field_imag
+        keeping = 1.0 - image_ref[0].astype(jnp.float32) * lax.rsqrt(jnp.maximum(power, 1.0))
         resid = jnp.concatenate([field_real * keeping, field_imag * keeping], axis=0)
         columns = pl.ds(pl.multiple_of(step * block, block), block)
         resid_ref[:, columns] = resid.astype(jnp.bfloat16)
@@ -265,7 +270,7 @@
                 pl.BlockSpec((pl.Element(win.rows), pl.Element(crop_width)), row),
                 pl.BlockSpec((pl.Element(win.rows), pl.Element(2 * band)), row),
             ]
-            + [pl.BlockSpec(memory_space=pl.ANY)] * count,
+            + [pl.BlockSpec(memory_space=pl.ANY)] * len(backs),
             out_specs=pl.BlockSpec(spectrum.shape, lambda i, meta: (0, 0, 0)),
             scratch_shapes=[
                 pltpu.VMEM((2, 2, band, crop_width), jnp.bfloat16),
@@ -279,19 +284,17 @@
     )(meta, spectrum, pupil, band_table, *backs)
 
 
-def middle(own, up, down, image, cos_table, sin_table):
-    _, band, crop_width = own.shape
+def middle(terms, image, cos_table, sin_table):
+    _, band, crop_width = terms[0].shape
     block = min(256, crop_width)
     blocks = crop_width // block
     table = pl.BlockSpec((crop_width, block), lambda j: (0, j % blocks))
     whole = pl.BlockSpec((2, band, crop_width), lambda j: (0, 0, 0))
     return pl.pallas_call(
-        middle_kernel,
+        functools.partial(middle_kernel, terms=len(terms)),
         grid=(2 * blocks,),
-        in_specs=[
-            whole,
-            whole,
-            whole,
+        in_specs=[whole] * len(terms)
+        + [
             pl.BlockSpec((1, band, block), lambda j: (0, 0, jnp.minimum(j, blocks - 1))),
             table,
             table,
@@ -306,37 +309,11 @@
             transcendentals=0,
         ),
         name="middle",
-    )(own, up, down, image, cos_table, sin_table)
+    )(*terms, image, cos_table, sin_table)
 
 
 def total(*terms):
     return sum(term.astype(jnp.float32) for term in terms).astype(jnp.bfloat16)
-
-
-def far_first(planes):
-    rows = []
-    for z in range(planes):
-        upward = 2 * z < planes
-        rows.append(
-            sorted(range(planes), key=lambda q: (-abs(q - z), (q < z) if upward else (q > z)))
-        )
-    return rows
-
-
-def chosen(plane, options):
-    groups = []
-    for z, value in options.items():
-        for entry in groups:
-            if entry[0] is value:
-                entry[1].append(z)
-                break
-        else:
-            groups.append((value, [z]))
-    result = groups[0][0]
-    for value, members in groups[1:]:
-        here = functools.reduce(jnp.logical_or, [plane == z for z in members])
-        result = jnp.where(here, value, result)
-    return result
 
 
 def per_device(spectrum, pupil, measured, centre_rows, centre_cols):
@@ -355,25 +332,31 @@
     )
     cos_table, sin_table = jnp.asarray(cos_table), jnp.asarray(sin_table)
 
-    order = far_first(planes)
-    first = [(0, 2)]
-    second = [(0, 0), (1, 2), (1, 0)]
-    others = [(j, y) for j in range(2, planes) for y in (2, 0)]
-    groups = [first, second, others]
+    half = crop_width // 2
+
+    def image_meta(ids):
+        match = ids[:, None] == jnp.arange(count, dtype=jnp.int32)[None, :]
+        tops = jnp.sum(jnp.where(match, centre_rows[None, :], 0), axis=1) - half
+        lefts = jnp.sum(jnp.where(match, centre_cols[None, :], 0), axis=1) - half
+        return jnp.stack([position * tile_rows - tops, lefts]).astype(jnp.int32)
+
+    if planes != 4:
+        meta = image_meta(jnp.arange(count, dtype=jnp.int32))
+        partial = forward(meta, spectrum, pupil, band_table, 0, count)
+        mid = lax.psum_scatter(partial, "ty", scatter_dimension=0, tiled=True)[0]
+        back = lax.all_gather(middle([mid], measured, cos_table, sin_table), "ty")
+        return backward(meta, spectrum, pupil, band_table, list(range(count)), [back])
+
+    first = [(3, 2)]
+    second = [(3, 0), (2, 2), (2, 0)]
+    others = [(1, 2), (1, 0), (0, 2), (0, 0)]
     slots = {}
     for core in (1, 0):
-        for group in groups:
-            for j, y in group:
-                slots[j, y + core] = len(slots)
-    ids = [
-        [order[i // 4][j] * 4 + (i % 4 ^ flip) for (j, flip) in slots] for i in range(count)
-    ]
+        for j, y in first + second + others:
+            slots[j, y + core] = len(slots)
+    ids = [[((i // 4) ^ j) * 4 + (i % 4 ^ flip) for (j, flip) in slots] for i in range(count)]
     my_ids = lax.dynamic_index_in_dim(jnp.asarray(ids, jnp.int32), position, keepdims=False)
-    match = my_ids[:, None] == jnp.arange(count, dtype=jnp.int32)[None, :]
-    half = crop_width // 2
-    tops = jnp.sum(jnp.where(match, centre_rows[None, :], 0), axis=1) - half
-    lefts = jnp.sum(jnp.where(match, centre_cols[None, :], 0), axis=1) - half
-    meta = jnp.stack([position * tile_rows - tops, lefts]).astype(jnp.int32)
+    meta = image_meta(my_ids)
 
     def sibling(value):
         return lax.ppermute(value, "ty", [(i, i ^ 1) for i in range(count)])
@@ -381,91 +364,100 @@
     def across(value):
         return lax.ppermute(value, "ty", [(i, i ^ 2) for i in range(count)])
 
-    def along(value, sources, by):
-        pairs = [(4 * z + i, 4 * (z + by) + i) for z in sources for i in range(4)]
+    def along(value, plane_pairs):
+        pairs = [(4 * a + i, 4 * b + i) for a, b in plane_pairs for i in range(4)]
         return lax.ppermute(value, "ty", pairs)
 
-    def theirs(group, after):
-        known = meta if after is None else lax.optimization_barrier((meta, after))[0]
+    swap_one = [(0, 1), (1, 0), (2, 3), (3, 2)]
+    swap_two = [(0, 2), (1, 3), (2, 0), (3, 1)]
+    swap_middle = [(1, 2), (2, 1)]
+
+    def after(value, *earlier):
+        return lax.optimization_barrier((value,) + earlier)[0]
+
+    def theirs(group, known):
         j, y = group[0]
         return forward(known, spectrum, pupil, band_table, slots[j, y + 1], len(group))
 
-    def mine(group, came, after):
-        known = meta if after is None else lax.optimization_barrier((meta, after))[0]
+    def mine(group, known, came=None):
         j, y = group[0]
         return forward(known, spectrum, pupil, band_table, slots[j, y], len(group), came)
 
-    sent = theirs(first, None)
-    came_first = sibling(sent)
-    sent = theirs(second, sent)
+    sent = theirs(first, meta)
+    came_first = sibling(sent[0])
+    known = after(meta, sent)
+    own = mine(first, known)
+    received = {3: across(total(own[0], came_first))}
+    known = after(meta, own)
+    sent = theirs(second, known)
     came_second = sibling(sent)
-    (leaving,) = mine(first, came_first, sent)
-    received = {0: across(leaving)}
+    known = after(meta, sent)
+    sent = theirs(others, known)
+    came_others = sibling(sent)
+    known = after(meta, sent)
     kept = {}
-    sent = theirs(others, leaving)
-    came_others = sibling(sent)
-    made = mine(second, came_second, sent)
-    kept[0], leaving, kept[1] = made
-    received[1] = across(leaving)
-    made = mine(others, came_others, made[0])
-    for (j, y), value in zip(others, made):
-        if y:
-            received[j] = across(value)
-        else:
-            kept[j] = value
-
-    up = down = None
-    summed = []
-    for s in range(1, planes + 1):
-        summed.append(total(kept[s - 1], received[s - 1]))
-        if s == planes:
-            break
-        sources = [z for z in range(planes - 1) if z < s]
-        value = chosen(plane, {z: summed[order[z].index(planes - s + z)] for z in sources})
-        going_up = value if up is None else total(value, up)
-        sources_down = [z for z in range(1, planes) if planes - 1 - z < s]
-        value = chosen(plane, {z: summed[order[z].index(s - planes + z)] for z in sources_down})
-        going_down = value if down is None else total(value, down)
-        up, down = along(going_up, sources, 1), along(going_down, sources_down, -1)
-    band_back = middle(summed[-1], up, down, measured, cos_table, sin_table)
-
-    near = [list(reversed(row)) for row in order]
-    result = spectrum
-    from_below, from_above = [band_back], [band_back]
-    waiting = []
-    value, turned = band_back, None
-    for s in range(planes):
-        j = planes - 1 - s
-        new_slots, arrived = [slots[j, 0]], [value]
-        started = [across(value), sibling(value)]
-        next_slots = [slots[j, 2], slots[j, 1]]
-        if turned is not None:
-            started.append(sibling(turned))
-            next_slots.append(slots[j + 1, 3])
-        if s < planes - 1:
-            started.append(along(from_below[-1], range(s, planes - 1), 1))
-            started.append(along(from_above[-1], range(1, planes - s), -1))
-        waiting.append((slots[j, 0], value))
-        if s > 0:
-            result = backward(
-                meta, result, pupil, band_table, [k for k, _ in waiting], [v for _, v in waiting]
-            )
-            waiting = []
-        started = list(lax.optimization_barrier(tuple([result] + started)))
-        result, started = started[0], started[1:]
-        waiting += list(zip(next_slots, started))
-        turned = started[0]
-        if s < planes - 1:
-            from_below.append(started[-2])
-            from_above.append(started[-1])
-            options = {}
-            for z in range(planes):
-                q = near[z][s + 1]
-                options[z] = from_below[z - q] if q < z else from_above[q - z]
-            value = chosen(plane, options)
-    waiting.append((slots[0, 3], sibling(turned)))
-    return backward(
-        meta, result, pupil, band_table, [k for k, _ in waiting], [v for _, v in waiting]
+    kept[3], leaving, kept[2] = mine(second, known, came_second)
+    received[2] = across(leaving)
+    known = after(meta, leaving)
+    leaving_1, kept[1], leaving_0, kept[0] = mine(others, known, came_others)
+    received[1] = across(leaving_1)
+    received[0] = across(leaving_0)
+
+    far = total(kept[3], received[3])
+    far_from_end = along(far, [(0, 1), (3, 2)])
+    far_from_middle = along(far, swap_middle)
+    kept[2] = after(kept[2], leaving_1)
+    two = along(total(kept[2], received[2], far_from_end), swap_two)
+    one = along(total(kept[1], received[1]), swap_one)
+    terms = [kept[0], received[0], one, far_from_middle, two]
+    back = middle(terms, measured, cos_table, sin_table)
+
+    def apply(result, pieces):
+        names, values = zip(*pieces)
+        return backward(
+            meta, result, pupil, band_table, [slots[name] for name in names], list(values)
+        )
+
+    from_two = along(back, swap_two)
+    from_one = along(back, swap_one)
+    other = across(back)
+    twin = sibling(back)
+    from_one, other, twin = lax.optimization_barrier((from_one, other, twin))
+    other_one = across(from_one)
+    result = apply(
+        spectrum, [((0, 0), back), ((0, 1), twin), ((1, 0), from_one), ((0, 2), other)]
+    )
+    from_one, other = lax.optimization_barrier((from_one, other, result))[:2]
+    twin_one, twin_other = sibling(from_one), sibling(other)
+
+    from_two, other_one, twin_one, twin_other, result, back = lax.optimization_barrier(
+        (from_two, other_one, twin_one, twin_other, result, back)
+    )
+    from_end = along(from_two, [(1, 0), (2, 3)])
+    from_middle = along(back, swap_middle)
+    other_two = across(from_two)
+    result = apply(
+        result,
+        [((1, 1), twin_one), ((0, 3), twin_other), ((2, 0), from_two), ((1, 2), other_one)],
+    )
+    from_two, other_one = lax.optimization_barrier((from_two, other_one, result))[:2]
+    twin_two, twin_other = sibling(from_two), sibling(other_one)
+
+    from_end, from_middle, other_two, twin_two, twin_other, result = lax.optimization_barrier(
+        (from_end, from_middle, other_two, twin_two, twin_other, result)
+    )
+    from_three = jnp.where((plane == 0) | (plane == 3), from_end, from_middle)
+    other_three = across(from_three)
+    result = apply(
+        result,
+        [((2, 1), twin_two), ((1, 3), twin_other), ((3, 0), from_three), ((2, 2), other_two)],
+    )
+    from_three, other_two = lax.optimization_barrier((from_three, other_two, result))[:2]
+    twin_three, twin_other = sibling(from_three), sibling(other_two)
+    twin_last = sibling(other_three)
+    return apply(
+        result,
+        [((3, 1), twin_three), ((2, 3), twin_other), ((3, 2), other_three), ((3, 3), twin_last)],
     )
 
 

time: 307 us -> 340 us (1.11)
  waiting for transfers between devices: 126 us -> 176 us
  local copies, waits for them, and re-layouts: 7.27 us -> 1.67 us
    ppermute x12 -> x8, waiting for transfers between devices: 28.4 us -> 100 us  [along(): return lax.ppermute(value, 'ty', pairs)]
    ppermute x8, waiting for transfers between devices: 95.4 us -> 59.7 us  [across(): return lax.ppermute(value, 'ty', [(i, i ^ 2) for i in range(count)])]
    ppermute x11, waiting for transfers between devices: 2.31 us -> 15.4 us  [sibling(): return lax.ppermute(value, 'ty', [(i, i ^ 1) for i in range(count)])]
    ppermute x12 -> x8, starting transfers between devices: 31.3 us -> 23.1 us  [along(): return lax.ppermute(value, 'ty', pairs)]
    ppermute x11, starting transfers between devices: 14.3 us -> 21.3 us  [sibling(): return lax.ppermute(value, 'ty', [(i, i ^ 1) for i in range(count)])]
    unnamed x44 -> x12, local copies, waits for them, and re-layouts: 6.58 us -> 0.98 us
    convert_element_type x5 -> x4, other arithmetic: 11.6 us -> 8.47 us  [total(): sum((term.astype(jnp.float32) for term in terms)).astype(jnp.bfloat16)]
  transfers between devices with their start and end apart: 31 -> 27, of which waited for: 18 -> 17; matrix products, arithmetic and copies ran while one was open for 4% -> 2% of each run, Pallas kernels for 25% -> 16%
where the time goes in v4:
time: 340 us; the launch traced here: 339 us
  waiting for transfers between devices  176 us (52%)
  Pallas kernels  100 us (29%)
  starting transfers between devices  50.4 us (15%)
  other arithmetic  11 us (3%)
    ppermute x8, waiting for transfers between devices, along(): return lax.ppermute(value, 'ty', pairs)  100 us
    ppermute x8, waiting for transfers between devices, across(): return lax.ppermute(value, 'ty', [(i, i ^ 2) for i in range(count)])  59.7 us
    pallas_call x4, Pallas kernels, backward(): pl.pallas_call(functools.partial(backward_kernel, slots=slots, win=win),...  49.2 us
    pallas_call x6, Pallas kernels, forward(): pl.pallas_call(functools.partial(forward_kernel, base=base, win=win, addi...  38.6 us
    ppermute x8, starting transfers between devices, along(): return lax.ppermute(value, 'ty', pairs)  23.1 us
    ppermute x11, starting transfers between devices, sibling(): return lax.ppermute(value, 'ty', [(i, i ^ 1) for i in range(count)])  21.3 us
    ppermute x11, waiting for transfers between devices, sibling(): return lax.ppermute(value, 'ty', [(i, i ^ 1) for i in range(count)])  15.4 us
    pallas_call x1, Pallas kernels, middle(): pl.pallas_call(functools.partial(middle_kernel, terms=len(terms)), grid=(...  12.3 us
  transfers between devices with their start and end apart: 27, of which 17 were waited for; matrix products, arithmetic and copies ran while one was open for 2% of the time, Pallas kernels for 16%

profile of v4, /device:TPU:11, one launch (start us, length us, event | category | flops | bytes accessed | tf_op | source)
XLA Modules:
  0.0 339.1 jit_solution(10592547508886049704)
XLA Ops:
  0.0 0.7 dynamic-slice_bitcast_fusion
  0.7 0.9 select_reduce_fusion.1
  1.6 0.6 pad_add_fusion.meta_ref
  2.1 4.2 %forward.6 = bf16[1,2,256,1024]{3,2,1,0:T(8,128)(2,1)} custom-call(s32[2,16]{1,0:T(2,128)} %pad_add_fusion.meta_ref, f32[2,128,8192]{2,1,0:T(8,128)} %spec_ref.13, bf16[1024,1024]{1,0:T(8,128)(2,1)} %pupil_ref.19, bf16[1024,512]{1,0:T(8,128)(2,1)} %constant.41.clone.band_ref), custom_call_target="tpu_custom_call" | custom-call | flops 536870912 | bytes 3000000 | tf_op jit(solution)/shard_map/forward/pallas_call | solution.py:228
  6.3 3.2 forward.7
  9.6 6.0 %forward.8 = bf16[3,2,256,1024]{3,2,1,0:T(8,128)(2,1)} custom-call(s32[2,16]{1,0:T(2,128)} %pad_add_fusion.meta_ref, f32[2,128,8192]{2,1,0:T(8,128)} %spec_ref.13, bf16[1024,1024]{1,0:T(8,128)(2,1)} %pupil_ref.19, bf16[1024,512]{1,0:T(8,128)(2,1)} %constant.41.clone.band_ref), custom_call_target="tpu_custom_call" | custom-call | flops 1610612736 | bytes 9000000 | tf_op jit(solution)/shard_map/forward/pallas_call | solution.py:228
  15.6 7.5 %forward.9 = bf16[4,2,256,1024]{3,2,1,0:T(8,128)(2,1)} custom-call(s32[2,16]{1,0:T(2,128)} %pad_add_fusion.meta_ref, f32[2,128,8192]{2,1,0:T(8,128)} %spec_ref.13, bf16[1024,1024]{1,0:T(8,128)(2,1)} %pupil_ref.19, bf16[1024,512]{1,0:T(8,128)(2,1)} %constant.41.clone.band_ref), custom_call_target="tpu_custom_call" | custom-call | flops 2147483648 | bytes 12000000 | tf_op jit(solution)/shard_map/forward/pallas_call | solution.py:228
  23.1 2.1 collective-permute-start.1
  25.2 0.0 collective-permute-start
  25.2 0.5 collective-permute-start.5
  25.8 8.6 %collective-permute-done.5 = bf16[2,256,1024]{2,1,0:T(8,128)(2,1)S(1)} collective-permute-done((bf16[2,256,1024]{2,1,0:T(8,128)(2,1)}, bf16[2,256,1024]{2,1,0:T(8,128)(2,1)S(1)}, u32[]{:S(2)}, u32[]{:S(2)}) %collective-permute-start.5) | collective-permute-done | bytes 1048608 | tf_op jit(solution)/shard_map/ppermute | solution.py:362
  34.3 2.6 fusion
  37.0 2.6 collective-permute-start.6
  39.6 8.3 %forward.10 = (bf16[2,256,1024]{2,1,0:T(8,128)(2,1)}, bf16[2,256,1024]{2,1,0:T(8,128)(2,1)}, bf16[2,256,1024]{2,1,0:T(8,128)(2,1)}) custom-call(s32[2,16]{1,0:T(2,128)} %pad_add_fusion.meta_ref, f32[2,128,8192]{2,1,0:T(8,128)} %spec_ref.13, bf16[1024,1024]{1,0:T(8,128)(2,1)} %pupil_ref.19, bf16[1024,512]{1,0:T(8,128)(2,1)} %constant.41.clone.band_ref, ...), custom_call_target="tpu_custom_call" | custom-call | flops 1610612736 | bytes 9000000 | tf_op jit(solution)/shard_map/forward/pallas_call | solution.py:228
  47.9 15.2 %collective-permute-done.6 = bf16[2,256,1024]{2,1,0:T(8,128)(2,1)} collective-permute-done((bf16[2,256,1024]{2,1,0:T(8,128)(2,1)}, bf16[2,256,1024]{2,1,0:T(8,128)(2,1)}, u32[]{:S(2)}, u32[]{:S(2)}) %collective-permute-start.6) | collective-permute-done | bytes 1048608 | tf_op jit(solution)/shard_map/ppermute | solution.py:365
  63.1 3.0 add_convert_fusion.1
  66.1 1.3 collective-permute-start.9
  67.4 1.2 collective-permute-start.8
  68.6 9.4 %forward.11 = (bf16[2,256,1024]{2,1,0:T(8,128)(2,1)}, bf16[2,256,1024]{2,1,0:T(8,128)(2,1)}, bf16[2,256,1024]{2,1,0:T(8,128)(2,1)}, bf16[2,256,1024]{2,1,0:T(8,128)(2,1)}) custom-call(s32[2,16]{1,0:T(2,128)} %pad_add_fusion.meta_ref, f32[2,128,8192]{2,1,0:T(8,128)} %spec_ref.13, bf16[1024,1024]{1,0:T(8,128)(2,1)} %pupil_ref.19, ...), custom_call_target="tpu_custom_call" | custom-call | flops 2147483648 | bytes 12000000 | tf_op jit(solution)/shard_map/forward/pallas_call | solution.py:228
  78.0 0.9 collective-permute-start.3
  78.9 3.8 %collective-permute-start.7 = (bf16[2,256,1024]{2,1,0:T(8,128)(2,1)}, bf16[2,256,1024]{2,1,0:T(8,128)(2,1)S(1)}, u32[]{:S(2)}, u32[]{:S(2)}) collective-permute-start(bf16[2,256,1024]{2,1,0:T(8,128)(2,1)} %add_convert_fusion.1), channel_id=1, source_target_pairs={{4,8},{5,9},{6,10},{7,11},{8,4},{9,5},{10,6},{11,7},{20,24},{21,25... | collective-permute-start | bytes 3145736 | tf_op jit(solution)/shard_map/ppermute | solution.py:369
  82.7 9.4 %collective-permute-done.9 = bf16[2,256,1024]{2,1,0:T(8,128)(2,1)} collective-permute-done((bf16[2,256,1024]{2,1,0:T(8,128)(2,1)}, bf16[2,256,1024]{2,1,0:T(8,128)(2,1)}, u32[]{:S(2)}, u32[]{:S(2)}) %collective-permute-start.9) | collective-permute-done | bytes 1048608 | tf_op jit(solution)/shard_map/ppermute | solution.py:369
  92.1 2.5 add_convert_fusion
  94.6 4.0 %collective-permute-start.10 = (bf16[2,256,1024]{2,1,0:T(8,128)(2,1)S(1)}, bf16[2,256,1024]{2,1,0:T(8,128)(2,1)S(1)}, u32[]{:S(2)}, u32[]{:S(2)}) collective-permute-start(bf16[2,256,1024]{2,1,0:T(8,128)(2,1)S(1)} %add_convert_fusion), channel_id=1, source_target_pairs={{0,8},{1,9},{2,10},{3,11},{4,12},{5,13},{6,14},{7,15},{8,0},{9,1},... | collective-permute-start | bytes 3145736 | tf_op jit(solution)/shard_map/ppermute | solution.py:369
  98.6 0.8 collective-permute-start.2
  99.4 14.5 %collective-permute-done.3 = bf16[2,256,1024]{2,1,0:T(8,128)(2,1)S(1)} collective-permute-done((bf16[2,256,1024]{2,1,0:T(8,128)(2,1)}, bf16[2,256,1024]{2,1,0:T(8,128)(2,1)S(1)}, u32[]{:S(2)}, u32[]{:S(2)}) %collective-permute-start.3) | collective-permute-done | bytes 1048608 | tf_op jit(solution)/shard_map/ppermute | solution.py:365
  113.9 0.4 add_convert_fusion.2
  114.4 2.8 collective-permute-start.4
  117.1 9.8 %collective-permute-done.7.refs_3_ = bf16[2,256,1024]{2,1,0:T(8,128)(2,1)S(1)} collective-permute-done((bf16[2,256,1024]{2,1,0:T(8,128)(2,1)}, bf16[2,256,1024]{2,1,0:T(8,128)(2,1)S(1)}, u32[]{:S(2)}, u32[]{:S(2)}) %collective-permute-start.7) | collective-permute-done | bytes 1048608 | tf_op jit(solution)/shard_map/ppermute | solution.py:369
  126.9 21.5 %collective-permute-done.10.refs_4_ = bf16[2,256,1024]{2,1,0:T(8,128)(2,1)S(1)} collective-permute-done((bf16[2,256,1024]{2,1,0:T(8,128)(2,1)S(1)}, bf16[2,256,1024]{2,1,0:T(8,128)(2,1)S(1)}, u32[]{:S(2)}, u32[]{:S(2)}) %collective-permute-start.10) | collective-permute-done | bytes 1048608 | tf_op jit(solution)/shard_map/ppermute | solution.py:369
  148.4 9.8 %collective-permute-done.4.refs_2_ = bf16[2,256,1024]{2,1,0:T(8,128)(2,1)S(1)} collective-permute-done((bf16[2,256,1024]{2,1,0:T(8,128)(2,1)S(1)}, bf16[2,256,1024]{2,1,0:T(8,128)(2,1)S(1)}, u32[]{:S(2)}, u32[]{:S(2)}) %collective-permute-start.4) | collective-permute-done | bytes 1048608 | tf_op jit(solution)/shard_map/ppermute | solution.py:369
  158.3 1.0 copy-done.5
  159.2 12.3 %middle.1.refs_0_ = bf16[2,256,1024]{2,1,0:T(8,128)(2,1)} custom-call(bf16[2,256,1024]{2,1,0:T(8,128)(2,1)} %get-tuple-element.45.refs_0_, bf16[2,256,1024]{2,1,0:T(8,128)(2,1)} %copy-done.4, bf16[2,256,1024]{2,1,0:T(8,128)(2,1)} %copy-done.5, bf16[2,256,1024]{2,1,0:T(8,128)(2,1)} %copy-done.1, bf16[2,256,1024]{2,1,0:T(8,128)(2,1)} %copy-done.3, ...), custom_call_target="tpu_custom_call" | custom-call | flops 4294967296 | bytes 15728640 | tf_op jit(solution)/shard_map/middle/pallas_call | solution.py:293
  171.5 2.2 collective-permute-start.12
  173.7 0.2 collective-permute-start.13
  173.9 5.9 %collective-permute-start.14 = (bf16[2,256,1024]{2,1,0:T(8,128)(2,1)}, bf16[2,256,1024]{2,1,0:T(8,128)(2,1)}, u32[]{:S(2)}, u32[]{:S(2)}) collective-permute-start(bf16[2,256,1024]{2,1,0:T(8,128)(2,1)} %middle.1.refs_0_), channel_id=1, source_target_pairs={{0,1},{1,0},{2,3},{3,2},{4,5},{5,4},{6,7},{7,6},{8,9},{9,8},{10,11... | collective-permute-start | bytes 3145736 | tf_op jit(solution)/shard_map/ppermute | solution.py:362
  179.8 1.5 collective-permute-start.11
  181.3 26.7 %collective-permute-done.12.refs_2_ = bf16[2,256,1024]{2,1,0:T(8,128)(2,1)} collective-permute-done((bf16[2,256,1024]{2,1,0:T(8,128)(2,1)}, bf16[2,256,1024]{2,1,0:T(8,128)(2,1)}, u32[]{:S(2)}, u32[]{:S(2)}) %collective-permute-start.12) | collective-permute-done | bytes 1048608 | tf_op jit(solution)/shard_map/ppermute | solution.py:369
  208.0 12.2 %backward.4.spec_ref = f32[2,128,8192]{2,1,0:T(8,128)} custom-call(s32[2,16]{1,0:T(2,128)} %pad_add_fusion.meta_ref, f32[2,128,8192]{2,1,0:T(8,128)} %spec_ref.13, bf16[1024,1024]{1,0:T(8,128)(2,1)} %pupil_ref.19, bf16[1024,512]{1,0:T(8,128)(2,1)} %constant.41.clone.band_ref, bf16[2,256,1024]{2,1,0:T(8,128)(2,1)} %middle.1.refs_0_, ...), custom_call_target="tpu_custom_call" | custom-call | flops 2147483648 | bytes 28777216 | tf_op jit(solution)/shard_map/backward/pallas_call | solution.py:261
  220.2 6.4 %collective-permute-start.16 = (bf16[2,256,1024]{2,1,0:T(8,128)(2,1)}, bf16[2,256,1024]{2,1,0:T(8,128)(2,1)}, u32[]{:S(2)}, u32[]{:S(2)}) collective-permute-start(bf16[2,256,1024]{2,1,0:T(8,128)(2,1)} %collective-permute-done.12.refs_2_), channel_id=1, source_target_pairs={{0,1},{1,0},{2,3},{3,2},{4,5},{5,4},{6,7},{7,6},{8,9},{9,8},{10,11... | collective-permute-start | bytes 3145736 | tf_op jit(solution)/shard_map/ppermute | solution.py:362
  226.6 0.1 collective-permute-start.17
  226.7 0.0 collective-permute-done.11.refs_2_
  226.7 2.5 collective-permute-done.16.refs_0_
  229.2 1.5 collective-permute-done.17.refs_1_
  230.7 20.6 %collective-permute-done.15.refs_3_ = bf16[2,256,1024]{2,1,0:T(8,128)(2,1)} collective-permute-done((bf16[2,256,1024]{2,1,0:T(8,128)(2,1)}, bf16[2,256,1024]{2,1,0:T(8,128)(2,1)}, u32[]{:S(2)}, u32[]{:S(2)}) %collective-permute-start.15) | collective-permute-done | bytes 1048608 | tf_op jit(solution)/shard_map/ppermute | solution.py:365
  251.3 3.9 %collective-permute-start.18 = (bf16[2,256,1024]{2,1,0:T(8,128)(2,1)}, bf16[2,256,1024]{2,1,0:T(8,128)(2,1)}, u32[]{:S(2)}, u32[]{:S(2)}) collective-permute-start(bf16[2,256,1024]{2,1,0:T(8,128)(2,1)} %collective-permute-done.11.refs_2_), channel_id=1, source_target_pairs={{4,0},{5,1},{6,2},{7,3},{8,12},{9,13},{10,14},{11,15},{20,16},{21,... | collective-permute-start | bytes 3145736 | tf_op jit(solution)/shard_map/ppermute | solution.py:369
  255.2 12.1 %backward.5.spec_ref = f32[2,128,8192]{2,1,0:T(8,128)} custom-call(s32[2,16]{1,0:T(2,128)} %pad_add_fusion.meta_ref, f32[2,128,8192]{2,1,0:T(8,128)} %backward.4.spec_ref, bf16[1024,1024]{1,0:T(8,128)(2,1)} %pupil_ref.19, bf16[1024,512]{1,0:T(8,128)(2,1)} %constant.41.clone.band_ref, bf16[2,256,1024]{2,1,0:T(8,128)(2,1)} %collective-permute-done.16.refs_0_, ...), custom_call_target="tpu_custom_call" | custom-call | flops 2147483648 | bytes 28777216 | tf_op jit(solution)/shard_map/backward/pallas_call | solution.py:261
  267.3 0.9 collective-permute-start.21
  268.2 0.1 collective-permute-start.22
  268.2 3.7 %collective-permute-start.19 = (bf16[2,256,1024]{2,1,0:T(8,128)(2,1)}, bf16[2,256,1024]{2,1,0:T(8,128)(2,1)S(1)}, u32[]{:S(2)}, u32[]{:S(2)}) collective-permute-start(bf16[2,256,1024]{2,1,0:T(8,128)(2,1)} %middle.1.refs_0_), channel_id=1, source_target_pairs={{4,8},{5,9},{6,10},{7,11},{8,4},{9,5},{10,6},{11,7},{20,24},{21,25... | collective-permute-start | bytes 3145736 | tf_op jit(solution)/shard_map/ppermute | solution.py:369
  272.0 0.1 collective-permute-start.20
  272.1 0.2 collective-permute-done.22.refs_1_
  272.3 3.4 %collective-permute-done.18 = bf16[2,256,1024]{2,1,0:T(8,128)(2,1)} collective-permute-done((bf16[2,256,1024]{2,1,0:T(8,128)(2,1)}, bf16[2,256,1024]{2,1,0:T(8,128)(2,1)}, u32[]{:S(2)}, u32[]{:S(2)}) %collective-permute-start.18) | collective-permute-done | bytes 1048608 | tf_op jit(solution)/shard_map/ppermute | solution.py:369
  275.7 19.7 %collective-permute-done.19 = bf16[2,256,1024]{2,1,0:T(8,128)(2,1)S(1)} collective-permute-done((bf16[2,256,1024]{2,1,0:T(8,128)(2,1)}, bf16[2,256,1024]{2,1,0:T(8,128)(2,1)S(1)}, u32[]{:S(2)}, u32[]{:S(2)}) %collective-permute-start.19) | collective-permute-done | bytes 1048608 | tf_op jit(solution)/shard_map/ppermute | solution.py:369
  295.4 0.9 collective-permute-done.20.refs_3_
  296.3 1.1 broadcast_select_fusion.refs_2_
  297.4 0.1 collective-permute-start.25
  297.5 12.0 %backward.6.spec_ref = f32[2,128,8192]{2,1,0:T(8,128)} custom-call(s32[2,16]{1,0:T(2,128)} %pad_add_fusion.meta_ref, f32[2,128,8192]{2,1,0:T(8,128)} %backward.5.spec_ref, bf16[1024,1024]{1,0:T(8,128)(2,1)} %pupil_ref.19, bf16[1024,512]{1,0:T(8,128)(2,1)} %constant.41.clone.band_ref, bf16[2,256,1024]{2,1,0:T(8,128)(2,1)} %collective-permute-done.21.refs_0_, ...), custom_call_target="tpu_custom_call" | custom-call | flops 2147483648 | bytes 28777216 | tf_op jit(solution)/shard_map/backward/pallas_call | solution.py:261
  309.5 2.7 collective-permute-start.23
  312.2 0.1 collective-permute-start.24
  312.3 8.5 %collective-permute-done.25.refs_2_ = bf16[2,256,1024]{2,1,0:T(8,128)(2,1)} collective-permute-done((bf16[2,256,1024]{2,1,0:T(8,128)(2,1)}, bf16[2,256,1024]{2,1,0:T(8,128)(2,1)}, u32[]{:S(2)}, u32[]{:S(2)}) %collective-permute-start.25) | collective-permute-done | bytes 1048608 | tf_op jit(solution)/shard_map/ppermute | solution.py:365
  320.8 2.5 collective-permute-start.26
  323.3 2.6 collective-permute-done.26.refs_3_
  325.9 13.0 %backward.7 = f32[2,128,8192]{2,1,0:T(8,128)} custom-call(s32[2,16]{1,0:T(2,128)} %pad_add_fusion.meta_ref, f32[2,128,8192]{2,1,0:T(8,128)} %backward.6.spec_ref, bf16[1024,1024]{1,0:T(8,128)(2,1)} %pupil_ref.19, bf16[1024,512]{1,0:T(8,128)(2,1)} %constant.41.clone.band_ref, bf16[2,256,1024]{2,1,0:T(8,128)(2,1)} %collective-permute-done.23.refs_0_, ...), custom_call_target="tpu_custom_call" | custom-call | flops 2147483648 | bytes 28777216 | tf_op jit(solution)/shard_map/backward/pallas_call | solution.py:261
  (22 shorter events, 0.1 us)
Async XLA Ops:
  23.1 45.5 %collective-permute-start.1 = (bf16[4,2,256,1024]{3,2,1,0:T(8,128)(2,1)}, bf16[4,2,256,1024]{3,2,1,0:T(8,128)(2,1)}, u32[]{:S(2)}, u32[]{:S(2)}) collective-permute-start(bf16[4,2,256,1024]{3,2,1,0:T(8,128)(2,1)} %forward.9), channel_id=1, source_target_pairs={{0,1},{1,0},{2,3},{3,2},{4,5},{5,4},{6,7},{7,6},{8,9},{9,8},{10,11... | collective-permute-start | bytes 12582920 | tf_op jit(solution)/shard_map/ppermute | solution.py:362
  25.2 14.4 %collective-permute-start = (bf16[3,2,256,1024]{3,2,1,0:T(8,128)(2,1)}, bf16[3,2,256,1024]{3,2,1,0:T(8,128)(2,1)}, u32[]{:S(2)}, u32[]{:S(2)}) collective-permute-start(bf16[3,2,256,1024]{3,2,1,0:T(8,128)(2,1)} %forward.8), channel_id=1, source_target_pairs={{0,1},{1,0},{2,3},{3,2},{4,5},{5,4},{6,7},{7,6},{8,9},{9,8},{10,11... | collective-permute-start | bytes 9437192 | tf_op jit(solution)/shard_map/ppermute | solution.py:362
  25.2 9.1 %collective-permute-start.5 = (bf16[2,256,1024]{2,1,0:T(8,128)(2,1)}, bf16[2,256,1024]{2,1,0:T(8,128)(2,1)S(1)}, u32[]{:S(2)}, u32[]{:S(2)}) collective-permute-start(bf16[2,256,1024]{2,1,0:T(8,128)(2,1)} %bitcast.10), channel_id=1, source_target_pairs={{0,1},{1,0},{2,3},{3,2},{4,5},{5,4},{6,7},{7,6},{8,9},{9,8},{10,11... | collective-permute-start | bytes 3145736 | tf_op jit(solution)/shard_map/ppermute | solution.py:362
  37.0 26.2 %collective-permute-start.6 = (bf16[2,256,1024]{2,1,0:T(8,128)(2,1)}, bf16[2,256,1024]{2,1,0:T(8,128)(2,1)}, u32[]{:S(2)}, u32[]{:S(2)}) collective-permute-start(bf16[2,256,1024]{2,1,0:T(8,128)(2,1)} %fusion), channel_id=1, source_target_pairs={{0,2},{1,3},{2,0},{3,1},{4,6},{5,7},{6,4},{7,5},{8,10},{9,11},{10,... | collective-permute-start | bytes 3145736 | tf_op jit(solution)/shard_map/ppermute | solution.py:365
  66.1 26.0 %collective-permute-start.9 = (bf16[2,256,1024]{2,1,0:T(8,128)(2,1)}, bf16[2,256,1024]{2,1,0:T(8,128)(2,1)}, u32[]{:S(2)}, u32[]{:S(2)}) collective-permute-start(bf16[2,256,1024]{2,1,0:T(8,128)(2,1)} %add_convert_fusion.1), channel_id=1, source_target_pairs={{0,4},{1,5},{2,6},{3,7},{12,8},{13,9},{14,10},{15,11},{16,20},{17,... | collective-permute-start | bytes 3145736 | tf_op jit(solution)/shard_map/ppermute | solution.py:369
  67.4 24.7 %collective-permute-start.8 = (bf16[2,256,1024]{2,1,0:T(8,128)(2,1)}, bf16[2,256,1024]{2,1,0:T(8,128)(2,1)}, u32[]{:S(2)}, u32[]{:S(2)}) collective-permute-start(bf16[2,256,1024]{2,1,0:T(8,128)(2,1)} %get-tuple-element.43), channel_id=1, source_target_pairs={{0,2},{1,3},{2,0},{3,1},{4,6},{5,7},{6,4},{7,5},{8,10},{9,11},{10,... | collective-permute-start | bytes 3145736 | tf_op jit(solution)/shard_map/ppermute | solution.py:365
  78.0 35.9 %collective-permute-start.3 = (bf16[2,256,1024]{2,1,0:T(8,128)(2,1)}, bf16[2,256,1024]{2,1,0:T(8,128)(2,1)S(1)}, u32[]{:S(2)}, u32[]{:S(2)}) collective-permute-start(bf16[2,256,1024]{2,1,0:T(8,128)(2,1)} %get-tuple-element.48), channel_id=1, source_target_pairs={{0,2},{1,3},{2,0},{3,1},{4,6},{5,7},{6,4},{7,5},{8,10},{9,11},{10,... | collective-permute-start | bytes 3145736 | tf_op jit(solution)/shard_map/ppermute | solution.py:365
  78.9 48.0 %collective-permute-start.7 = (bf16[2,256,1024]{2,1,0:T(8,128)(2,1)}, bf16[2,256,1024]{2,1,0:T(8,128)(2,1)S(1)}, u32[]{:S(2)}, u32[]{:S(2)}) collective-permute-start(bf16[2,256,1024]{2,1,0:T(8,128)(2,1)} %add_convert_fusion.1), channel_id=1, source_target_pairs={{4,8},{5,9},{6,10},{7,11},{8,4},{9,5},{10,6},{11,7},{20,24},{21,25... | collective-permute-start | bytes 3145736 | tf_op jit(solution)/shard_map/ppermute | solution.py:369
  82.7 15.8 %copy-start.2 = (bf16[2,256,1024]{2,1,0:T(8,128)(2,1)S(1)}, bf16[2,256,1024]{2,1,0:T(8,128)(2,1)}, u32[]{:S(2)}) copy-start(bf16[2,256,1024]{2,1,0:T(8,128)(2,1)} %get-tuple-element.46) | copy-start | bytes 3145732
  82.7 31.2 %copy-start = (bf16[2,256,1024]{2,1,0:T(8,128)(2,1)S(1)}, bf16[2,256,1024]{2,1,0:T(8,128)(2,1)}, u32[]{:S(2)}) copy-start(bf16[2,256,1024]{2,1,0:T(8,128)(2,1)} %get-tuple-element.47) | copy-start | bytes 3145732
  94.6 53.8 %collective-permute-start.10 = (bf16[2,256,1024]{2,1,0:T(8,128)(2,1)S(1)}, bf16[2,256,1024]{2,1,0:T(8,128)(2,1)S(1)}, u32[]{:S(2)}, u32[]{:S(2)}) collective-permute-start(bf16[2,256,1024]{2,1,0:T(8,128)(2,1)S(1)} %add_convert_fusion), channel_id=1, source_target_pairs={{0,8},{1,9},{2,10},{3,11},{4,12},{5,13},{6,14},{7,15},{8,0},{9,1},... | collective-permute-start | bytes 3145736 | tf_op jit(solution)/shard_map/ppermute | solution.py:369
  98.6 49.9 %collective-permute-start.2 = (bf16[2,256,1024]{2,1,0:T(8,128)(2,1)S(1)}, bf16[2,256,1024]{2,1,0:T(8,128)(2,1)S(1)}, u32[]{:S(2)}, u32[]{:S(2)}) collective-permute-start(bf16[2,256,1024]{2,1,0:T(8,128)(2,1)S(1)} %copy-done.2), channel_id=1, source_target_pairs={{0,2},{1,3},{2,0},{3,1},{4,6},{5,7},{6,4},{7,5},{8,10},{9,11},{10,... | collective-permute-start | bytes 3145736 | tf_op jit(solution)/shard_map/ppermute | solution.py:365
  114.4 43.9 %collective-permute-start.4 = (bf16[2,256,1024]{2,1,0:T(8,128)(2,1)S(1)}, bf16[2,256,1024]{2,1,0:T(8,128)(2,1)S(1)}, u32[]{:S(2)}, u32[]{:S(2)}) collective-permute-start(bf16[2,256,1024]{2,1,0:T(8,128)(2,1)S(1)} %add_convert_fusion.2), channel_id=1, source_target_pairs={{0,4},{1,5},{2,6},{3,7},{4,0},{5,1},{6,2},{7,3},{8,12},{9,13},{10,... | collective-permute-start | bytes 3145736 | tf_op jit(solution)/shard_map/ppermute | solution.py:369
  126.9 31.3 %copy-start.1 = (bf16[2,256,1024]{2,1,0:T(8,128)(2,1)}, bf16[2,256,1024]{2,1,0:T(8,128)(2,1)S(1)}, u32[]{:S(2)}) copy-start(bf16[2,256,1024]{2,1,0:T(8,128)(2,1)S(1)} %collective-permute-done.7.refs_3_) | copy-start | bytes 3145732
  148.4 9.8 %copy-start.3 = (bf16[2,256,1024]{2,1,0:T(8,128)(2,1)}, bf16[2,256,1024]{2,1,0:T(8,128)(2,1)S(1)}, u32[]{:S(2)}) copy-start(bf16[2,256,1024]{2,1,0:T(8,128)(2,1)S(1)} %collective-permute-done.10.refs_4_) | copy-start | bytes 3145732
  148.4 9.8 %copy-start.4 = (bf16[2,256,1024]{2,1,0:T(8,128)(2,1)}, bf16[2,256,1024]{2,1,0:T(8,128)(2,1)S(1)}, u32[]{:S(2)}) copy-start(bf16[2,256,1024]{2,1,0:T(8,128)(2,1)S(1)} %collective-permute-done.2.refs_1_) | copy-start | bytes 3145732
  158.3 1.0 copy-start.5
  171.5 36.4 %collective-permute-start.12 = (bf16[2,256,1024]{2,1,0:T(8,128)(2,1)}, bf16[2,256,1024]{2,1,0:T(8,128)(2,1)}, u32[]{:S(2)}, u32[]{:S(2)}) collective-permute-start(bf16[2,256,1024]{2,1,0:T(8,128)(2,1)} %middle.1.refs_0_), channel_id=1, source_target_pairs={{0,4},{1,5},{2,6},{3,7},{4,0},{5,1},{6,2},{7,3},{8,12},{9,13},{10,... | collective-permute-start | bytes 3145736 | tf_op jit(solution)/shard_map/ppermute | solution.py:369
  173.7 34.2 %collective-permute-start.13 = (bf16[2,256,1024]{2,1,0:T(8,128)(2,1)}, bf16[2,256,1024]{2,1,0:T(8,128)(2,1)}, u32[]{:S(2)}, u32[]{:S(2)}) collective-permute-start(bf16[2,256,1024]{2,1,0:T(8,128)(2,1)} %middle.1.refs_0_), channel_id=1, source_target_pairs={{0,2},{1,3},{2,0},{3,1},{4,6},{5,7},{6,4},{7,5},{8,10},{9,11},{10,... | collective-permute-start | bytes 3145736 | tf_op jit(solution)/shard_map/ppermute | solution.py:365
  173.9 34.1 %collective-permute-start.14 = (bf16[2,256,1024]{2,1,0:T(8,128)(2,1)}, bf16[2,256,1024]{2,1,0:T(8,128)(2,1)}, u32[]{:S(2)}, u32[]{:S(2)}) collective-permute-start(bf16[2,256,1024]{2,1,0:T(8,128)(2,1)} %middle.1.refs_0_), channel_id=1, source_target_pairs={{0,1},{1,0},{2,3},{3,2},{4,5},{5,4},{6,7},{7,6},{8,9},{9,8},{10,11... | collective-permute-start | bytes 3145736 | tf_op jit(solution)/shard_map/ppermute | solution.py:362
  179.8 46.9 %collective-permute-start.11 = (bf16[2,256,1024]{2,1,0:T(8,128)(2,1)}, bf16[2,256,1024]{2,1,0:T(8,128)(2,1)}, u32[]{:S(2)}, u32[]{:S(2)}) collective-permute-start(bf16[2,256,1024]{2,1,0:T(8,128)(2,1)} %middle.1.refs_0_), channel_id=1, source_target_pairs={{0,8},{1,9},{2,10},{3,11},{4,12},{5,13},{6,14},{7,15},{8,0},{9,1},... | collective-permute-start | bytes 3145736 | tf_op jit(solution)/shard_map/ppermute | solution.py:369
  220.2 9.0 %collective-permute-start.16 = (bf16[2,256,1024]{2,1,0:T(8,128)(2,1)}, bf16[2,256,1024]{2,1,0:T(8,128)(2,1)}, u32[]{:S(2)}, u32[]{:S(2)}) collective-permute-start(bf16[2,256,1024]{2,1,0:T(8,128)(2,1)} %collective-permute-done.12.refs_2_), channel_id=1, source_target_pairs={{0,1},{1,0},{2,3},{3,2},{4,5},{5,4},{6,7},{7,6},{8,9},{9,8},{10,11... | collective-permute-start | bytes 3145736 | tf_op jit(solution)/shard_map/ppermute | solution.py:362
  226.6 4.1 %collective-permute-start.17 = (bf16[2,256,1024]{2,1,0:T(8,128)(2,1)}, bf16[2,256,1024]{2,1,0:T(8,128)(2,1)}, u32[]{:S(2)}, u32[]{:S(2)}) collective-permute-start(bf16[2,256,1024]{2,1,0:T(8,128)(2,1)} %collective-permute-done.13.refs_3_), channel_id=1, source_target_pairs={{0,1},{1,0},{2,3},{3,2},{4,5},{5,4},{6,7},{7,6},{8,9},{9,8},{10,11... | collective-permute-start | bytes 3145736 | tf_op jit(solution)/shard_map/ppermute | solution.py:362
  226.7 24.6 %collective-permute-start.15 = (bf16[2,256,1024]{2,1,0:T(8,128)(2,1)}, bf16[2,256,1024]{2,1,0:T(8,128)(2,1)}, u32[]{:S(2)}, u32[]{:S(2)}) collective-permute-start(bf16[2,256,1024]{2,1,0:T(8,128)(2,1)} %collective-permute-done.12.refs_2_), channel_id=1, source_target_pairs={{0,2},{1,3},{2,0},{3,1},{4,6},{5,7},{6,4},{7,5},{8,10},{9,11},{10,... | collective-permute-start | bytes 3145736 | tf_op jit(solution)/shard_map/ppermute | solution.py:365
  251.3 24.4 %collective-permute-start.18 = (bf16[2,256,1024]{2,1,0:T(8,128)(2,1)}, bf16[2,256,1024]{2,1,0:T(8,128)(2,1)}, u32[]{:S(2)}, u32[]{:S(2)}) collective-permute-start(bf16[2,256,1024]{2,1,0:T(8,128)(2,1)} %collective-permute-done.11.refs_2_), channel_id=1, source_target_pairs={{4,0},{5,1},{6,2},{7,3},{8,12},{9,13},{10,14},{11,15},{20,16},{21,... | collective-permute-start | bytes 3145736 | tf_op jit(solution)/shard_map/ppermute | solution.py:369
  267.3 4.8 %collective-permute-start.21 = (bf16[2,256,1024]{2,1,0:T(8,128)(2,1)}, bf16[2,256,1024]{2,1,0:T(8,128)(2,1)}, u32[]{:S(2)}, u32[]{:S(2)}) collective-permute-start(bf16[2,256,1024]{2,1,0:T(8,128)(2,1)} %collective-permute-done.11.refs_2_), channel_id=1, source_target_pairs={{0,1},{1,0},{2,3},{3,2},{4,5},{5,4},{6,7},{7,6},{8,9},{9,8},{10,11... | collective-permute-start | bytes 3145736 | tf_op jit(solution)/shard_map/ppermute | solution.py:362
  268.2 4.1 %collective-permute-start.22 = (bf16[2,256,1024]{2,1,0:T(8,128)(2,1)}, bf16[2,256,1024]{2,1,0:T(8,128)(2,1)}, u32[]{:S(2)}, u32[]{:S(2)}) collective-permute-start(bf16[2,256,1024]{2,1,0:T(8,128)(2,1)} %collective-permute-done.15.refs_3_), channel_id=1, source_target_pairs={{0,1},{1,0},{2,3},{3,2},{4,5},{5,4},{6,7},{7,6},{8,9},{9,8},{10,11... | collective-permute-start | bytes 3145736 | tf_op jit(solution)/shard_map/ppermute | solution.py:362
  268.2 27.2 %collective-permute-start.19 = (bf16[2,256,1024]{2,1,0:T(8,128)(2,1)}, bf16[2,256,1024]{2,1,0:T(8,128)(2,1)S(1)}, u32[]{:S(2)}, u32[]{:S(2)}) collective-permute-start(bf16[2,256,1024]{2,1,0:T(8,128)(2,1)} %middle.1.refs_0_), channel_id=1, source_target_pairs={{4,8},{5,9},{6,10},{7,11},{8,4},{9,5},{10,6},{11,7},{20,24},{21,25... | collective-permute-start | bytes 3145736 | tf_op jit(solution)/shard_map/ppermute | solution.py:369
  272.0 24.4 %collective-permute-start.20 = (bf16[2,256,1024]{2,1,0:T(8,128)(2,1)}, bf16[2,256,1024]{2,1,0:T(8,128)(2,1)}, u32[]{:S(2)}, u32[]{:S(2)}) collective-permute-start(bf16[2,256,1024]{2,1,0:T(8,128)(2,1)} %collective-permute-done.11.refs_2_), channel_id=1, source_target_pairs={{0,2},{1,3},{2,0},{3,1},{4,6},{5,7},{6,4},{7,5},{8,10},{9,11},{10,... | collective-permute-start | bytes 3145736 | tf_op jit(solution)/shard_map/ppermute | solution.py:365
  297.4 23.4 %collective-permute-start.25 = (bf16[2,256,1024]{2,1,0:T(8,128)(2,1)}, bf16[2,256,1024]{2,1,0:T(8,128)(2,1)}, u32[]{:S(2)}, u32[]{:S(2)}) collective-permute-start(bf16[2,256,1024]{2,1,0:T(8,128)(2,1)} %broadcast_select_fusion.refs_2_), channel_id=1, source_target_pairs={{0,2},{1,3},{2,0},{3,1},{4,6},{5,7},{6,4},{7,5},{8,10},{9,11},{10,... | collective-permute-start | bytes 3145736 | tf_op jit(solution)/shard_map/ppermute | solution.py:365
  309.5 13.8 %collective-permute-start.23 = (bf16[2,256,1024]{2,1,0:T(8,128)(2,1)}, bf16[2,256,1024]{2,1,0:T(8,128)(2,1)}, u32[]{:S(2)}, u32[]{:S(2)}) collective-permute-start(bf16[2,256,1024]{2,1,0:T(8,128)(2,1)} %broadcast_select_fusion.refs_2_), channel_id=1, source_target_pairs={{0,1},{1,0},{2,3},{3,2},{4,5},{5,4},{6,7},{7,6},{8,9},{9,8},{10,11... | collective-permute-start | bytes 3145736 | tf_op jit(solution)/shard_map/ppermute | solution.py:362
  312.2 11.1 %collective-permute-start.24 = (bf16[2,256,1024]{2,1,0:T(8,128)(2,1)}, bf16[2,256,1024]{2,1,0:T(8,128)(2,1)}, u32[]{:S(2)}, u32[]{:S(2)}) collective-permute-start(bf16[2,256,1024]{2,1,0:T(8,128)(2,1)} %collective-permute-done.20.refs_3_), channel_id=1, source_target_pairs={{0,1},{1,0},{2,3},{3,2},{4,5},{5,4},{6,7},{7,6},{8,9},{9,8},{10,11... | collective-permute-start | bytes 3145736 | tf_op jit(solution)/shard_map/ppermute | solution.py:362
  320.8 5.1 %collective-permute-start.26 = (bf16[2,256,1024]{2,1,0:T(8,128)(2,1)}, bf16[2,256,1024]{2,1,0:T(8,128)(2,1)}, u32[]{:S(2)}, u32[]{:S(2)}) collective-permute-start(bf16[2,256,1024]{2,1,0:T(8,128)(2,1)} %collective-permute-done.25.refs_2_), channel_id=1, source_target_pairs={{0,1},{1,0},{2,3},{3,2},{4,5},{5,4},{6,7},{7,6},{8,9},{9,8},{10,11... | collective-permute-start | bytes 3145736 | tf_op jit(solution)/shard_map/ppermute | solution.py:362
